TPU v7x, 32 devices: a whole 2x2x4 slice. The times are simulated.
32 devices in a mesh: group: 2 (over x), out: 8 (over z, y), inp: 2 (over core).
Axes of the slice: x: 2, y: 2, z: 4, core: 2. Of those that a mesh axis runs over, the one named last changes fastest.
Arguments:
- tokens: bfloat16 [2, 128, 8192], P(None, ('group', 'out')), parts along dimension 1, may hold values from -6 to 6
- norm_gain: float32 [8192], replicated, may hold values from 0.1 to 1.9
- query_weight: bfloat16 [8192, 8192], P('inp', 'out'), may hold values from -0.0625 to 0.0625
- key_matrix: bfloat16 [8192, 1024], P('inp', 'out'), may hold values from -0.0625 to 0.0625
- value_matrix: bfloat16 [8192, 1024], P('inp', 'out'), may hold values from -0.0625 to 0.0625
- output_weight: bfloat16 [8192, 8192], P('inp', 'out'), may hold values from -0.0625 to 0.0625
- cache_keys: bfloat16 [128, 512, 8, 128], P(('group', 'out'), None, 'inp'), parts along dimension 0, may hold values from -400 to 400
- stored_cache_values: bfloat16 [128, 512, 8, 128], P(('group', 'out'), None, 'inp'), parts along dimension 0, may hold values from -16 to 16
- lengths: int32 [128], P(('group', 'out')), parts along dimension 0, may hold values from 1 to 512, as said below
- positions: int32 [128], P(('group', 'out')), parts along dimension 0, may hold values from 512 to 8191
Outputs:
- mixed: bfloat16 [2, 128, 8192], P(None, ('group', 'out')), parts along dimension 1
There are 2 independent parts, one for each index of `group`. A program takes and returns all parts, laid end to end along the dimension named above; an argument that names none is the same for every part. Nothing has to cross between parts.
Inputs may be any that keep to these rules, and one draw needn't show every extreme that they name: `lengths`: each row's valid cache entries start at slot 0; in every draw some row holds all 512 and some row holds 1.
All inputs are finite; a program needn't handle non-finite values.
Results may differ from a plain program's by a relative error of at most 0.0065.
The roundings to bfloat16 on the way count: a program that leaves them out, or rounds other values in their place, can miss the bound.
Values may be sent and summed in bfloat16 or wider, within the bound.
No kernel may reach another device: no remote copies, remote signals or barrier semaphores. Data moves between devices by JAX's collectives and lax.ppermute only.
A program may use at most 128 MiB of HBM per device.

v0:
```python
import math

import jax
import jax.numpy as jnp
from jax import lax
from jax.sharding import PartitionSpec as P

HEAD_SIZE = 128


def rms_normed(tokens, gain):
    values = tokens.astype(jnp.float32)
    factor = lax.rsqrt(jnp.mean(values * values, axis=-1, keepdims=True) + 1e-05)
    return (values * factor * gain).astype(jnp.bfloat16)


def rotate(heads, position):
    head_size = heads.shape[-1]
    half_size = head_size // 2
    frequency = jnp.exp(
        -math.log(500000.0) * 2.0 * jnp.arange(half_size, dtype=jnp.float32) / head_size
    )
    angles = position.astype(jnp.float32)[..., None, None] * frequency
    cosine = jnp.cos(angles)
    sine_part = jnp.sin(angles)
    leading = heads[..., :half_size]
    trailing = heads[..., half_size:]
    return jnp.concatenate(
        [leading * cosine - trailing * sine_part, trailing * cosine + leading * sine_part], axis=-1
    )


def attend_one(queries, new_keys, new_values, cache_keys, stored_cache_values, lengths):
    count_of_rows, head_count, head_size = queries.shape
    key_heads = cache_keys.shape[2]
    grouped = queries.reshape(count_of_rows, key_heads, head_count // key_heads, head_size)
    factor = head_size ** (-0.5)
    cached = (
        jnp.einsum("rkgd,rckd->rkgc", grouped, cache_keys, preferred_element_type=jnp.float32)
        * factor
    )
    visible = jnp.arange(cache_keys.shape[1])[None, :] < lengths[:, None]
    cached = jnp.where(visible[:, None, None, :], cached, -jnp.inf)
    fresh_scores = (
        jnp.einsum("rkgd,nrkd->rkgn", grouped, new_keys, preferred_element_type=jnp.float32)
        * factor
    )
    highest = jnp.maximum(jnp.max(cached, axis=-1), jnp.max(fresh_scores, axis=-1))
    cached_exp = jnp.exp(cached - highest[..., None])
    fresh_exp = jnp.exp(fresh_scores - highest[..., None])
    totals = jnp.sum(cached_exp, axis=-1) + jnp.sum(fresh_exp, axis=-1)
    cached_prob = (cached_exp / totals[..., None]).astype(jnp.bfloat16)
    fresh_prob = (fresh_exp / totals[..., None]).astype(jnp.bfloat16)
    attended = jnp.einsum(
        "rkgc,rckd->rkgd", cached_prob, stored_cache_values, preferred_element_type=jnp.float32
    )
    attended = attended + jnp.einsum(
        "rkgn,nrkd->rkgd", fresh_prob, new_values, preferred_element_type=jnp.float32
    )
    return attended.reshape(count_of_rows, head_count * head_size).astype(jnp.bfloat16)


def project(normalized_input, query_weight, key_matrix, value_matrix, positions, first_step):
    out_count = lax.axis_size("out")
    inp_count = lax.axis_size("inp")
    inp_index = lax.axis_index("inp")
    step_count = normalized_input.shape[0]
    row_local = normalized_input.shape[1]
    feature_width = normalized_input.shape[2] // inp_count
    own_slice = lax.dynamic_slice_in_dim(
        normalized_input, inp_index * feature_width, feature_width, 2
    )
    query_cols = query_weight.shape[1]
    key_cols = key_matrix.shape[1]
    block_width = query_cols + 2 * key_cols
    shard_rows = lax.all_gather(own_slice, "out", axis=1, tiled=True)
    partials = jnp.concatenate(
        [
            jnp.dot(shard_rows, weight, preferred_element_type=jnp.float32)
            for weight in (query_weight, key_matrix, value_matrix)
        ],
        axis=-1,
    )
    totals = lax.psum(partials, "inp")
    regrouped = lax.all_to_all(totals, "out", split_axis=1, concat_axis=2, tiled=True)
    regrouped = regrouped.reshape(step_count, row_local, out_count, block_width)
    block_count = out_count // inp_count
    summed = lax.dynamic_slice_in_dim(regrouped, inp_index * block_count, block_count, 2)
    query_part = summed[..., :query_cols].reshape(step_count, row_local, -1, HEAD_SIZE)
    key_part = summed[..., query_cols : query_cols + key_cols].reshape(
        step_count, row_local, -1, HEAD_SIZE
    )
    value_part = summed[..., query_cols + key_cols :].reshape(step_count, row_local, -1, HEAD_SIZE)
    placed = positions[None, :] + (first_step + jnp.arange(step_count, dtype=jnp.int32))[:, None]
    queries = rotate(query_part, placed).astype(jnp.bfloat16)
    incoming_keys = rotate(key_part, placed).astype(jnp.bfloat16)
    incoming_values = value_part.astype(jnp.bfloat16)
    return (queries, incoming_keys, incoming_values)


def mix_out(attended, output_weight):
    partials = jnp.dot(
        lax.all_gather(attended, "out", axis=1, tiled=True),
        output_weight,
        preferred_element_type=jnp.float32,
    )
    totals = lax.psum(partials, "inp")
    return lax.all_to_all(
        totals.astype(jnp.bfloat16), "out", split_axis=1, concat_axis=2, tiled=True
    )


def body(
    tokens,
    norm_gain,
    query_weight,
    key_matrix,
    value_matrix,
    output_weight,
    cache_keys,
    stored_cache_values,
    lengths,
    positions,
):
    normalized_input = rms_normed(tokens, norm_gain)
    key_list = []
    value_list = []
    results = []
    for token_step in range(2):
        queries, incoming_keys, incoming_values = project(
            normalized_input[token_step : token_step + 1],
            query_weight,
            key_matrix,
            value_matrix,
            positions,
            token_step,
        )
        key_list.append(incoming_keys[0])
        value_list.append(incoming_values[0])
        attended = attend_one(
            queries[0],
            jnp.stack(key_list),
            jnp.stack(value_list),
            cache_keys,
            stored_cache_values,
            lengths,
        )
        results.append(mix_out(attended[None], output_weight)[0])
    return jnp.stack(results)


def solution(mesh):
    placed = (
        P(None, ("group", "out"), None),
        P(),
        P("inp", "out"),
        P("inp", "out"),
        P("inp", "out"),
        P("inp", "out"),
        P(("group", "out"), None, "inp", None),
        P(("group", "out"), None, "inp", None),
        P(("group", "out")),
        P(("group", "out")),
    )
    return jax.shard_map(
        body, mesh=mesh, in_specs=placed, out_specs=P(None, ("group", "out"), None), check_vma=False
    )
```

profile of v0, /device:TPU:0, one launch (start us, length us, event | category | flops | bytes accessed | tf_op | source)
XLA Modules:
  0.0 255.4 jit_solution(10394599203297113461)
XLA Ops:
  6.5 1.2 fusion.32
  7.8 1.1 fusion.34
  8.9 0.0 slice-start
  8.9 33.1 %all_gather.12 = bf16[1,64,4096]{2,1,0:T(8,128)(2,1)S(1)} all-gather(bf16[1,8,4096]{2,1,0:T(8,128)(2,1)S(1)} %constant_dynamic-slice_fusion.3), channel_id=1, replica_groups=mesh['group'=2,'out'=8,'inp'=2] {'out'}, dimensions={1}, use_global_device_ids=true | all-gather | bytes 589824 | tf_op jit(solution)/shard_map/all_gather | solution.py:76
  42.0 5.1 %convolution_bitcast_fusion.3 = f32[1,64,1024]{2,1,0:T(8,128)S(1)} fusion(bf16[4096,1024]{1,0:T(8,128)(2,1)} %param.12, bf16[1,64,4096]{2,1,0:T(8,128)(2,1)S(1)} %all_gather.12), kind=kOutput, calls=%fused_computation.15 | convolution fusion | flops 536870912 | bytes 9175040 | tf_op jit(solution)/shard_map/dot_general | solution.py:79
  47.2 0.3 convolution_bitcast_fusion.6
  47.5 31.3 %all_gather.14 = bf16[1,64,4096]{2,1,0:T(8,128)(2,1)S(1)} all-gather(bf16[1,8,4096]{2,1,0:T(8,128)(2,1)S(1)} %constant_dynamic-slice_fusion.1), channel_id=1, replica_groups=mesh['group'=2,'out'=8,'inp'=2] {'out'}, dimensions={1}, use_global_device_ids=true | all-gather | bytes 589824 | tf_op jit(solution)/shard_map/all_gather | solution.py:76
  78.8 1.6 convolution_bitcast_fusion.1
  80.4 0.3 convolution_bitcast_fusion.4
  80.7 0.0 copy-start.6
  80.8 0.0 copy-start.3
  80.8 0.3 convolution_bitcast_fusion.7
  81.1 0.3 convolution_bitcast_fusion.5
  81.4 0.7 pad_maximum_fusion
  82.2 0.7 pad_maximum_fusion.1
  82.9 0.0 all-reduce.5.cloned.1.call-update
  82.9 20.4 %all-reduce.5.cloned.1.call-done = (f32[1,64,1280]{2,1,0:T(8,128)}, f32[1,64,1280]{2,1,0:T(8,128)}) async-done(((f32[1,64,1280]{2,1,0:T(8,128)}, f32[1,64,1280]{2,1,0:T(8,128)}), (f32[1,64,1280]{2,1,0:T(8,128)}, f32[1,64,1280]{2,1,0:T(8,128)})) %all-reduce.5.cloned.1.call-update) | async-done | bytes 655376 | tf_op jit(solution)/shard_map/psum | solution.py:84
  103.3 2.0 copy.42
  105.3 5.8 %all-to-all-start.2 = ((f32[1,64,1280]{2,0,1:T(1,128)}), f32[1,64,1280]{2,0,1:T(1,128)S(1)}, u32[]{:S(2)}, u32[]{:S(2)}) async-start(f32[1,64,1280]{2,0,1:T(1,128)} %copy.42), calls=%async_computation.2 | async-start | bytes 655360 | tf_op jit(solution)/shard_map/all_to_all | solution.py:85
  111.1 2.0 copy.35
  113.1 8.7 %all-to-all-done.2 = f32[1,64,1280]{2,0,1:T(1,128)S(1)} async-done(((f32[1,64,1280]{2,0,1:T(1,128)}), f32[1,64,1280]{2,0,1:T(1,128)S(1)}, u32[]{:S(2)}, u32[]{:S(2)}) %all-to-all-start.2) | async-done | bytes 327712 | tf_op jit(solution)/shard_map/all_to_all | solution.py:85
  121.8 3.6 %all-to-all-start = ((f32[1,64,1280]{2,0,1:T(1,128)}), f32[1,64,1280]{2,0,1:T(1,128)S(1)}, u32[]{:S(2)}, u32[]{:S(2)}) async-start(f32[1,64,1280]{2,0,1:T(1,128)} %copy.35), calls=%async_computation | async-start | bytes 655360 | tf_op jit(solution)/shard_map/all_to_all | solution.py:85
  125.5 0.1 iota_compare_fusion
  125.6 0.1 multiply_cosine_fusion.1
  125.7 10.2 %all-to-all-done = f32[1,64,1280]{2,0,1:T(1,128)S(1)} async-done(((f32[1,64,1280]{2,0,1:T(1,128)}), f32[1,64,1280]{2,0,1:T(1,128)S(1)}, u32[]{:S(2)}, u32[]{:S(2)}) %all-to-all-start) | async-done | bytes 327712 | tf_op jit(solution)/shard_map/all_to_all | solution.py:85
  136.0 0.0 copy-start.4
  136.0 0.2 copy.96
  136.2 0.2 copy.95
  136.4 0.1 subtract_convert_fusion.3
  136.6 0.1 fusion.49
  136.7 0.1 maximum_bitcast_fusion
  136.8 0.2 fusion.67
  137.0 3.7 %fusion.81 = (f32[8,4,8]{2,1,0:T(4,128)S(1)}, f32[8,4,8,512]{3,2,1,0:T(8,128)S(1)}) fusion(bf16[8,512,4,128]{3,2,1,0:T(4,128)(2,1)} %param.16, bf16[8,4,8,64]{3,2,1,0:T(8,128)(2,1)S(1)} %get-tuple-element.18, bf16[8,4,8,64]{3,2,1,0:T(8,128)(2,1)S(1)} %get-tuple-element.17, pred[8,512]{1,0:T(8,128)(4,1)S(1)} %iota_compare_fusion), kind=kOutput, calls=%fused_computation.119 | convolution fusion | flops 34078464 | bytes 4789248 | tf_op jit(solution)/shard_map/rkgd,rckd->rkgc/dot_general | solution.py:39
  140.7 0.3 fusion.43
  141.0 0.7 fusion.29
  141.8 31.5 %all_gather.13 = bf16[1,64,4096]{2,1,0:T(8,128)(2,1)S(1)} all-gather(bf16[1,8,4096]{2,1,0:T(8,128)(2,1)S(1)} %convert_element_type.96), channel_id=1, replica_groups=mesh['group'=2,'out'=8,'inp'=2] {'out'}, dimensions={1}, use_global_device_ids=true | all-gather | bytes 589824 | tf_op jit(solution)/shard_map/all_gather | solution.py:103
  173.3 5.1 %convolution_bitcast_fusion.2 = f32[1,64,1024]{2,1,0:T(8,128)S(1)} fusion(bf16[4096,1024]{1,0:T(8,128)(2,1)} %param.15, bf16[1,64,4096]{2,1,0:T(8,128)(2,1)S(1)} %all_gather.13), kind=kOutput, calls=%fused_computation.14 | convolution fusion | flops 536870912 | bytes 9175040 | tf_op jit(solution)/shard_map/dot_general | solution.py:102
  178.5 0.0 copy-start.5
  178.5 0.1 subtract_convert_fusion.2
  178.6 0.1 fusion.51
  178.7 1.4 fusion.79
  180.1 0.3 fusion.80
  180.4 0.1 fusion.53
  180.5 0.3 fusion.44
  180.7 0.2 fusion.54
  181.0 0.0 copy-done.5
  181.0 0.7 fusion.26
  181.8 31.5 %all_gather.15 = bf16[1,64,4096]{2,1,0:T(8,128)(2,1)S(1)} all-gather(bf16[1,8,4096]{2,1,0:T(8,128)(2,1)S(1)} %convert_element_type.102), channel_id=1, replica_groups=mesh['group'=2,'out'=8,'inp'=2] {'out'}, dimensions={1}, use_global_device_ids=true | all-gather | bytes 589824 | tf_op jit(solution)/shard_map/all_gather | solution.py:103
  213.2 5.0 %convolution_bitcast_fusion = f32[1,64,1024]{2,1,0:T(8,128)S(1)} fusion(bf16[4096,1024]{1,0:T(8,128)(2,1)} %param.15, bf16[1,64,4096]{2,1,0:T(8,128)(2,1)S(1)} %all_gather.15), kind=kOutput, calls=%fused_computation.12 | convolution fusion | flops 536870912 | bytes 9175040 | tf_op jit(solution)/shard_map/dot_general | solution.py:102
  218.2 4.8 %all-reduce.6 = (bf16[1,64,1024]{2,1,0:T(8,128)(2,1)S(1)}, bf16[1,64,1024]{2,1,0:T(8,128)(2,1)S(1)}) all-reduce(f32[1,64,1024]{2,1,0:T(8,128)S(1)} %convolution_bitcast_fusion, f32[1,64,1024]{2,1,0:T(8,128)S(1)} %convolution_bitcast_fusion.2), channel_id=1, replica_groups=mesh['group'=2,'out'=8,'inp'=2] {'inp'}, use_global_device_ids=true, to_apply=%region_10.11 | all-reduce | flops 131072 | bytes 786432 | tf_op jit(solution)/shard_map/psum | solution.py:107
  223.0 0.2 copy.100
  223.2 0.5 broadcast.140
  223.8 1.4 reduce.1
  225.2 0.7 reshape.364
  225.9 3.5 %all-to-all-start.1 = ((bf16[8,2,4096]{2,1,0:T(2,128)(2,1)}), bf16[8,2,4096]{2,1,0:T(2,128)(2,1)S(1)}, u32[]{:S(2)}, u32[]{:S(2)}) async-start(bf16[8,2,4096]{2,1,0:T(2,128)(2,1)} %reshape.364), calls=%async_computation.1 | async-start | bytes 262144 | tf_op jit(solution)/shard_map/all_to_all | solution.py:108
  229.4 0.2 copy.99
  229.6 1.4 reduce
  231.0 0.7 reshape.362
  231.7 5.3 %all-to-all-done.1 = bf16[8,2,4096]{2,1,0:T(2,128)(2,1)S(1)} async-done(((bf16[8,2,4096]{2,1,0:T(2,128)(2,1)}), bf16[8,2,4096]{2,1,0:T(2,128)(2,1)S(1)}, u32[]{:S(2)}, u32[]{:S(2)}) %all-to-all-start.1) | async-done | bytes 131104 | tf_op jit(solution)/shard_map/all_to_all | solution.py:108
  237.0 3.4 %all-to-all-start.3 = ((bf16[8,2,4096]{2,1,0:T(2,128)(2,1)}), bf16[8,2,4096]{2,1,0:T(2,128)(2,1)S(1)}, u32[]{:S(2)}, u32[]{:S(2)}) async-start(bf16[8,2,4096]{2,1,0:T(2,128)(2,1)} %reshape.362), calls=%async_computation.3 | async-start | bytes 262144 | tf_op jit(solution)/shard_map/all_to_all | solution.py:108
  240.4 0.1 reshape.365
  240.5 7.1 %all-to-all-done.3 = bf16[8,2,4096]{2,1,0:T(2,128)(2,1)S(1)} async-done(((bf16[8,2,4096]{2,1,0:T(2,128)(2,1)}), bf16[8,2,4096]{2,1,0:T(2,128)(2,1)S(1)}, u32[]{:S(2)}, u32[]{:S(2)}) %all-to-all-start.3) | async-done | bytes 131104 | tf_op jit(solution)/shard_map/all_to_all | solution.py:108
  247.6 0.1 reshape.363
  247.8 0.7 pad_maximum_fusion.2
  (37 shorter events, 0.5 us)
Async XLA Ops:
  6.5 40.6 %copy-start = (bf16[4096,128]{1,0:T(8,128)(2,1)S(1)}, bf16[4096,128]{1,0:T(8,128)(2,1)}, u32[]{:S(2)}) copy-start(bf16[4096,128]{1,0:T(8,128)(2,1)} %param.14) | copy-start | bytes 3145732
  6.5 96.7 %all-reduce.5.cloned.1.call-start = ((), (), s32[]{:S(2)}) async-start(), calls=%async_computation.4 | async-start | bytes 1310720 | tf_op jit(solution)/shard_map/psum | solution.py:84
  8.9 69.9 %slice-start = ((s8[8388608]{0:T(1024)(128)(4,1)}), s8[4194304]{0:T(1024)(128)(4,1)S(1)}, s32[]{:S(2)}) async-start(s8[8388608]{0:T(1024)(128)(4,1)} %bitcast.99), calls=%async_computation.5 | async-start | bytes 8388608
  42.0 36.8 %slice-start.1 = ((s8[8388608]{0:T(1024)(128)(4,1)}), s8[4194304]{0:T(1024)(128)(4,1)S(1)}, s32[]{:S(2)}) async-start(s8[8388608]{0:T(1024)(128)(4,1)} %bitcast.99), calls=%async_computation.6 | async-start | bytes 8388608
  78.8 1.9 copy-start.2
  80.7 44.7 %copy-start.6 = (s32[8]{0:T(128)S(1)}, s32[8]{0:T(128)}, u32[]{:S(2)}) copy-start(s32[8]{0:T(128)} %param.19) | copy-start | bytes 100
  80.8 44.7 %copy-start.3 = (s32[8]{0:T(128)S(1)}, s32[8]{0:T(128)}, u32[]{:S(2)}) copy-start(s32[8]{0:T(128)} %param.18) | copy-start | bytes 100
  105.3 16.5 %all-to-all-start.2 = ((f32[1,64,1280]{2,0,1:T(1,128)}), f32[1,64,1280]{2,0,1:T(1,128)S(1)}, u32[]{:S(2)}, u32[]{:S(2)}) async-start(f32[1,64,1280]{2,0,1:T(1,128)} %copy.42), calls=%async_computation.2 | async-start | bytes 655360 | tf_op jit(solution)/shard_map/all_to_all | solution.py:85
  121.8 14.1 %all-to-all-start = ((f32[1,64,1280]{2,0,1:T(1,128)}), f32[1,64,1280]{2,0,1:T(1,128)S(1)}, u32[]{:S(2)}, u32[]{:S(2)}) async-start(f32[1,64,1280]{2,0,1:T(1,128)} %copy.35), calls=%async_computation | async-start | bytes 655360 | tf_op jit(solution)/shard_map/all_to_all | solution.py:85
  136.0 5.1 %copy-start.4 = (bf16[8,512,4,128]{3,2,1,0:T(4,128)(2,1)S(1)}, bf16[8,512,4,128]{3,2,1,0:T(4,128)(2,1)}, u32[]{:S(2)}) copy-start(bf16[8,512,4,128]{3,2,1,0:T(4,128)(2,1)} %param.17) | copy-start | bytes 12582916
  173.3 5.4 %copy-start.1 = (bf16[8,512,4,128]{3,2,1,0:T(4,128)(2,1)S(1)}, bf16[8,512,4,128]{3,2,1,0:T(4,128)(2,1)}, u32[]{:S(2)}) copy-start(bf16[8,512,4,128]{3,2,1,0:T(4,128)(2,1)} %param.16) | copy-start | bytes 12582916
  178.5 2.5 copy-start.5
  225.9 11.1 %all-to-all-start.1 = ((bf16[8,2,4096]{2,1,0:T(2,128)(2,1)}), bf16[8,2,4096]{2,1,0:T(2,128)(2,1)S(1)}, u32[]{:S(2)}, u32[]{:S(2)}) async-start(bf16[8,2,4096]{2,1,0:T(2,128)(2,1)} %reshape.364), calls=%async_computation.1 | async-start | bytes 262144 | tf_op jit(solution)/shard_map/all_to_all | solution.py:108
  237.0 10.7 %all-to-all-start.3 = ((bf16[8,2,4096]{2,1,0:T(2,128)(2,1)}), bf16[8,2,4096]{2,1,0:T(2,128)(2,1)S(1)}, u32[]{:S(2)}, u32[]{:S(2)}) async-start(bf16[8,2,4096]{2,1,0:T(2,128)(2,1)} %reshape.362), calls=%async_computation.3 | async-start | bytes 262144 | tf_op jit(solution)/shard_map/all_to_all | solution.py:108
Sparse Core Ops, SparseCore 0:
  83.0 20.1 all-reduce.4
where the time goes:
time: 256 us; the launch traced here: 255 us
  blocking collectives  132 us (52%)
  waiting for transfers between devices  51.6 us (20%)
  matrix products  25.3 us (10%)
  starting transfers between devices  16.3 us (6%)
  between operations  13.8 us (5%)
  other arithmetic  8.63 us (3%)
  local copies, waits for them, and re-layouts  7.43 us (3%)
    all_gather x2, blocking collectives, project(): shard_rows = lax.all_gather(own_slice, 'out', axis=1, tiled=True)  64.4 us
    all_gather x2, blocking collectives, mix_out(): lax.all_gather(attended, 'out', axis=1, tiled=True)  63 us
    psum x1, waiting for transfers between devices, project(): totals = lax.psum(partials, 'inp')  20.4 us
    all_to_all x2, waiting for transfers between devices, project(): lax.all_to_all(totals, 'out', split_axis=1, concat_axis=2, tiled=True)  18.9 us
    all_to_all x2, waiting for transfers between devices, mix_out(): lax.all_to_all(totals.astype(jnp.bfloat16), 'out', split_axis=1, concat_a...  12.4 us
    dot_general x2, matrix products, mix_out(): jnp.dot(lax.all_gather(attended, 'out', axis=1, tiled=True), output_weigh...  10.1 us
    all_to_all x2, starting transfers between devices, project(): lax.all_to_all(totals, 'out', split_axis=1, concat_axis=2, tiled=True)  9.43 us
    dot_general x6, matrix products, project(): jnp.dot(shard_rows, weight, preferred_element_type=jnp.float32)  7.96 us
  transfers between devices with their start and end apart: 5, of which 5 were waited for; matrix products, arithmetic and copies ran while one was open for 2% of the time, Pallas kernels for 0%

commit v1 on v0

--- a/solution.py
+++ b/solution.py
@@ -108,6 +108,144 @@
     return lax.all_to_all(
         totals.astype(jnp.bfloat16), "out", split_axis=1, concat_axis=2, tiled=True
     )
+
+
+def exchange_orders(step):
+    return {"far": (4, 4), "near": (2, 1), "last": (1, 2)}[step]
+
+
+def swap_blocks(block, step):
+    flips = exchange_orders(step)
+    pairs = [(2 * o + i, 2 * (o ^ flips[i]) + i) for o in range(8) for i in range(2)]
+    return lax.ppermute(block, ("out", "inp"), pairs)
+
+
+def gather_blocks(block):
+    far = swap_blocks(block, "far")
+    near = swap_blocks(block, "near")
+    last = swap_blocks(block, "last")
+    near_last = swap_blocks(near, "last")
+    far_near = swap_blocks(far, "near")
+    far_last = swap_blocks(far, "last")
+    far_near_last = swap_blocks(far_near, "last")
+    return (block, near, last, near_last), (far, far_near, far_last, far_near_last)
+
+
+def swap_cores(block):
+    return lax.ppermute(block, "inp", [(0, 1), (1, 0)])
+
+
+def offset_of(core, place):
+    return (0, 2, 1, 3)[place] if core == 0 else place
+
+
+def hand_out(blocks):
+    received = []
+    for place, block in enumerate(blocks):
+        pairs = []
+        for o in range(8):
+            for i in range(2):
+                target = o ^ (4 * i) ^ offset_of(i, place)
+                pairs.append((2 * o + i, 2 * target + o // 4))
+        received.append(lax.ppermute(block, ("out", "inp"), pairs))
+    return received
+
+
+def in_order(received):
+    own_out = lax.axis_index("out")
+    own_core = lax.axis_index("inp")
+    crossed = (own_out // 4) ^ own_core
+    stacked = jnp.stack(received)
+    ordered = []
+    for column in range(4):
+        offset = column ^ (own_out % 4)
+        swapped = jnp.where((offset == 1) | (offset == 2), 3 - offset, offset)
+        place = jnp.where(crossed == 0, swapped, offset)
+        ordered.append(lax.dynamic_index_in_dim(stacked, place, 0, keepdims=False))
+    return ordered
+
+
+def pair_summed(lower, upper, multiply):
+    core = lax.axis_index("inp")
+    lower = jnp.concatenate(lower)
+    upper = jnp.concatenate(upper)
+    given = multiply(jnp.where(core == 0, upper, lower))
+    kept = multiply(jnp.where(core == 0, lower, upper))
+    count = kept.shape[0] // 4
+    arrived = swap_cores(given)
+    arrived = arrived.reshape(4, count, -1)
+    arrived = jnp.stack([arrived[0], arrived[2], arrived[1], arrived[3]])
+    return kept.reshape(arrived.shape) + arrived
+
+
+def attend_both(queries, new_keys, new_values, cache_keys, cache_values, lengths):
+    factor = HEAD_SIZE ** (-0.5)
+    steps = queries.shape[1]
+    cached = jnp.einsum("ktrgd,rckd->rktgc", queries, cache_keys, preferred_element_type=jnp.float32) * factor
+    visible = jnp.arange(cache_keys.shape[1])[None, :] < lengths[:, None]
+    cached = jnp.where(visible[:, None, None, None, :], cached, -jnp.inf)
+    fresh = jnp.einsum("ktrgd,knrd->rktgn", queries, new_keys, preferred_element_type=jnp.float32) * factor
+    causal = jnp.arange(steps)[:, None] >= jnp.arange(steps)[None, :]
+    fresh = jnp.where(causal[None, None, :, None, :], fresh, -jnp.inf)
+    highest = jnp.maximum(jnp.max(cached, axis=-1), jnp.max(fresh, axis=-1))
+    cached_exp = jnp.exp(cached - highest[..., None])
+    fresh_exp = jnp.exp(fresh - highest[..., None])
+    totals = jnp.sum(cached_exp, axis=-1) + jnp.sum(fresh_exp, axis=-1)
+    cached_prob = (cached_exp / totals[..., None]).astype(jnp.bfloat16)
+    fresh_prob = (fresh_exp / totals[..., None]).astype(jnp.bfloat16)
+    attended = jnp.einsum("rktgc,rckd->trkgd", cached_prob, cache_values, preferred_element_type=jnp.float32)
+    attended = attended + jnp.einsum("rktgn,knrd->trkgd", fresh_prob, new_values, preferred_element_type=jnp.float32)
+    return attended.astype(jnp.bfloat16)
+
+
+def eight_chip_body(
+    tokens, norm_gain, query_weight, key_matrix, value_matrix, output_weight, cache_keys, cache_values, lengths, positions
+):
+    steps, rows, width = tokens.shape
+    core = lax.axis_index("inp")
+    half = width // 2
+    query_cols = query_weight.shape[1]
+    key_cols = key_matrix.shape[1]
+    normed = rms_normed(tokens, norm_gain)
+    own = lax.dynamic_slice_in_dim(normed, core * half, half, 2).reshape(steps * rows, half)
+    tag = jnp.stack([positions // 128, positions % 128], axis=-1).astype(jnp.bfloat16)
+    tag = jnp.pad(jnp.tile(tag, (steps, 1)), ((0, 0), (0, 126)))
+    lower, upper = gather_blocks(jnp.concatenate([own, tag], axis=1))
+
+    def multiply(block):
+        return jnp.concatenate(
+            [
+                jnp.dot(block[:, :half], weight, preferred_element_type=jnp.float32)
+                for weight in (query_weight, key_matrix, value_matrix)
+            ],
+            axis=-1,
+        )
+
+    sums = pair_summed(lower, upper, multiply)
+    tags = jnp.where(core == 0, jnp.stack([b[:, half : half + 2] for b in lower]), jnp.stack([b[:, half : half + 2] for b in upper]))
+    tags = tags.astype(jnp.float32)
+    placed = tags[..., 0] * 128.0 + tags[..., 1]
+    placed = placed.reshape(4, steps, rows) + jnp.arange(steps, dtype=jnp.float32)[None, :, None]
+    placed = placed.reshape(4, steps * rows)
+    turned = query_cols + key_cols
+    rotated = rotate(sums[..., :turned].reshape(4, steps * rows, -1, HEAD_SIZE), placed)
+    outgoing = jnp.concatenate([rotated.reshape(4, steps * rows, turned), sums[..., turned:]], axis=-1).astype(jnp.bfloat16)
+    heads = jnp.stack(in_order(hand_out([outgoing[k] for k in range(4)])))
+    heads = heads.reshape(4, steps, rows, -1, HEAD_SIZE)
+    group = query_cols // HEAD_SIZE
+    attended = attend_both(
+        heads[:, :, :, :group], heads[:, :, :, group], heads[:, :, :, group + 1], cache_keys, cache_values, lengths
+    )
+    lower, upper = gather_blocks(attended.reshape(steps * rows, half))
+    mixed = pair_summed(
+        lower, upper, lambda block: jnp.dot(block, output_weight, preferred_element_type=jnp.float32)
+    ).astype(jnp.bfloat16)
+    own_half = jnp.concatenate(in_order(hand_out([mixed[k] for k in range(4)])), axis=-1)
+    other_half = swap_cores(own_half)
+    whole = jnp.concatenate(
+        [jnp.where(core == 0, own_half, other_half), jnp.where(core == 0, other_half, own_half)], axis=-1
+    )
+    return whole.reshape(steps, rows, width)
 
 
 def body(
@@ -162,6 +300,7 @@
         P(("group", "out")),
         P(("group", "out")),
     )
+    chosen = eight_chip_body if (mesh.shape["out"], mesh.shape["inp"]) == (8, 2) else body
     return jax.shard_map(
-        body, mesh=mesh, in_specs=placed, out_specs=P(None, ("group", "out"), None), check_vma=False
-    )
+        chosen, mesh=mesh, in_specs=placed, out_specs=P(None, ("group", "out"), None), check_vma=False
+    )

time: 256 us -> 96.8 us (0.38)
  blocking collectives: 132 us -> 0 us
  waiting for transfers between devices: 51.6 us -> 25.1 us
  starting transfers between devices: 16.3 us -> 37.2 us
  between operations: 13.8 us -> 0.56 us
  matrix products: 25.3 us -> 16.9 us
    all_gather x4 -> x0, blocking collectives: 127 us -> none  [the longest x2 64.4 us: project(): shard_rows = lax.all_gather(own_slice, 'out', axis=1, tiled=True)]
    ppermute x0 -> x25, starting transfers between devices: none -> 37.2 us  [the longest x14 23.8 us: swap_blocks(): return lax.ppermute(block, ('out', 'inp'), pairs)]
    all_to_all x4 -> x0, waiting for transfers between devices: 31.3 us -> none  [the longest x2 18.9 us: project(): lax.all_to_all(totals, 'out', split_axis=1, concat_axis=2, tiled=True)]
    ppermute x0 -> x25, waiting for transfers between devices: none -> 25.1 us  [the longest x14 16.5 us: swap_blocks(): return lax.ppermute(block, ('out', 'inp'), pairs)]
    psum x1 -> x0, waiting for transfers between devices: 20.4 us -> none  [project(): totals = lax.psum(partials, 'inp')]
    all_to_all x4 -> x0, starting transfers between devices: 16.3 us -> none  [the longest x2 9.43 us: project(): lax.all_to_all(totals, 'out', split_axis=1, concat_axis=2, tiled=True)]
    dot_general x15 -> x12, matrix products: 25.3 us -> 16.9 us  [the longest x2 6.69 us: eight_chip_body(): jnp.dot(block, output_weight, preferred_element_type=jnp.float32)]
    psum x1 -> x0, blocking collectives: 4.84 us -> none  [mix_out(): totals = lax.psum(partials, 'inp')]
  transfers between devices with their start and end apart: 5 -> 25, of which waited for: 5 -> 15; matrix products, arithmetic and copies ran while one was open for 2% -> 9% of each run, Pallas kernels for 0% -> 0%
where the time goes in v1:
time: 96.8 us; the launch traced here: 96.3 us
  starting transfers between devices  37.2 us (38%)
  waiting for transfers between devices  25.1 us (26%)
  matrix products  16.9 us (17%)
  local copies, waits for them, and re-layouts  9.6 us (10%)
  other arithmetic  7.04 us (7%)
    ppermute x14, starting transfers between devices, swap_blocks(): return lax.ppermute(block, ('out', 'inp'), pairs)  23.8 us
    ppermute x14, waiting for transfers between devices, swap_blocks(): return lax.ppermute(block, ('out', 'inp'), pairs)  16.5 us
    ppermute x8, starting transfers between devices, hand_out(): received.append(lax.ppermute(block, ('out', 'inp'), pairs))  8.41 us
    dot_general x2, matrix products, eight_chip_body(): jnp.dot(block, output_weight, preferred_element_type=jnp.float32)  6.69 us
    ppermute x8, waiting for transfers between devices, hand_out(): received.append(lax.ppermute(block, ('out', 'inp'), pairs))  6.2 us
    ppermute x3, starting transfers between devices, swap_cores(): return lax.ppermute(block, 'inp', [(0, 1), (1, 0)])  4.98 us
    dot_general x6, matrix products, multiply(): jnp.dot(block[:, :half], weight, preferred_element_type=jnp.float32)  4.44 us
    unnamed x24, local copies, waits for them, and re-layouts  4 us
  transfers between devices with their start and end apart: 25, of which 15 were waited for; matrix products, arithmetic and copies ran while one was open for 9% of the time, Pallas kernels for 0%

profile of v1, /device:TPU:0, one launch (start us, length us, event | category | flops | bytes accessed | tf_op | source)
XLA Modules:
  0.0 96.3 jit_solution(14691274835850169106)
XLA Ops:
  0.0 1.3 %multiply_reduce_fusion = f32[2,8]{1,0:T(2,128)S(1)} fusion(bf16[2,8,8192]{2,1,0:T(8,128)(2,1)} %param.10), kind=kLoop, calls=%fused_computation.24 | loop fusion | flops 393200 | bytes 262208 | tf_op jit(solution)/shard_map/reduce_sum | solution.py:13
  1.3 1.0 %convert_element_type.29 = f32[2,8,8192]{2,1,0:T(8,128)S(1)} convert(bf16[2,8,8192]{2,1,0:T(8,128)(2,1)} %param.10) | non-fusion elementwise | flops 131072 | bytes 786432 | tf_op jit(solution)/shard_map/convert_element_type | solution.py:12
  2.3 0.7 convert_bitcast_fusion
  3.1 0.7 dynamic-slice
  3.9 4.1 %collective-permute-start.3 = (bf16[16,4224]{1,0:T(8,128)(2,1)S(1)}, bf16[16,4224]{1,0:T(8,128)(2,1)}, u32[]{:S(2)}, u32[]{:S(2)}) collective-permute-start(bf16[16,4224]{1,0:T(8,128)(2,1)S(1)} %pad_maximum_fusion.5), channel_id=1, source_target_pairs={{0,8},{1,9},{2,10},{3,11},{4,12},{5,13},{6,14},{7,15},{8,0},{9,1},... | collective-permute-start | bytes 405512 | tf_op jit(solution)/shard_map/ppermute | solution.py:120
  8.0 1.5 %collective-permute-start.1 = (bf16[16,4224]{1,0:T(8,128)(2,1)S(1)}, bf16[16,4224]{1,0:T(8,128)(2,1)S(1)}, u32[]{:S(2)}, u32[]{:S(2)}) collective-permute-start(bf16[16,4224]{1,0:T(8,128)(2,1)S(1)} %pad_maximum_fusion.5), channel_id=1, source_target_pairs={{0,2},{1,5},{2,0},{3,7},{4,6},{5,1},{6,4},{7,3},{8,10},{9,13},{10,... | collective-permute-start | bytes 405512 | tf_op jit(solution)/shard_map/ppermute | solution.py:120
  9.5 1.6 %collective-permute-start = (bf16[16,4224]{1,0:T(8,128)(2,1)S(1)}, bf16[16,4224]{1,0:T(8,128)(2,1)S(1)}, u32[]{:S(2)}, u32[]{:S(2)}) collective-permute-start(bf16[16,4224]{1,0:T(8,128)(2,1)S(1)} %pad_maximum_fusion.5), channel_id=1, source_target_pairs={{0,4},{1,3},{2,6},{3,1},{4,0},{5,7},{6,2},{7,5},{8,12},{9,11},{10,... | collective-permute-start | bytes 405512 | tf_op jit(solution)/shard_map/ppermute | solution.py:120
  11.1 0.7 iota_compare_fusion
  12.0 2.7 %collective-permute-done.3 = bf16[16,4224]{1,0:T(8,128)(2,1)} collective-permute-done((bf16[16,4224]{1,0:T(8,128)(2,1)S(1)}, bf16[16,4224]{1,0:T(8,128)(2,1)}, u32[]{:S(2)}, u32[]{:S(2)}) %collective-permute-start.3) | collective-permute-done | bytes 135200 | tf_op jit(solution)/shard_map/ppermute | solution.py:120
  14.7 0.6 collective-permute-start.4
  15.3 0.3 collective-permute-done
  15.6 1.2 %collective-permute-start.2 = (bf16[16,4224]{1,0:T(8,128)(2,1)S(1)}, bf16[16,4224]{1,0:T(8,128)(2,1)}, u32[]{:S(2)}, u32[]{:S(2)}) collective-permute-start(bf16[16,4224]{1,0:T(8,128)(2,1)S(1)} %collective-permute-done), channel_id=1, source_target_pairs={{0,2},{1,5},{2,0},{3,7},{4,6},{5,1},{6,4},{7,3},{8,10},{9,13},{10,... | collective-permute-start | bytes 405512 | tf_op jit(solution)/shard_map/ppermute | solution.py:120
  16.7 0.9 constant_dynamic-update-slice_fusion.3
  17.7 0.7 slice.187
  18.6 0.9 collective-permute-start.5
  19.5 0.8 collective-permute-done.4
  20.3 1.3 %collective-permute-start.6 = (bf16[16,4224]{1,0:T(8,128)(2,1)}, bf16[16,4224]{1,0:T(8,128)(2,1)}, u32[]{:S(2)}, u32[]{:S(2)}) collective-permute-start(bf16[16,4224]{1,0:T(8,128)(2,1)} %collective-permute-done.4), channel_id=1, source_target_pairs={{0,2},{1,5},{2,0},{3,7},{4,6},{5,1},{6,4},{7,3},{8,10},{9,13},{10,... | collective-permute-start | bytes 405512 | tf_op jit(solution)/shard_map/ppermute | solution.py:120
  21.6 1.0 %pad_maximum_fusion = bf16[64,4224]{1,0:T(8,128)(2,1)S(1)} fusion(bf16[16,4224]{1,0:T(8,128)(2,1)} %collective-permute-done.2, bf16[16,4224]{1,0:T(8,128)(2,1)S(1)} %collective-permute-done.1, bf16[16,4224]{1,0:T(8,128)(2,1)} %copy-done.3, bf16[16,128]{1,0:T(8,128)(2,1)S(1)} %pad.4, bf16[16,4096]{1,0:T(8,128)(2,1)S(1)} %fusion.32), kind=kLoop, calls=%fused_computation.15 | loop fusion | flops 2703360 | bytes 1081344 | tf_op jit(solution)/shard_map/concatenate | solution.py:170
  22.6 0.9 constant_dynamic-update-slice_fusion.2
  23.5 0.3 collective-permute-done.5
  24.0 0.7 slice.188
  24.7 0.7 slice.186
  25.7 0.9 constant_dynamic-update-slice_fusion
  26.7 0.3 fusion.56
  27.0 0.3 fusion.57
  27.3 0.3 fusion.53
  27.7 0.3 fusion.54
  28.0 2.0 %copy-done.1 = bf16[4096,1024]{1,0:T(8,128)(2,1)S(1)} copy-done((bf16[4096,1024]{1,0:T(8,128)(2,1)S(1)}, bf16[4096,1024]{1,0:T(8,128)(2,1)}, u32[]{:S(2)}) %copy-start.1) | copy-done | bytes 8388632
  30.0 1.6 %fusion.55 = f32[64,1024]{1,0:T(8,128)S(1)} fusion(bf16[64,4096]{1,0:T(8,128)(2,1)S(1)} %get-tuple-element.5, bf16[4096,1024]{1,0:T(8,128)(2,1)S(1)} %copy-done.1), kind=kOutput, calls=%fused_computation.131 | convolution fusion | flops 536870912 | bytes 9175040 | tf_op jit(solution)/shard_map/dot_general | solution.py:218
  31.5 1.6 %fusion.52 = f32[64,1024]{1,0:T(8,128)S(1)} fusion(bf16[64,4096]{1,0:T(8,128)(2,1)S(1)} %get-tuple-element.6, bf16[4096,1024]{1,0:T(8,128)(2,1)S(1)} %copy-done.1), kind=kOutput, calls=%fused_computation.128 | convolution fusion | flops 536870912 | bytes 9175040 | tf_op jit(solution)/shard_map/dot_general | solution.py:218
  33.1 0.7 slice.190
  34.3 1.4 %collective-permute-done.7 = f32[64,1280]{1,0:T(8,128)S(1)} collective-permute-done((f32[64,1280]{1,0:T(8,128)S(1)}, f32[64,1280]{1,0:T(8,128)S(1)}, u32[]{:S(2)}, u32[]{:S(2)}) %collective-permute-start.7) | collective-permute-done | bytes 327712 | tf_op jit(solution)/shard_map/ppermute | solution.py:135
  36.4 0.7 collective-permute-start.8
  37.0 1.7 %collective-permute-start.9 = (bf16[16,1280]{1,0:T(8,128)(2,1)S(1)}, bf16[16,1280]{1,0:T(8,128)(2,1)S(1)}, u32[]{:S(2)}, u32[]{:S(2)}) collective-permute-start(bf16[16,1280]{1,0:T(8,128)(2,1)S(1)} %get-tuple-element.26), channel_id=1, source_target_pairs={{0,4},{1,10},{2,6},{3,8},{4,0},{5,14},{6,2},{7,12},{8,13},{9,3},{1... | collective-permute-start | bytes 122888 | tf_op jit(solution)/shard_map/ppermute | solution.py:150
  38.7 1.1 %collective-permute-start.11 = (bf16[16,1280]{1,0:T(8,128)(2,1)S(1)}, bf16[16,1280]{1,0:T(8,128)(2,1)S(1)}, u32[]{:S(2)}, u32[]{:S(2)}) collective-permute-start(bf16[16,1280]{1,0:T(8,128)(2,1)S(1)} %get-tuple-element.27), channel_id=1, source_target_pairs={{0,6},{1,14},{2,4},{3,12},{4,2},{5,10},{6,0},{7,8},{8,15},{9,7},{1... | collective-permute-start | bytes 122888 | tf_op jit(solution)/shard_map/ppermute | solution.py:150
  39.8 0.8 collective-permute-start.10
  40.6 0.5 collective-permute-done.9
  41.1 2.6 %collective-permute-done.11 = bf16[16,1280]{1,0:T(8,128)(2,1)S(1)} collective-permute-done((bf16[16,1280]{1,0:T(8,128)(2,1)S(1)}, bf16[16,1280]{1,0:T(8,128)(2,1)S(1)}, u32[]{:S(2)}, u32[]{:S(2)}) %collective-permute-start.11) | collective-permute-done | bytes 40992 | tf_op jit(solution)/shard_map/ppermute | solution.py:150
  43.7 0.4 collective-permute-done.10
  44.2 0.7 fusion.51
  44.9 3.8 %fusion.50 = (f32[8,4,2,8]{3,2,1,0:T(2,128)S(1)}, f32[8,4,2,8,512]{4,3,2,1,0:T(8,128)S(1)}) fusion(bf16[8,512,4,128,1]{3,2,1,0,4:T(4,128)(2,1)} %bitcast.108, bf16[4,2,8,8,128]{4,2,3,1,0:T(8,128)(2,1)S(1)} %slice.201, pred[8,512]{1,0:T(8,128)(4,1)S(1)} %iota_compare_fusion), kind=kOutput, calls=%fused_computation.126 | convolution fusion | flops 67894784 | bytes 5380096 | tf_op jit(solution)/shard_map/ktrgd,rckd->rktgc/dot_general | solution.py:184
  49.0 0.4 fusion.20
  49.4 0.3 convolution_bitcast_fusion
  49.6 0.9 fusion.16
  50.7 6.2 %collective-permute-start.15 = (bf16[16,4096]{1,0:T(8,128)(2,1)S(1)}, bf16[16,4096]{1,0:T(8,128)(2,1)S(1)}, u32[]{:S(2)}, u32[]{:S(2)}) collective-permute-start(bf16[16,4096]{1,0:T(8,128)(2,1)S(1)} %reshape.153), channel_id=1, source_target_pairs={{0,8},{1,9},{2,10},{3,11},{4,12},{5,13},{6,14},{7,15},{8,0},{9,1},... | collective-permute-start | bytes 393224 | tf_op jit(solution)/shard_map/ppermute | solution.py:120
  56.9 1.6 %collective-permute-start.13 = (bf16[16,4096]{1,0:T(8,128)(2,1)S(1)}, bf16[16,4096]{1,0:T(8,128)(2,1)S(1)}, u32[]{:S(2)}, u32[]{:S(2)}) collective-permute-start(bf16[16,4096]{1,0:T(8,128)(2,1)S(1)} %reshape.153), channel_id=1, source_target_pairs={{0,2},{1,5},{2,0},{3,7},{4,6},{5,1},{6,4},{7,3},{8,10},{9,13},{10,... | collective-permute-start | bytes 393224 | tf_op jit(solution)/shard_map/ppermute | solution.py:120
  58.5 1.1 %collective-permute-start.12 = (bf16[16,4096]{1,0:T(8,128)(2,1)S(1)}, bf16[16,4096]{1,0:T(8,128)(2,1)S(1)}, u32[]{:S(2)}, u32[]{:S(2)}) collective-permute-start(bf16[16,4096]{1,0:T(8,128)(2,1)S(1)} %reshape.153), channel_id=1, source_target_pairs={{0,4},{1,3},{2,6},{3,1},{4,0},{5,7},{6,2},{7,5},{8,12},{9,11},{10,... | collective-permute-start | bytes 393224 | tf_op jit(solution)/shard_map/ppermute | solution.py:120
  59.6 4.3 %collective-permute-done.15 = bf16[16,4096]{1,0:T(8,128)(2,1)S(1)} collective-permute-done((bf16[16,4096]{1,0:T(8,128)(2,1)S(1)}, bf16[16,4096]{1,0:T(8,128)(2,1)S(1)}, u32[]{:S(2)}, u32[]{:S(2)}) %collective-permute-start.15) | collective-permute-done | bytes 131104 | tf_op jit(solution)/shard_map/ppermute | solution.py:120
  63.9 1.7 %collective-permute-start.17 = (bf16[16,4096]{1,0:T(8,128)(2,1)S(1)}, bf16[16,4096]{1,0:T(8,128)(2,1)S(1)}, u32[]{:S(2)}, u32[]{:S(2)}) collective-permute-start(bf16[16,4096]{1,0:T(8,128)(2,1)S(1)} %collective-permute-done.15), channel_id=1, source_target_pairs={{0,2},{1,5},{2,0},{3,7},{4,6},{5,1},{6,4},{7,3},{8,10},{9,13},{10,... | collective-permute-start | bytes 393224 | tf_op jit(solution)/shard_map/ppermute | solution.py:120
  65.6 0.7 collective-permute-start.14
  66.4 4.5 %collective-permute-done.16 = bf16[16,4096]{1,0:T(8,128)(2,1)S(1)} collective-permute-done((bf16[16,4096]{1,0:T(8,128)(2,1)S(1)}, bf16[16,4096]{1,0:T(8,128)(2,1)S(1)}, u32[]{:S(2)}, u32[]{:S(2)}) %collective-permute-start.16) | collective-permute-done | bytes 131104 | tf_op jit(solution)/shard_map/ppermute | solution.py:120
  70.8 1.4 %collective-permute-start.18 = (bf16[16,4096]{1,0:T(8,128)(2,1)S(1)}, bf16[16,4096]{1,0:T(8,128)(2,1)S(1)}, u32[]{:S(2)}, u32[]{:S(2)}) collective-permute-start(bf16[16,4096]{1,0:T(8,128)(2,1)S(1)} %collective-permute-done.16), channel_id=1, source_target_pairs={{0,2},{1,5},{2,0},{3,7},{4,6},{5,1},{6,4},{7,3},{8,10},{9,13},{10,... | collective-permute-start | bytes 393224 | tf_op jit(solution)/shard_map/ppermute | solution.py:120
  72.3 3.5 %collective-permute-done.18 = bf16[16,4096]{1,0:T(8,128)(2,1)S(1)} collective-permute-done((bf16[16,4096]{1,0:T(8,128)(2,1)S(1)}, bf16[16,4096]{1,0:T(8,128)(2,1)S(1)}, u32[]{:S(2)}, u32[]{:S(2)}) %collective-permute-start.18) | collective-permute-done | bytes 131104 | tf_op jit(solution)/shard_map/ppermute | solution.py:120
  75.8 5.1 %fusion.21 = f32[64,1024]{1,0:T(8,128)S(1)} fusion(bf16[4096,1024]{1,0:T(8,128)(2,1)} %param.15, bf16[64,4096]{1,0:T(8,128)(2,1)S(1)} %constant_dynamic-update-slice_fusion.8, bf16[64,4096]{1,0:T(8,128)(2,1)S(1)} %constant_dynamic-update-slice_fusion.4, pred[]{:T(512)S(6)} %eq.31), kind=kOutput, calls=%fused_computation.16 | convolution fusion | flops 537133056 | bytes 9699329 | tf_op jit(solution)/shard_map/dot_general | solution.py:241
  81.0 1.6 %fusion.23 = f32[64,1024]{1,0:T(8,128)S(1)} fusion(bf16[4096,1024]{1,0:T(8,128)(2,1)S(1)} %bitcast.107, bf16[64,4096]{1,0:T(8,128)(2,1)S(1)} %constant_dynamic-update-slice_fusion.4, bf16[64,4096]{1,0:T(8,128)(2,1)S(1)} %constant_dynamic-update-slice_fusion.8, pred[]{:T(512)S(6)} %eq.31), kind=kOutput, calls=%fused_computation.18 | convolution fusion | flops 537133056 | bytes 9699329 | tf_op jit(solution)/shard_map/dot_general | solution.py:241
  82.7 0.7 collective-permute-start.20
  83.4 0.7 collective-permute-start.23
  84.1 1.6 %collective-permute-start.22 = (bf16[16,1024]{1,0:T(8,128)(2,1)S(1)}, bf16[16,1024]{1,0:T(8,128)(2,1)S(1)}, u32[]{:S(2)}, u32[]{:S(2)}) collective-permute-start(bf16[16,1024]{1,0:T(8,128)(2,1)S(1)} %get-tuple-element.35), channel_id=1, source_target_pairs={{0,2},{1,12},{2,0},{3,14},{4,6},{5,8},{6,4},{7,10},{8,11},{9,5},{1... | collective-permute-start | bytes 98312 | tf_op jit(solution)/shard_map/ppermute | solution.py:150
  85.7 1.2 %collective-permute-start.21 = (bf16[16,1024]{1,0:T(8,128)(2,1)S(1)}, bf16[16,1024]{1,0:T(8,128)(2,1)S(1)}, u32[]{:S(2)}, u32[]{:S(2)}) collective-permute-start(bf16[16,1024]{1,0:T(8,128)(2,1)S(1)} %get-tuple-element.36), channel_id=1, source_target_pairs={{0,4},{1,10},{2,6},{3,8},{4,0},{5,14},{6,2},{7,12},{8,13},{9,3},{1... | collective-permute-start | bytes 98312 | tf_op jit(solution)/shard_map/ppermute | solution.py:150
  86.9 1.4 %collective-permute-done.23 = bf16[16,1024]{1,0:T(8,128)(2,1)S(1)} collective-permute-done((bf16[16,1024]{1,0:T(8,128)(2,1)S(1)}, bf16[16,1024]{1,0:T(8,128)(2,1)S(1)}, u32[]{:S(2)}, u32[]{:S(2)}) %collective-permute-start.23) | collective-permute-done | bytes 32800 | tf_op jit(solution)/shard_map/ppermute | solution.py:150
  88.4 1.2 %collective-permute-done.21 = bf16[16,1024]{1,0:T(8,128)(2,1)S(1)} collective-permute-done((bf16[16,1024]{1,0:T(8,128)(2,1)S(1)}, bf16[16,1024]{1,0:T(8,128)(2,1)S(1)}, u32[]{:S(2)}, u32[]{:S(2)}) %collective-permute-start.21) | collective-permute-done | bytes 32800 | tf_op jit(solution)/shard_map/ppermute | solution.py:150
  89.7 4.8 %collective-permute-start.24 = (bf16[16,4096]{1,0:T(8,128)(2,1)S(1)}, bf16[16,4096]{1,0:T(8,128)(2,1)S(1)}, u32[]{:S(2)}, u32[]{:S(2)}) collective-permute-start(bf16[16,4096]{1,0:T(8,128)(2,1)S(1)} %pad_maximum_fusion.7), channel_id=1, source_target_pairs={{0,1},{1,0},{2,3},{3,2},{4,5},{5,4},{6,7},{7,6},{8,9},{9,8},{10,11... | collective-permute-start | bytes 393224 | tf_op jit(solution)/shard_map/ppermute | solution.py:135
  94.5 1.0 %collective-permute-done.24 = bf16[16,4096]{1,0:T(8,128)(2,1)S(1)} collective-permute-done((bf16[16,4096]{1,0:T(8,128)(2,1)S(1)}, bf16[16,4096]{1,0:T(8,128)(2,1)S(1)}, u32[]{:S(2)}, u32[]{:S(2)}) %collective-permute-start.24) | collective-permute-done | bytes 131104 | tf_op jit(solution)/shard_map/ppermute | solution.py:135
  95.6 0.7 maximum_bitcast_fusion
  (93 shorter events, 3.1 us)
Async XLA Ops:
  0.0 26.7 %copy-start = (bf16[4096,128]{1,0:T(8,128)(2,1)S(1)}, bf16[4096,128]{1,0:T(8,128)(2,1)}, u32[]{:S(2)}) copy-start(bf16[4096,128]{1,0:T(8,128)(2,1)} %param.13) | copy-start | bytes 3145732
  0.0 27.0 %copy-start.2 = (bf16[4096,128]{1,0:T(8,128)(2,1)S(1)}, bf16[4096,128]{1,0:T(8,128)(2,1)}, u32[]{:S(2)}) copy-start(bf16[4096,128]{1,0:T(8,128)(2,1)} %param.14) | copy-start | bytes 3145732
  3.9 10.8 %collective-permute-start.3 = (bf16[16,4224]{1,0:T(8,128)(2,1)S(1)}, bf16[16,4224]{1,0:T(8,128)(2,1)}, u32[]{:S(2)}, u32[]{:S(2)}) collective-permute-start(bf16[16,4224]{1,0:T(8,128)(2,1)S(1)} %pad_maximum_fusion.5), channel_id=1, source_target_pairs={{0,8},{1,9},{2,10},{3,11},{4,12},{5,13},{6,14},{7,15},{8,0},{9,1},... | collective-permute-start | bytes 405512 | tf_op jit(solution)/shard_map/ppermute | solution.py:120
  8.0 10.4 %collective-permute-start.1 = (bf16[16,4224]{1,0:T(8,128)(2,1)S(1)}, bf16[16,4224]{1,0:T(8,128)(2,1)S(1)}, u32[]{:S(2)}, u32[]{:S(2)}) collective-permute-start(bf16[16,4224]{1,0:T(8,128)(2,1)S(1)} %pad_maximum_fusion.5), channel_id=1, source_target_pairs={{0,2},{1,5},{2,0},{3,7},{4,6},{5,1},{6,4},{7,3},{8,10},{9,13},{10,... | collective-permute-start | bytes 405512 | tf_op jit(solution)/shard_map/ppermute | solution.py:120
  9.5 6.1 %collective-permute-start = (bf16[16,4224]{1,0:T(8,128)(2,1)S(1)}, bf16[16,4224]{1,0:T(8,128)(2,1)S(1)}, u32[]{:S(2)}, u32[]{:S(2)}) collective-permute-start(bf16[16,4224]{1,0:T(8,128)(2,1)S(1)} %pad_maximum_fusion.5), channel_id=1, source_target_pairs={{0,4},{1,3},{2,6},{3,1},{4,0},{5,7},{6,2},{7,5},{8,12},{9,11},{10,... | collective-permute-start | bytes 405512 | tf_op jit(solution)/shard_map/ppermute | solution.py:120
  14.7 5.6 %collective-permute-start.4 = (bf16[16,4224]{1,0:T(8,128)(2,1)}, bf16[16,4224]{1,0:T(8,128)(2,1)}, u32[]{:S(2)}, u32[]{:S(2)}) collective-permute-start(bf16[16,4224]{1,0:T(8,128)(2,1)} %collective-permute-done.3), channel_id=1, source_target_pairs={{0,4},{1,3},{2,6},{3,1},{4,0},{5,7},{6,2},{7,5},{8,12},{9,11},{10,... | collective-permute-start | bytes 405512 | tf_op jit(solution)/shard_map/ppermute | solution.py:120
  15.6 6.0 %copy-start.3 = (bf16[16,4224]{1,0:T(8,128)(2,1)}, bf16[16,4224]{1,0:T(8,128)(2,1)S(1)}, u32[]{:S(2)}) copy-start(bf16[16,4224]{1,0:T(8,128)(2,1)S(1)} %collective-permute-done) | copy-start | bytes 405508
  15.6 6.0 %collective-permute-start.2 = (bf16[16,4224]{1,0:T(8,128)(2,1)S(1)}, bf16[16,4224]{1,0:T(8,128)(2,1)}, u32[]{:S(2)}, u32[]{:S(2)}) collective-permute-start(bf16[16,4224]{1,0:T(8,128)(2,1)S(1)} %collective-permute-done), channel_id=1, source_target_pairs={{0,2},{1,5},{2,0},{3,7},{4,6},{5,1},{6,4},{7,3},{8,10},{9,13},{10,... | collective-permute-start | bytes 405512 | tf_op jit(solution)/shard_map/ppermute | solution.py:120
  18.6 5.2 %collective-permute-start.5 = (bf16[16,4224]{1,0:T(8,128)(2,1)}, bf16[16,4224]{1,0:T(8,128)(2,1)S(1)}, u32[]{:S(2)}, u32[]{:S(2)}) collective-permute-start(bf16[16,4224]{1,0:T(8,128)(2,1)} %collective-permute-done.3), channel_id=1, source_target_pairs={{0,2},{1,5},{2,0},{3,7},{4,6},{5,1},{6,4},{7,3},{8,10},{9,13},{10,... | collective-permute-start | bytes 405512 | tf_op jit(solution)/shard_map/ppermute | solution.py:120
  20.3 5.3 %collective-permute-start.6 = (bf16[16,4224]{1,0:T(8,128)(2,1)}, bf16[16,4224]{1,0:T(8,128)(2,1)}, u32[]{:S(2)}, u32[]{:S(2)}) collective-permute-start(bf16[16,4224]{1,0:T(8,128)(2,1)} %collective-permute-done.4), channel_id=1, source_target_pairs={{0,2},{1,5},{2,0},{3,7},{4,6},{5,1},{6,4},{7,3},{8,10},{9,13},{10,... | collective-permute-start | bytes 405512 | tf_op jit(solution)/shard_map/ppermute | solution.py:120
  26.6 3.4 %copy-start.1 = (bf16[4096,1024]{1,0:T(8,128)(2,1)S(1)}, bf16[4096,1024]{1,0:T(8,128)(2,1)}, u32[]{:S(2)}) copy-start(bf16[4096,1024]{1,0:T(8,128)(2,1)} %param.12) | copy-start | bytes 25165828
  34.0 1.7 %collective-permute-start.7 = (f32[64,1280]{1,0:T(8,128)S(1)}, f32[64,1280]{1,0:T(8,128)S(1)}, u32[]{:S(2)}, u32[]{:S(2)}) collective-permute-start(f32[64,1280]{1,0:T(8,128)S(1)} %pad_maximum_fusion.2), channel_id=1, source_target_pairs={{0,1},{1,0},{2,3},{3,2},{4,5},{5,4},{6,7},{7,6},{8,9},{9,8},{10,11... | collective-permute-start | bytes 983048 | tf_op jit(solution)/shard_map/ppermute | solution.py:135
  36.4 4.2 %collective-permute-start.8 = (bf16[16,1280]{1,0:T(8,128)(2,1)S(1)}, bf16[16,1280]{1,0:T(8,128)(2,1)S(1)}, u32[]{:S(2)}, u32[]{:S(2)}) collective-permute-start(bf16[16,1280]{1,0:T(8,128)(2,1)S(1)} %get-tuple-element.25), channel_id=1, source_target_pairs={{0,0},{1,8},{2,2},{3,10},{4,4},{5,12},{6,6},{7,14},{8,9},{9,1},{10... | collective-permute-start | bytes 122888 | tf_op jit(solution)/shard_map/ppermute | solution.py:150
  37.0 4.1 %collective-permute-start.9 = (bf16[16,1280]{1,0:T(8,128)(2,1)S(1)}, bf16[16,1280]{1,0:T(8,128)(2,1)S(1)}, u32[]{:S(2)}, u32[]{:S(2)}) collective-permute-start(bf16[16,1280]{1,0:T(8,128)(2,1)S(1)} %get-tuple-element.26), channel_id=1, source_target_pairs={{0,4},{1,10},{2,6},{3,8},{4,0},{5,14},{6,2},{7,12},{8,13},{9,3},{1... | collective-permute-start | bytes 122888 | tf_op jit(solution)/shard_map/ppermute | solution.py:150
  38.7 4.9 %collective-permute-start.11 = (bf16[16,1280]{1,0:T(8,128)(2,1)S(1)}, bf16[16,1280]{1,0:T(8,128)(2,1)S(1)}, u32[]{:S(2)}, u32[]{:S(2)}) collective-permute-start(bf16[16,1280]{1,0:T(8,128)(2,1)S(1)} %get-tuple-element.27), channel_id=1, source_target_pairs={{0,6},{1,14},{2,4},{3,12},{4,2},{5,10},{6,0},{7,8},{8,15},{9,7},{1... | collective-permute-start | bytes 122888 | tf_op jit(solution)/shard_map/ppermute | solution.py:150
  39.8 4.3 %collective-permute-start.10 = (bf16[16,1280]{1,0:T(8,128)(2,1)S(1)}, bf16[16,1280]{1,0:T(8,128)(2,1)S(1)}, u32[]{:S(2)}, u32[]{:S(2)}) collective-permute-start(bf16[16,1280]{1,0:T(8,128)(2,1)S(1)} %get-tuple-element.28), channel_id=1, source_target_pairs={{0,2},{1,12},{2,0},{3,14},{4,6},{5,8},{6,4},{7,10},{8,11},{9,5},{1... | collective-permute-start | bytes 122888 | tf_op jit(solution)/shard_map/ppermute | solution.py:150
  44.2 5.4 %copy-start.4 = (bf16[8,512,4,128]{3,2,1,0:T(4,128)(2,1)S(1)}, bf16[8,512,4,128]{3,2,1,0:T(4,128)(2,1)}, u32[]{:S(2)}) copy-start(bf16[8,512,4,128]{3,2,1,0:T(4,128)(2,1)} %param.17) | copy-start | bytes 12582916
  50.7 13.2 %collective-permute-start.15 = (bf16[16,4096]{1,0:T(8,128)(2,1)S(1)}, bf16[16,4096]{1,0:T(8,128)(2,1)S(1)}, u32[]{:S(2)}, u32[]{:S(2)}) collective-permute-start(bf16[16,4096]{1,0:T(8,128)(2,1)S(1)} %reshape.153), channel_id=1, source_target_pairs={{0,8},{1,9},{2,10},{3,11},{4,12},{5,13},{6,14},{7,15},{8,0},{9,1},... | collective-permute-start | bytes 393224 | tf_op jit(solution)/shard_map/ppermute | solution.py:120
  56.9 9.4 %collective-permute-start.13 = (bf16[16,4096]{1,0:T(8,128)(2,1)S(1)}, bf16[16,4096]{1,0:T(8,128)(2,1)S(1)}, u32[]{:S(2)}, u32[]{:S(2)}) collective-permute-start(bf16[16,4096]{1,0:T(8,128)(2,1)S(1)} %reshape.153), channel_id=1, source_target_pairs={{0,2},{1,5},{2,0},{3,7},{4,6},{5,1},{6,4},{7,3},{8,10},{9,13},{10,... | collective-permute-start | bytes 393224 | tf_op jit(solution)/shard_map/ppermute | solution.py:120
  58.5 7.1 %collective-permute-start.12 = (bf16[16,4096]{1,0:T(8,128)(2,1)S(1)}, bf16[16,4096]{1,0:T(8,128)(2,1)S(1)}, u32[]{:S(2)}, u32[]{:S(2)}) collective-permute-start(bf16[16,4096]{1,0:T(8,128)(2,1)S(1)} %reshape.153), channel_id=1, source_target_pairs={{0,4},{1,3},{2,6},{3,1},{4,0},{5,7},{6,2},{7,5},{8,12},{9,11},{10,... | collective-permute-start | bytes 393224 | tf_op jit(solution)/shard_map/ppermute | solution.py:120
  63.9 8.4 %collective-permute-start.17 = (bf16[16,4096]{1,0:T(8,128)(2,1)S(1)}, bf16[16,4096]{1,0:T(8,128)(2,1)S(1)}, u32[]{:S(2)}, u32[]{:S(2)}) collective-permute-start(bf16[16,4096]{1,0:T(8,128)(2,1)S(1)} %collective-permute-done.15), channel_id=1, source_target_pairs={{0,2},{1,5},{2,0},{3,7},{4,6},{5,1},{6,4},{7,3},{8,10},{9,13},{10,... | collective-permute-start | bytes 393224 | tf_op jit(solution)/shard_map/ppermute | solution.py:120
  65.6 5.2 %collective-permute-start.16 = (bf16[16,4096]{1,0:T(8,128)(2,1)S(1)}, bf16[16,4096]{1,0:T(8,128)(2,1)S(1)}, u32[]{:S(2)}, u32[]{:S(2)}) collective-permute-start(bf16[16,4096]{1,0:T(8,128)(2,1)S(1)} %collective-permute-done.15), channel_id=1, source_target_pairs={{0,4},{1,3},{2,6},{3,1},{4,0},{5,7},{6,2},{7,5},{8,12},{9,11},{10,... | collective-permute-start | bytes 393224 | tf_op jit(solution)/shard_map/ppermute | solution.py:120
  65.6 6.7 %collective-permute-start.14 = (bf16[16,4096]{1,0:T(8,128)(2,1)S(1)}, bf16[16,4096]{1,0:T(8,128)(2,1)S(1)}, u32[]{:S(2)}, u32[]{:S(2)}) collective-permute-start(bf16[16,4096]{1,0:T(8,128)(2,1)S(1)} %collective-permute-done.12), channel_id=1, source_target_pairs={{0,2},{1,5},{2,0},{3,7},{4,6},{5,1},{6,4},{7,3},{8,10},{9,13},{10,... | collective-permute-start | bytes 393224 | tf_op jit(solution)/shard_map/ppermute | solution.py:120
  70.8 5.0 %collective-permute-start.18 = (bf16[16,4096]{1,0:T(8,128)(2,1)S(1)}, bf16[16,4096]{1,0:T(8,128)(2,1)S(1)}, u32[]{:S(2)}, u32[]{:S(2)}) collective-permute-start(bf16[16,4096]{1,0:T(8,128)(2,1)S(1)} %collective-permute-done.16), channel_id=1, source_target_pairs={{0,2},{1,5},{2,0},{3,7},{4,6},{5,1},{6,4},{7,3},{8,10},{9,13},{10,... | collective-permute-start | bytes 393224 | tf_op jit(solution)/shard_map/ppermute | solution.py:120
  72.2 8.8 %slice-start = ((s8[8388608]{0:T(1024)(128)(4,1)}), s8[4194304]{0:T(1024)(128)(4,1)S(1)}, s32[]{:S(2)}) async-start(s8[8388608]{0:T(1024)(128)(4,1)} %bitcast.106), calls=%async_computation | async-start | bytes 8388608
  75.8 5.2 %slice-start.1 = ((s8[8388608]{0:T(1024)(128)(4,1)}), s8[4194304]{0:T(1024)(128)(4,1)S(1)}, s32[]{:S(2)}) async-start(s8[8388608]{0:T(1024)(128)(4,1)} %bitcast.106), calls=%async_computation.1 | async-start | bytes 8388608
  80.9 1.7 %collective-permute-start.19 = (f32[64,1024]{1,0:T(8,128)S(1)}, f32[64,1024]{1,0:T(8,128)S(1)}, u32[]{:S(2)}, u32[]{:S(2)}) collective-permute-start(f32[64,1024]{1,0:T(8,128)S(1)} %fusion.21), channel_id=1, source_target_pairs={{0,1},{1,0},{2,3},{3,2},{4,5},{5,4},{6,7},{7,6},{8,9},{9,8},{10,11... | collective-permute-start | bytes 786440 | tf_op jit(solution)/shard_map/ppermute | solution.py:135
  82.7 4.2 %collective-permute-start.20 = (bf16[16,1024]{1,0:T(8,128)(2,1)S(1)}, bf16[16,1024]{1,0:T(8,128)(2,1)S(1)}, u32[]{:S(2)}, u32[]{:S(2)}) collective-permute-start(bf16[16,1024]{1,0:T(8,128)(2,1)S(1)} %get-tuple-element.33), channel_id=1, source_target_pairs={{0,0},{1,8},{2,2},{3,10},{4,4},{5,12},{6,6},{7,14},{8,9},{9,1},{10... | collective-permute-start | bytes 98312 | tf_op jit(solution)/shard_map/ppermute | solution.py:150
  83.4 5.0 %collective-permute-start.23 = (bf16[16,1024]{1,0:T(8,128)(2,1)S(1)}, bf16[16,1024]{1,0:T(8,128)(2,1)S(1)}, u32[]{:S(2)}, u32[]{:S(2)}) collective-permute-start(bf16[16,1024]{1,0:T(8,128)(2,1)S(1)} %get-tuple-element.34), channel_id=1, source_target_pairs={{0,6},{1,14},{2,4},{3,12},{4,2},{5,10},{6,0},{7,8},{8,15},{9,7},{1... | collective-permute-start | bytes 98312 | tf_op jit(solution)/shard_map/ppermute | solution.py:150
  84.1 4.3 %collective-permute-start.22 = (bf16[16,1024]{1,0:T(8,128)(2,1)S(1)}, bf16[16,1024]{1,0:T(8,128)(2,1)S(1)}, u32[]{:S(2)}, u32[]{:S(2)}) collective-permute-start(bf16[16,1024]{1,0:T(8,128)(2,1)S(1)} %get-tuple-element.35), channel_id=1, source_target_pairs={{0,2},{1,12},{2,0},{3,14},{4,6},{5,8},{6,4},{7,10},{8,11},{9,5},{1... | collective-permute-start | bytes 98312 | tf_op jit(solution)/shard_map/ppermute | solution.py:150
  85.7 3.9 %collective-permute-start.21 = (bf16[16,1024]{1,0:T(8,128)(2,1)S(1)}, bf16[16,1024]{1,0:T(8,128)(2,1)S(1)}, u32[]{:S(2)}, u32[]{:S(2)}) collective-permute-start(bf16[16,1024]{1,0:T(8,128)(2,1)S(1)} %get-tuple-element.36), channel_id=1, source_target_pairs={{0,4},{1,10},{2,6},{3,8},{4,0},{5,14},{6,2},{7,12},{8,13},{9,3},{1... | collective-permute-start | bytes 98312 | tf_op jit(solution)/shard_map/ppermute | solution.py:150
  89.7 5.8 %collective-permute-start.24 = (bf16[16,4096]{1,0:T(8,128)(2,1)S(1)}, bf16[16,4096]{1,0:T(8,128)(2,1)S(1)}, u32[]{:S(2)}, u32[]{:S(2)}) collective-permute-start(bf16[16,4096]{1,0:T(8,128)(2,1)S(1)} %pad_maximum_fusion.7), channel_id=1, source_target_pairs={{0,1},{1,0},{2,3},{3,2},{4,5},{5,4},{6,7},{7,6},{8,9},{9,8},{10,11... | collective-permute-start | bytes 393224 | tf_op jit(solution)/shard_map/ppermute | solution.py:135

commit v2 on v1

--- a/solution.py
+++ b/solution.py
@@ -3,6 +3,8 @@
 import jax
 import jax.numpy as jnp
 from jax import lax
+from jax.experimental import pallas as pl
+from jax.experimental.pallas import tpu as pltpu
 from jax.sharding import PartitionSpec as P
 
 HEAD_SIZE = 128
@@ -151,31 +153,175 @@
     return received
 
 
+def place_of(column, crossed):
+    offset = column ^ (lax.axis_index("out") % 4)
+    swapped = jnp.where((offset == 1) | (offset == 2), 3 - offset, offset)
+    return jnp.where(crossed == 0, swapped, offset)
+
+
+def crossing(core):
+    return (lax.axis_index("out") // 4) ^ core
+
+
 def in_order(received):
-    own_out = lax.axis_index("out")
-    own_core = lax.axis_index("inp")
-    crossed = (own_out // 4) ^ own_core
+    crossed = crossing(lax.axis_index("inp"))
     stacked = jnp.stack(received)
-    ordered = []
+    return jnp.stack([lax.dynamic_index_in_dim(stacked, place_of(c, crossed), 0, keepdims=False) for c in range(4)])
+
+
+VMEM_SPEC = pl.BlockSpec(memory_space=pltpu.VMEM)
+SMEM_SPEC = pl.BlockSpec(memory_space=pltpu.SMEM)
+MEGABYTE = 1 << 20
+
+
+def on_chip(kernel, out_shape, scalars, *operands, scratch=(), megabytes=16, moved=1, place=VMEM_SPEC):
+    return pl.pallas_call(
+        kernel,
+        out_shape=out_shape,
+        in_specs=[SMEM_SPEC] * len(scalars) + [place] * len(operands),
+        out_specs=jax.tree.map(lambda _: VMEM_SPEC, out_shape),
+        scratch_shapes=scratch,
+        compiler_params=pltpu.CompilerParams(vmem_limit_bytes=megabytes * MEGABYTE),
+        cost_estimate=pl.CostEstimate(flops=0, bytes_accessed=moved * MEGABYTE, transcendentals=0),
+    )(*scalars, *operands)
+
+
+def norm_kernel(position_hbm, token_hbm, gain_hbm, out_ref, position_ref, token_ref, gain_ref, arrivals):
+    pairs = ((token_hbm, token_ref), (gain_hbm, gain_ref), (position_hbm, position_ref))
+    copies = [pltpu.make_async_copy(source, target, arrivals.at[n]) for n, (source, target) in enumerate(pairs)]
+    for copy in copies:
+        copy.start()
+    core = lax.axis_index("inp")
+    half = token_ref.shape[1] // 2
+    rows = position_ref.shape[0]
+    own = pl.ds(pl.multiple_of(core * half, 128), half)
+    copies[0].wait()
+    values = token_ref[...].astype(jnp.float32)
+    factor = lax.rsqrt(jnp.mean(values * values, axis=-1, keepdims=True) + 1e-05)
+    copies[1].wait()
+    out_ref[:, :half] = (token_ref[:, own].astype(jnp.float32) * factor * gain_ref[:, own]).astype(jnp.bfloat16)
+    shape = (token_ref.shape[0], 128)
+    row = lax.broadcasted_iota(jnp.int32, shape, 0) % rows
+    lane = lax.broadcasted_iota(jnp.int32, shape, 1)
+    tag = jnp.zeros(shape, jnp.int32)
+    copies[2].wait()
+    for r in range(rows):
+        place = position_ref[r]
+        tag = jnp.where(row == r, jnp.where(lane == 0, place // 128, place % 128), tag)
+    out_ref[:, half:] = tag.astype(jnp.float32).astype(jnp.bfloat16)
+
+
+def fetch_kernel(*refs):
+    count = (len(refs) - 1) // 2
+    arrivals = refs[-1]
+    copies = []
+    for n in range(count):
+        source, target = refs[n], refs[count + n]
+        size = source.shape[0] // 4
+        for part in range(4):
+            here = pl.ds(part * size, size)
+            copies.append(pltpu.make_async_copy(source.at[here], target.at[here], arrivals.at[n, part]))
+    for copy in copies:
+        copy.start()
+    for copy in copies:
+        copy.wait()
+
+
+def distant(array):
+    return pltpu.with_memory_space_constraint(array, pltpu.HBM)
+
+
+def fetched(*arrays):
+    return pl.pallas_call(
+        fetch_kernel,
+        out_shape=[pltpu.VMEM(array.shape, array.dtype) for array in arrays],
+        in_specs=[pl.BlockSpec(memory_space=pl.ANY)] * len(arrays),
+        out_specs=[VMEM_SPEC] * len(arrays),
+        scratch_shapes=[pltpu.SemaphoreType.DMA((len(arrays), 4))],
+        compiler_params=pltpu.CompilerParams(vmem_limit_bytes=MEGABYTE),
+        cost_estimate=pl.CostEstimate(
+            flops=0,
+            bytes_accessed=sum(array.size * array.dtype.itemsize for array in arrays),
+            transcendentals=0,
+        ),
+    )(*map(distant, arrays))
+
+
+def stack_rows(core, pieces, rows_ref):
+    rows, depth = pieces[0].shape[0], rows_ref.shape[1]
+    for n, piece in enumerate(pieces):
+        upper = n // 4
+        half = (upper + core + 1) % 2
+        start = pl.multiple_of((half * 4 + n % 4) * rows, rows)
+        rows_ref[pl.ds(start, rows), :] = piece[:, :depth]
+
+
+def project_kernel(*refs):
+    core = lax.axis_index("inp")
+    pieces, (query_ref, key_ref, value_ref, given_ref, kept_ref, tag_ref, rows_ref) = refs[:8], refs[8:]
+    stack_rows(core, pieces, rows_ref)
+    count = given_ref.shape[0]
+    rows, depth = pieces[0].shape[0], rows_ref.shape[1]
+    for n in range(4):
+        lower, upper = pieces[n][:, depth:], pieces[n + 4][:, depth:]
+        tag_ref[pl.ds(n * rows, rows), :] = jnp.where(core == 0, lower.astype(jnp.float32), upper.astype(jnp.float32))
+    first = 0
+    for weight_ref in (query_ref, key_ref, value_ref):
+        width = weight_ref.shape[1]
+        block = min(256, width)
+        for at in range(0, width, block):
+            sums = jnp.dot(rows_ref[...], weight_ref[:, at : at + block], preferred_element_type=jnp.float32)
+            given_ref[:, first + at : first + at + block] = sums[:count]
+            kept_ref[:, first + at : first + at + block] = sums[count:]
+        first += width
+
+
+def mix_kernel(*refs):
+    core = lax.axis_index("inp")
+    pieces, (weight_ref, given_ref, kept_ref, rows_ref) = refs[:8], refs[8:]
+    stack_rows(core, pieces, rows_ref)
+    count = given_ref.shape[0]
+    for at in range(0, weight_ref.shape[1], 256):
+        sums = jnp.dot(rows_ref[...], weight_ref[:, at : at + 256], preferred_element_type=jnp.float32)
+        given_ref[:, at : at + 256] = sums[:count]
+        kept_ref[:, at : at + 256] = sums[count:]
+
+
+ARRIVAL = (0, 2, 1, 3)
+
+
+def turn_kernel(kept_ref, arrived_ref, cosine_ref, sine_ref, *out_refs):
+    rows = out_refs[0].shape[0]
+    heads = kept_ref.shape[1] // HEAD_SIZE
+    for n, out_ref in enumerate(out_refs):
+        here = pl.ds(n * rows, rows)
+        there = pl.ds(ARRIVAL[n] * rows, rows)
+        cosine, sine = cosine_ref[here, :], sine_ref[here, :]
+        for head in range(heads):
+            columns = slice(head * HEAD_SIZE, (head + 1) * HEAD_SIZE)
+            total = kept_ref[here, columns] + arrived_ref[there, columns]
+            if head < heads - 1:
+                total = total * cosine + pltpu.roll(total, HEAD_SIZE // 2, 1) * sine
+            out_ref[:, columns] = total.astype(jnp.bfloat16)
+
+
+def round_kernel(kept_ref, arrived_ref, *out_refs):
+    rows = out_refs[0].shape[0]
+    for n, out_ref in enumerate(out_refs):
+        total = kept_ref[pl.ds(n * rows, rows), :] + arrived_ref[pl.ds(ARRIVAL[n] * rows, rows), :]
+        out_ref[...] = total.astype(jnp.bfloat16)
+
+
+def place_kernel(own_places, other_places, own_ref, other_ref, out_ref):
+    core = lax.axis_index("inp")
+    width = own_ref.shape[2]
     for column in range(4):
-        offset = column ^ (own_out % 4)
-        swapped = jnp.where((offset == 1) | (offset == 2), 3 - offset, offset)
-        place = jnp.where(crossed == 0, swapped, offset)
-        ordered.append(lax.dynamic_index_in_dim(stacked, place, 0, keepdims=False))
-    return ordered
-
-
-def pair_summed(lower, upper, multiply):
-    core = lax.axis_index("inp")
-    lower = jnp.concatenate(lower)
-    upper = jnp.concatenate(upper)
-    given = multiply(jnp.where(core == 0, upper, lower))
-    kept = multiply(jnp.where(core == 0, lower, upper))
-    count = kept.shape[0] // 4
-    arrived = swap_cores(given)
-    arrived = arrived.reshape(4, count, -1)
-    arrived = jnp.stack([arrived[0], arrived[2], arrived[1], arrived[3]])
-    return kept.reshape(arrived.shape) + arrived
+        own = own_ref[own_places[column]]
+        other = other_ref[other_places[column]]
+        left = jnp.where(core == 0, own.astype(jnp.float32), other.astype(jnp.float32))
+        right = jnp.where(core == 0, other.astype(jnp.float32), own.astype(jnp.float32))
+        out_ref[:, column * width : (column + 1) * width] = left.astype(jnp.bfloat16)
+        out_ref[:, (column + 4) * width : (column + 5) * width] = right.astype(jnp.bfloat16)
 
 
 def attend_both(queries, new_keys, new_values, cache_keys, cache_values, lengths):
@@ -198,54 +344,95 @@
     return attended.astype(jnp.bfloat16)
 
 
+def resident(array):
+    return pltpu.with_memory_space_constraint(array, pltpu.VMEM)
+
+
 def eight_chip_body(
     tokens, norm_gain, query_weight, key_matrix, value_matrix, output_weight, cache_keys, cache_values, lengths, positions
 ):
     steps, rows, width = tokens.shape
+    count = steps * rows
+    half = width // 2
     core = lax.axis_index("inp")
-    half = width // 2
     query_cols = query_weight.shape[1]
-    key_cols = key_matrix.shape[1]
-    normed = rms_normed(tokens, norm_gain)
-    own = lax.dynamic_slice_in_dim(normed, core * half, half, 2).reshape(steps * rows, half)
-    tag = jnp.stack([positions // 128, positions % 128], axis=-1).astype(jnp.bfloat16)
-    tag = jnp.pad(jnp.tile(tag, (steps, 1)), ((0, 0), (0, 126)))
-    lower, upper = gather_blocks(jnp.concatenate([own, tag], axis=1))
-
-    def multiply(block):
-        return jnp.concatenate(
-            [
-                jnp.dot(block[:, :half], weight, preferred_element_type=jnp.float32)
-                for weight in (query_weight, key_matrix, value_matrix)
-            ],
-            axis=-1,
-        )
-
-    sums = pair_summed(lower, upper, multiply)
-    tags = jnp.where(core == 0, jnp.stack([b[:, half : half + 2] for b in lower]), jnp.stack([b[:, half : half + 2] for b in upper]))
-    tags = tags.astype(jnp.float32)
-    placed = tags[..., 0] * 128.0 + tags[..., 1]
-    placed = placed.reshape(4, steps, rows) + jnp.arange(steps, dtype=jnp.float32)[None, :, None]
-    placed = placed.reshape(4, steps * rows)
-    turned = query_cols + key_cols
-    rotated = rotate(sums[..., :turned].reshape(4, steps * rows, -1, HEAD_SIZE), placed)
-    outgoing = jnp.concatenate([rotated.reshape(4, steps * rows, turned), sums[..., turned:]], axis=-1).astype(jnp.bfloat16)
-    heads = jnp.stack(in_order(hand_out([outgoing[k] for k in range(4)])))
-    heads = heads.reshape(4, steps, rows, -1, HEAD_SIZE)
+    qkv_cols = query_cols + 2 * key_matrix.shape[1]
+    shape = jax.ShapeDtypeStruct
+    own = on_chip(
+        norm_kernel,
+        shape((count, half + 128), jnp.bfloat16),
+        (),
+        distant(positions),
+        distant(tokens.reshape(count, width)),
+        distant(norm_gain.reshape(1, width)),
+        scratch=[
+            pltpu.SMEM((rows,), jnp.int32),
+            pltpu.VMEM((count, width), jnp.bfloat16),
+            pltpu.VMEM((1, width), jnp.float32),
+            pltpu.SemaphoreType.DMA((3,)),
+        ],
+        place=pl.BlockSpec(memory_space=pltpu.HBM),
+    )
+    near_query, near_key, near_value = fetched(query_weight, key_matrix, value_matrix)
+    cache_keys, cache_values = fetched(cache_keys, cache_values)
+    lower, upper = gather_blocks(own)
+    given, kept, tags = on_chip(
+        project_kernel,
+        [shape((4 * count, qkv_cols), jnp.float32)] * 2 + [shape((4 * count, 128), jnp.float32)],
+        (),
+        *lower,
+        *upper,
+        resident(near_query),
+        resident(near_key),
+        resident(near_value),
+        scratch=[pltpu.VMEM((8 * count, half), jnp.bfloat16)],
+    )
+    arrived = swap_cores(given)
+    frequency = jnp.exp(
+        -math.log(500000.0) * 2.0 * jnp.arange(HEAD_SIZE // 2, dtype=jnp.float32) / HEAD_SIZE
+    )
+    step = (jnp.arange(4 * count) // rows % steps).astype(jnp.float32)
+    angles = (tags[:, 0] * 128.0 + tags[:, 1] + step)[:, None] * frequency
+    cosine, sine = jnp.cos(angles), jnp.sin(angles)
+    outgoing = on_chip(
+        turn_kernel,
+        [shape((count, qkv_cols), jnp.bfloat16)] * 4,
+        (),
+        kept,
+        arrived,
+        jnp.concatenate([cosine, cosine], axis=-1),
+        jnp.concatenate([-sine, sine], axis=-1),
+    )
+    heads = in_order(hand_out(outgoing)).reshape(4, steps, rows, -1, HEAD_SIZE)
     group = query_cols // HEAD_SIZE
     attended = attend_both(
         heads[:, :, :, :group], heads[:, :, :, group], heads[:, :, :, group + 1], cache_keys, cache_values, lengths
     )
-    lower, upper = gather_blocks(attended.reshape(steps * rows, half))
-    mixed = pair_summed(
-        lower, upper, lambda block: jnp.dot(block, output_weight, preferred_element_type=jnp.float32)
-    ).astype(jnp.bfloat16)
-    own_half = jnp.concatenate(in_order(hand_out([mixed[k] for k in range(4)])), axis=-1)
-    other_half = swap_cores(own_half)
-    whole = jnp.concatenate(
-        [jnp.where(core == 0, own_half, other_half), jnp.where(core == 0, other_half, own_half)], axis=-1
-    )
-    return whole.reshape(steps, rows, width)
+    lower, upper = gather_blocks(attended.reshape(count, half))
+    mix_cols = output_weight.shape[1]
+    given, kept = on_chip(
+        mix_kernel,
+        [shape((4 * count, mix_cols), jnp.float32)] * 2,
+        (),
+        *lower,
+        *upper,
+        resident(output_weight),
+        scratch=[pltpu.VMEM((8 * count, half), jnp.bfloat16)],
+    )
+    outgoing = on_chip(
+        round_kernel, [shape((count, mix_cols), jnp.bfloat16)] * 4, (), kept, swap_cores(given)
+    )
+    own_half = jnp.stack(hand_out(outgoing))
+    own_places = jnp.stack([place_of(c, crossing(core)) for c in range(4)]).astype(jnp.int32)
+    other_places = jnp.stack([place_of(c, crossing(1 - core)) for c in range(4)]).astype(jnp.int32)
+    mixed = on_chip(
+        place_kernel,
+        shape((count, width), jnp.bfloat16),
+        (own_places, other_places),
+        own_half,
+        swap_cores(own_half),
+    )
+    return mixed.reshape(steps, rows, width)
 
 
 def body(

time: 96.8 us -> 80.9 us (0.84)
  matrix products: 16.9 us -> 3.24 us
  Pallas kernels: 0 us -> 13.4 us
  local copies, waits for them, and re-layouts: 9.6 us -> 0.15 us
  other arithmetic: 7.04 us -> 1.92 us
    pallas_call x0 -> x8, Pallas kernels: none -> 13.4 us  [the longest x2 7.51 us: fetched(): pl.pallas_call(fetch_kernel, out_shape=[pltpu.VMEM(array.shape, array.dty...]
    dot_general x8 -> x0, matrix products: 11.1 us -> none  [the longest x2 6.69 us: eight_chip_body(): jnp.dot(block, output_weight, preferred_element_type=jnp.float32)]
    unnamed x24 -> x4, local copies, waits for them, and re-layouts: 4 us -> 0.02 us
    ppermute x8, waiting for transfers between devices: 6.2 us -> 2.72 us  [hand_out(): received.append(lax.ppermute(block, ('out', 'inp'), pairs))]
    slice x18 -> x1, local copies, waits for them, and re-layouts: 3.45 us -> 0.01 us  [eight_chip_body(): heads[:, :, :, group + 1]]
    dot_general x1, matrix products: 3.85 us -> 1.37 us  [attend_both(): jnp.einsum('ktrgd,rckd->rktgc', queries, cache_keys, preferred_element_ty...]
    ppermute x14, waiting for transfers between devices: 16.5 us -> 18.9 us  [swap_blocks(): return lax.ppermute(block, ('out', 'inp'), pairs)]
    ppermute x3, waiting for transfers between devices: 2.36 us -> 3.75 us  [swap_cores(): return lax.ppermute(block, 'inp', [(0, 1), (1, 0)])]
  transfers between devices with their start and end apart: 25 -> 25, of which waited for: 15 -> 12; matrix products, arithmetic and copies ran while one was open for 9% -> 1% of each run, Pallas kernels for 0% -> 9%
where the time goes in v2:
time: 80.9 us; the launch traced here: 80.7 us
  starting transfers between devices  36.3 us (45%)
  waiting for transfers between devices  25.4 us (31%)
  Pallas kernels  13.4 us (17%)
  matrix products  3.24 us (4%)
  other arithmetic  1.92 us (2%)
    ppermute x14, starting transfers between devices, swap_blocks(): return lax.ppermute(block, ('out', 'inp'), pairs)  22.9 us
    ppermute x14, waiting for transfers between devices, swap_blocks(): return lax.ppermute(block, ('out', 'inp'), pairs)  18.9 us
    ppermute x8, starting transfers between devices, hand_out(): received.append(lax.ppermute(block, ('out', 'inp'), pairs))  8.4 us
    pallas_call x2, Pallas kernels, fetched(): pl.pallas_call(fetch_kernel, out_shape=[pltpu.VMEM(array.shape, array.dty...  7.51 us
    pallas_call x6, Pallas kernels, on_chip(): pl.pallas_call(kernel, out_shape=out_shape, in_specs=[SMEM_SPEC] * len(sc...  5.93 us
    ppermute x3, starting transfers between devices, swap_cores(): return lax.ppermute(block, 'inp', [(0, 1), (1, 0)])  4.96 us
    ppermute x3, waiting for transfers between devices, swap_cores(): return lax.ppermute(block, 'inp', [(0, 1), (1, 0)])  3.75 us
    ppermute x8, waiting for transfers between devices, hand_out(): received.append(lax.ppermute(block, ('out', 'inp'), pairs))  2.72 us
  transfers between devices with their start and end apart: 25, of which 12 were waited for; matrix products, arithmetic and copies ran while one was open for 1% of the time, Pallas kernels for 9%

profile of v2, /device:TPU:0, one launch (start us, length us, event | category | flops | bytes accessed | tf_op | source)
XLA Modules:
  0.0 80.7 jit_solution(10428908344106177045)
XLA Ops:
  0.0 1.2 %shard_map.101.refs_0_ = bf16[16,4224]{1,0:T(8,128)(2,1)S(1)} custom-call(s32[8]{0:T(128)} %position_hbm.1, bf16[16,8192]{1,0:T(8,128)(2,1)} %bitcast.48, f32[1,8192]{1,0:T(1,128)} %bitcast.53), custom_call_target="tpu_custom_call" | custom-call | bytes 1048576 | tf_op jit(solution)/shard_map/pallas_call | solution.py:178
  1.2 4.1 %collective-permute-start.3 = (bf16[16,4224]{1,0:T(8,128)(2,1)S(1)}, bf16[16,4224]{1,0:T(8,128)(2,1)S(1)}, u32[]{:S(2)}, u32[]{:S(2)}) collective-permute-start(bf16[16,4224]{1,0:T(8,128)(2,1)S(1)} %shard_map.101.refs_0_), channel_id=1, source_target_pairs={{0,8},{1,9},{2,10},{3,11},{4,12},{5,13},{6,14},{7,15},{8,0},{9,1},... | collective-permute-start | bytes 405512 | tf_op jit(solution)/shard_map/ppermute | solution.py:122
  5.3 1.6 %collective-permute-start = (bf16[16,4224]{1,0:T(8,128)(2,1)S(1)}, bf16[16,4224]{1,0:T(8,128)(2,1)S(1)}, u32[]{:S(2)}, u32[]{:S(2)}) collective-permute-start(bf16[16,4224]{1,0:T(8,128)(2,1)S(1)} %shard_map.101.refs_0_), channel_id=1, source_target_pairs={{0,4},{1,3},{2,6},{3,1},{4,0},{5,7},{6,2},{7,5},{8,12},{9,11},{10,... | collective-permute-start | bytes 405512 | tf_op jit(solution)/shard_map/ppermute | solution.py:122
  6.9 5.0 %collective-permute-done.3.refs_4_ = bf16[16,4224]{1,0:T(8,128)(2,1)S(1)} collective-permute-done((bf16[16,4224]{1,0:T(8,128)(2,1)S(1)}, bf16[16,4224]{1,0:T(8,128)(2,1)S(1)}, u32[]{:S(2)}, u32[]{:S(2)}) %collective-permute-start.3) | collective-permute-done | bytes 135200 | tf_op jit(solution)/shard_map/ppermute | solution.py:122
  11.9 0.6 collective-permute-start.4
  12.5 1.5 %collective-permute-start.1 = (bf16[16,4224]{1,0:T(8,128)(2,1)S(1)}, bf16[16,4224]{1,0:T(8,128)(2,1)S(1)}, u32[]{:S(2)}, u32[]{:S(2)}) collective-permute-start(bf16[16,4224]{1,0:T(8,128)(2,1)S(1)} %shard_map.101.refs_0_), channel_id=1, source_target_pairs={{0,2},{1,5},{2,0},{3,7},{4,6},{5,1},{6,4},{7,3},{8,10},{9,13},{10,... | collective-permute-start | bytes 405512 | tf_op jit(solution)/shard_map/ppermute | solution.py:122
  14.1 0.5 collective-permute-start.5
  14.6 0.0 collective-permute-done.refs_1_
  14.6 1.5 %collective-permute-start.2 = (bf16[16,4224]{1,0:T(8,128)(2,1)S(1)}, bf16[16,4224]{1,0:T(8,128)(2,1)S(1)}, u32[]{:S(2)}, u32[]{:S(2)}) collective-permute-start(bf16[16,4224]{1,0:T(8,128)(2,1)S(1)} %collective-permute-done.refs_1_), channel_id=1, source_target_pairs={{0,2},{1,5},{2,0},{3,7},{4,6},{5,1},{6,4},{7,3},{8,10},{9,13},{10,... | collective-permute-start | bytes 405512 | tf_op jit(solution)/shard_map/ppermute | solution.py:122
  16.1 2.3 %collective-permute-done.4.refs_5_ = bf16[16,4224]{1,0:T(8,128)(2,1)S(1)} collective-permute-done((bf16[16,4224]{1,0:T(8,128)(2,1)S(1)}, bf16[16,4224]{1,0:T(8,128)(2,1)S(1)}, u32[]{:S(2)}, u32[]{:S(2)}) %collective-permute-start.4) | collective-permute-done | bytes 135200 | tf_op jit(solution)/shard_map/ppermute | solution.py:122
  18.4 1.7 %collective-permute-start.6 = (bf16[16,4224]{1,0:T(8,128)(2,1)S(1)}, bf16[16,4224]{1,0:T(8,128)(2,1)S(1)}, u32[]{:S(2)}, u32[]{:S(2)}) collective-permute-start(bf16[16,4224]{1,0:T(8,128)(2,1)S(1)} %collective-permute-done.4.refs_5_), channel_id=1, source_target_pairs={{0,2},{1,5},{2,0},{3,7},{4,6},{5,1},{6,4},{7,3},{8,10},{9,13},{10,... | collective-permute-start | bytes 405512 | tf_op jit(solution)/shard_map/ppermute | solution.py:122
  20.0 0.7 iota_compare_fusion
  20.7 4.0 %shard_map.102 = (bf16[4096,1024]{1,0:T(8,128)(2,1)S(1)}, bf16[4096,128]{1,0:T(8,128)(2,1)S(1)}, bf16[4096,128]{1,0:T(8,128)(2,1)S(1)}) custom-call(bf16[4096,1024]{1,0:T(8,128)(2,1)} %refs_0_.3, bf16[4096,128]{1,0:T(8,128)(2,1)} %refs_1_.3, bf16[4096,128]{1,0:T(8,128)(2,1)} %refs_2_.1), custom_call_target="tpu_custom_call" | custom-call | bytes 10485760 | tf_op jit(solution)/shard_map/pallas_call | solution.py:235
  24.8 0.0 collective-permute-done.5.refs_6_
  24.8 1.9 %shard_map.103 = (f32[64,1280]{1,0:T(8,128)S(1)}, f32[64,1280]{1,0:T(8,128)S(1)}, f32[64,128]{1,0:T(8,128)S(1)}) custom-call(bf16[16,4224]{1,0:T(8,128)(2,1)S(1)} %shard_map.101.refs_0_, bf16[16,4224]{1,0:T(8,128)(2,1)S(1)} %collective-permute-done.refs_1_, bf16[16,4224]{1,0:T(8,128)(2,1)S(1)} %collective-permute-done.1.refs_2_, ...), custom_call_target="tpu_custom_call" | custom-call | bytes 1048576 | tf_op jit(solution)/shard_map/pallas_call | solution.py:178
  26.8 0.2 fusion.22
  26.9 0.1 collective-permute-start.7
  27.0 0.2 fusion.28
  27.2 0.1 pad_maximum_fusion.2
  27.3 1.3 %collective-permute-done.7.arrived_ref = f32[64,1280]{1,0:T(8,128)S(1)} collective-permute-done((f32[64,1280]{1,0:T(8,128)S(1)}, f32[64,1280]{1,0:T(8,128)S(1)}, u32[]{:S(2)}, u32[]{:S(2)}) %collective-permute-start.7) | collective-permute-done | bytes 327712 | tf_op jit(solution)/shard_map/ppermute | solution.py:137
  28.6 0.1 shard_map.104
  28.8 0.7 collective-permute-start.8
  29.5 0.5 collective-permute-start.9
  30.0 0.3 collective-permute-start.10
  30.2 2.8 %collective-permute-start.11 = (bf16[16,1280]{1,0:T(8,128)(2,1)S(1)}, bf16[16,1280]{1,0:T(8,128)(2,1)S(1)}, u32[]{:S(2)}, u32[]{:S(2)}) collective-permute-start(bf16[16,1280]{1,0:T(8,128)(2,1)S(1)} %get-tuple-element.33), channel_id=1, source_target_pairs={{0,6},{1,14},{2,4},{3,12},{4,2},{5,10},{6,0},{7,8},{8,15},{9,7},{1... | collective-permute-start | bytes 122888 | tf_op jit(solution)/shard_map/ppermute | solution.py:152
  33.0 3.5 %shard_map.100 = (bf16[8,512,4,128]{3,2,1,0:T(4,128)(2,1)S(1)}, bf16[8,512,4,128]{3,2,1,0:T(4,128)(2,1)S(1)}) custom-call(bf16[8,512,4,128]{3,2,1,0:T(4,128)(2,1)} %refs_0_.2, bf16[8,512,4,128]{3,2,1,0:T(4,128)(2,1)} %refs_1_.2), custom_call_target="tpu_custom_call" | custom-call | bytes 8388608 | tf_op jit(solution)/shard_map/pallas_call | solution.py:235
  36.5 0.0 collective-permute-done.8
  36.5 0.0 collective-permute-done.9
  36.5 0.0 collective-permute-done.11
  36.7 0.7 fusion.31
  37.4 0.0 slice-start
  37.4 1.4 %fusion.30 = (f32[8,4,2,8]{3,2,1,0:T(2,128)S(1)}, f32[8,4,2,8,512]{4,3,2,1,0:T(8,128)S(1)}) fusion(bf16[8,512,4,128,1]{3,2,1,0,4:T(4,128)(2,1)S(1)} %bitcast.42, bf16[4,2,8,8,128]{4,2,3,1,0:T(8,128)(2,1)S(1)} %slice.20, pred[8,512]{1,0:T(8,128)(4,1)S(1)} %iota_compare_fusion), kind=kOutput, calls=%fused_computation.57 | convolution fusion | flops 67894784 | bytes 5380096 | tf_op jit(solution)/shard_map/ktrgd,rckd->rktgc/dot_general | solution.py:330
  38.8 0.1 fusion.18
  38.9 0.4 fusion.13
  39.3 0.0 slice-start.1
  39.4 0.9 %fusion.2 = f32[8,4,128,2,8]{2,4,3,1,0:T(8,128)S(1)} fusion(bf16[8,512,4,128,1]{3,2,1,0,4:T(4,128)(2,1)S(1)} %bitcast.47, f32[8,4,2,8,512]{4,3,2,1,0:T(8,128)S(1)} %get-tuple-element.51, f32[8,4,2,8]{3,2,1,0:T(2,128)S(1)} %add.77, f32[8,4,2,8]{3,2,1,0:T(2,128)S(1)} %max.7), kind=kOutput, calls=%fused_computation.2 | convolution fusion | flops 67895296 | bytes 5509120 | tf_op jit(solution)/shard_map/rktgc,rckd->trkgd/dot_general | solution.py:342
  40.2 0.3 fusion.11
  40.5 0.1 copy.22
  40.6 4.9 %collective-permute-start.15 = (bf16[16,4096]{1,0:T(8,128)(2,1)S(1)}, bf16[16,4096]{1,0:T(8,128)(2,1)S(1)}, u32[]{:S(2)}, u32[]{:S(2)}) collective-permute-start(bf16[16,4096]{1,0:T(8,128)(2,1)S(1)} %bitcast.43), channel_id=1, source_target_pairs={{0,8},{1,9},{2,10},{3,11},{4,12},{5,13},{6,14},{7,15},{8,0},{9,1},... | collective-permute-start | bytes 393224 | tf_op jit(solution)/shard_map/ppermute | solution.py:122
  45.6 3.2 %collective-permute-start.12 = (bf16[16,4096]{1,0:T(8,128)(2,1)S(1)}, bf16[16,4096]{1,0:T(8,128)(2,1)S(1)}, u32[]{:S(2)}, u32[]{:S(2)}) collective-permute-start(bf16[16,4096]{1,0:T(8,128)(2,1)S(1)} %bitcast.44), channel_id=1, source_target_pairs={{0,4},{1,3},{2,6},{3,1},{4,0},{5,7},{6,2},{7,5},{8,12},{9,11},{10,... | collective-permute-start | bytes 393224 | tf_op jit(solution)/shard_map/ppermute | solution.py:122
  48.7 3.7 %collective-permute-done.15.refs_4_ = bf16[16,4096]{1,0:T(8,128)(2,1)S(1)} collective-permute-done((bf16[16,4096]{1,0:T(8,128)(2,1)S(1)}, bf16[16,4096]{1,0:T(8,128)(2,1)S(1)}, u32[]{:S(2)}, u32[]{:S(2)}) %collective-permute-start.15) | collective-permute-done | bytes 131104 | tf_op jit(solution)/shard_map/ppermute | solution.py:122
  52.4 0.0 collective-permute-start.16
  52.4 1.3 %collective-permute-start.13 = (bf16[16,4096]{1,0:T(8,128)(2,1)S(1)}, bf16[16,4096]{1,0:T(8,128)(2,1)S(1)}, u32[]{:S(2)}, u32[]{:S(2)}) collective-permute-start(bf16[16,4096]{1,0:T(8,128)(2,1)S(1)} %bitcast.45), channel_id=1, source_target_pairs={{0,2},{1,5},{2,0},{3,7},{4,6},{5,1},{6,4},{7,3},{8,10},{9,13},{10,... | collective-permute-start | bytes 393224 | tf_op jit(solution)/shard_map/ppermute | solution.py:122
  53.7 0.7 collective-permute-start.17
  54.4 1.3 %collective-permute-start.14 = (bf16[16,4096]{1,0:T(8,128)(2,1)S(1)}, bf16[16,4096]{1,0:T(8,128)(2,1)S(1)}, u32[]{:S(2)}, u32[]{:S(2)}) collective-permute-start(bf16[16,4096]{1,0:T(8,128)(2,1)S(1)} %collective-permute-done.12.refs_1_), channel_id=1, source_target_pairs={{0,2},{1,5},{2,0},{3,7},{4,6},{5,1},{6,4},{7,3},{8,10},{9,13},{10,... | collective-permute-start | bytes 393224 | tf_op jit(solution)/shard_map/ppermute | solution.py:122
  55.7 3.0 %collective-permute-done.16.refs_5_ = bf16[16,4096]{1,0:T(8,128)(2,1)S(1)} collective-permute-done((bf16[16,4096]{1,0:T(8,128)(2,1)S(1)}, bf16[16,4096]{1,0:T(8,128)(2,1)S(1)}, u32[]{:S(2)}, u32[]{:S(2)}) %collective-permute-start.16) | collective-permute-done | bytes 131104 | tf_op jit(solution)/shard_map/ppermute | solution.py:122
  58.7 2.2 %collective-permute-done.14.refs_3_ = bf16[16,4096]{1,0:T(8,128)(2,1)S(1)} collective-permute-done((bf16[16,4096]{1,0:T(8,128)(2,1)S(1)}, bf16[16,4096]{1,0:T(8,128)(2,1)S(1)}, u32[]{:S(2)}, u32[]{:S(2)}) %collective-permute-start.14) | collective-permute-done | bytes 131104 | tf_op jit(solution)/shard_map/ppermute | solution.py:122
  60.9 0.0 collective-permute-done.17.refs_6_
  60.9 2.8 %collective-permute-done.18.refs_7_ = bf16[16,4096]{1,0:T(8,128)(2,1)S(1)} collective-permute-done((bf16[16,4096]{1,0:T(8,128)(2,1)S(1)}, bf16[16,4096]{1,0:T(8,128)(2,1)S(1)}, u32[]{:S(2)}, u32[]{:S(2)}) %collective-permute-start.18) | collective-permute-done | bytes 131104 | tf_op jit(solution)/shard_map/ppermute | solution.py:122
  63.7 1.3 %shard_map.105 = (f32[64,1024]{1,0:T(8,128)S(1)}, f32[64,1024]{1,0:T(8,128)S(1)}) custom-call(bf16[16,4096]{1,0:T(8,128)(2,1)S(1)} %bitcast.46, bf16[16,4096]{1,0:T(8,128)(2,1)S(1)} %collective-permute-done.12.refs_1_, bf16[16,4096]{1,0:T(8,128)(2,1)S(1)} %collective-permute-done.13.refs_2_, bf16[16,4096]{1,0:T(8,128)(2,1)S(1)} %collective-permute-done.14.refs_3_, ...), custom_call_target="tpu_custom_call" | custom-call | bytes 1048576 | tf_op jit(solution)/shard_map/pallas_call | solution.py:178
  65.0 0.1 collective-permute-start.19
  65.1 1.5 %collective-permute-done.19.arrived_ref = f32[64,1024]{1,0:T(8,128)S(1)} collective-permute-done((f32[64,1024]{1,0:T(8,128)S(1)}, f32[64,1024]{1,0:T(8,128)S(1)}, u32[]{:S(2)}, u32[]{:S(2)}) %collective-permute-start.19) | collective-permute-done | bytes 262176 | tf_op jit(solution)/shard_map/ppermute | solution.py:137
  66.6 0.7 collective-permute-start.20
  67.3 0.1 collective-permute-start.21
  67.4 1.3 %collective-permute-start.22 = (bf16[16,1024]{1,0:T(8,128)(2,1)S(1)}, bf16[16,1024]{1,0:T(8,128)(2,1)S(1)}, u32[]{:S(2)}, u32[]{:S(2)}) collective-permute-start(bf16[16,1024]{1,0:T(8,128)(2,1)S(1)} %get-tuple-element.39), channel_id=1, source_target_pairs={{0,2},{1,12},{2,0},{3,14},{4,6},{5,8},{6,4},{7,10},{8,11},{9,5},{1... | collective-permute-start | bytes 98312 | tf_op jit(solution)/shard_map/ppermute | solution.py:152
  68.8 2.1 %collective-permute-start.23 = (bf16[16,1024]{1,0:T(8,128)(2,1)S(1)}, bf16[16,1024]{1,0:T(8,128)(2,1)S(1)}, u32[]{:S(2)}, u32[]{:S(2)}) collective-permute-start(bf16[16,1024]{1,0:T(8,128)(2,1)S(1)} %get-tuple-element.40), channel_id=1, source_target_pairs={{0,6},{1,14},{2,4},{3,12},{4,2},{5,10},{6,0},{7,8},{8,15},{9,7},{1... | collective-permute-start | bytes 98312 | tf_op jit(solution)/shard_map/ppermute | solution.py:152
  70.9 0.0 collective-permute-done.20
  70.9 0.4 collective-permute-done.21
  71.3 0.1 collective-permute-done.22
  71.4 2.2 %collective-permute-done.23 = bf16[16,1024]{1,0:T(8,128)(2,1)S(1)} collective-permute-done((bf16[16,1024]{1,0:T(8,128)(2,1)S(1)}, bf16[16,1024]{1,0:T(8,128)(2,1)S(1)}, u32[]{:S(2)}, u32[]{:S(2)}) %collective-permute-start.23) | collective-permute-done | bytes 32800 | tf_op jit(solution)/shard_map/ppermute | solution.py:152
  73.6 4.8 %collective-permute-start.24 = (bf16[4,16,1024]{2,1,0:T(8,128)(2,1)S(1)}, bf16[4,16,1024]{2,1,0:T(8,128)(2,1)S(1)}, u32[]{:S(2)}, u32[]{:S(2)}) collective-permute-start(bf16[4,16,1024]{2,1,0:T(8,128)(2,1)S(1)} %pad_maximum_fusion.1.own_ref), channel_id=1, source_target_pairs={{0,1},{1,0},{2,3},{3,2},{4,5},{5,4},{6,7},{7,6},{8,9},{9,8},{10,11... | collective-permute-start | bytes 393224 | tf_op jit(solution)/shard_map/ppermute | solution.py:137
  78.4 0.1 pad_add_fusion
  78.5 0.9 %collective-permute-done.24.other_ref = bf16[4,16,1024]{2,1,0:T(8,128)(2,1)S(1)} collective-permute-done((bf16[4,16,1024]{2,1,0:T(8,128)(2,1)S(1)}, bf16[4,16,1024]{2,1,0:T(8,128)(2,1)S(1)}, u32[]{:S(2)}, u32[]{:S(2)}) %collective-permute-start.24) | collective-permute-done | bytes 131104 | tf_op jit(solution)/shard_map/ppermute | solution.py:137
  79.4 1.3 %shard_map.107 = bf16[16,8192]{1,0:T(8,128)(2,1)} custom-call(s32[4]{0:T(128)S(1)} %get-tuple-element.54.own_places, s32[4]{0:T(128)S(1)} %get-tuple-element.55.other_places, bf16[4,16,1024]{2,1,0:T(8,128)(2,1)S(1)} %pad_maximum_fusion.1.own_ref, bf16[4,16,1024]{2,1,0:T(8,128)(2,1)S(1)} %collective-permute-done.24.other_ref), custom_call_target="tpu_custom_call" | custom-call | bytes 1048576 | tf_op jit(solution)/shard_map/pallas_call | solution.py:178
  (21 shorter events, 0.2 us)
Async XLA Ops:
  1.2 10.7 %collective-permute-start.3 = (bf16[16,4224]{1,0:T(8,128)(2,1)S(1)}, bf16[16,4224]{1,0:T(8,128)(2,1)S(1)}, u32[]{:S(2)}, u32[]{:S(2)}) collective-permute-start(bf16[16,4224]{1,0:T(8,128)(2,1)S(1)} %shard_map.101.refs_0_), channel_id=1, source_target_pairs={{0,8},{1,9},{2,10},{3,11},{4,12},{5,13},{6,14},{7,15},{8,0},{9,1},... | collective-permute-start | bytes 405512 | tf_op jit(solution)/shard_map/ppermute | solution.py:122
  5.3 9.2 %collective-permute-start = (bf16[16,4224]{1,0:T(8,128)(2,1)S(1)}, bf16[16,4224]{1,0:T(8,128)(2,1)S(1)}, u32[]{:S(2)}, u32[]{:S(2)}) collective-permute-start(bf16[16,4224]{1,0:T(8,128)(2,1)S(1)} %shard_map.101.refs_0_), channel_id=1, source_target_pairs={{0,4},{1,3},{2,6},{3,1},{4,0},{5,7},{6,2},{7,5},{8,12},{9,11},{10,... | collective-permute-start | bytes 405512 | tf_op jit(solution)/shard_map/ppermute | solution.py:122
  11.9 6.4 %collective-permute-start.4 = (bf16[16,4224]{1,0:T(8,128)(2,1)S(1)}, bf16[16,4224]{1,0:T(8,128)(2,1)S(1)}, u32[]{:S(2)}, u32[]{:S(2)}) collective-permute-start(bf16[16,4224]{1,0:T(8,128)(2,1)S(1)} %collective-permute-done.3.refs_4_), channel_id=1, source_target_pairs={{0,4},{1,3},{2,6},{3,1},{4,0},{5,7},{6,2},{7,5},{8,12},{9,11},{10,... | collective-permute-start | bytes 405512 | tf_op jit(solution)/shard_map/ppermute | solution.py:122
  12.5 12.3 %collective-permute-start.1 = (bf16[16,4224]{1,0:T(8,128)(2,1)S(1)}, bf16[16,4224]{1,0:T(8,128)(2,1)S(1)}, u32[]{:S(2)}, u32[]{:S(2)}) collective-permute-start(bf16[16,4224]{1,0:T(8,128)(2,1)S(1)} %shard_map.101.refs_0_), channel_id=1, source_target_pairs={{0,2},{1,5},{2,0},{3,7},{4,6},{5,1},{6,4},{7,3},{8,10},{9,13},{10,... | collective-permute-start | bytes 405512 | tf_op jit(solution)/shard_map/ppermute | solution.py:122
  14.1 10.8 %collective-permute-start.5 = (bf16[16,4224]{1,0:T(8,128)(2,1)S(1)}, bf16[16,4224]{1,0:T(8,128)(2,1)S(1)}, u32[]{:S(2)}, u32[]{:S(2)}) collective-permute-start(bf16[16,4224]{1,0:T(8,128)(2,1)S(1)} %collective-permute-done.3.refs_4_), channel_id=1, source_target_pairs={{0,2},{1,5},{2,0},{3,7},{4,6},{5,1},{6,4},{7,3},{8,10},{9,13},{10,... | collective-permute-start | bytes 405512 | tf_op jit(solution)/shard_map/ppermute | solution.py:122
  14.6 10.3 %collective-permute-start.2 = (bf16[16,4224]{1,0:T(8,128)(2,1)S(1)}, bf16[16,4224]{1,0:T(8,128)(2,1)S(1)}, u32[]{:S(2)}, u32[]{:S(2)}) collective-permute-start(bf16[16,4224]{1,0:T(8,128)(2,1)S(1)} %collective-permute-done.refs_1_), channel_id=1, source_target_pairs={{0,2},{1,5},{2,0},{3,7},{4,6},{5,1},{6,4},{7,3},{8,10},{9,13},{10,... | collective-permute-start | bytes 405512 | tf_op jit(solution)/shard_map/ppermute | solution.py:122
  18.4 6.5 %collective-permute-start.6 = (bf16[16,4224]{1,0:T(8,128)(2,1)S(1)}, bf16[16,4224]{1,0:T(8,128)(2,1)S(1)}, u32[]{:S(2)}, u32[]{:S(2)}) collective-permute-start(bf16[16,4224]{1,0:T(8,128)(2,1)S(1)} %collective-permute-done.4.refs_5_), channel_id=1, source_target_pairs={{0,2},{1,5},{2,0},{3,7},{4,6},{5,1},{6,4},{7,3},{8,10},{9,13},{10,... | collective-permute-start | bytes 405512 | tf_op jit(solution)/shard_map/ppermute | solution.py:122
  26.9 1.7 %collective-permute-start.7 = (f32[64,1280]{1,0:T(8,128)S(1)}, f32[64,1280]{1,0:T(8,128)S(1)}, u32[]{:S(2)}, u32[]{:S(2)}) collective-permute-start(f32[64,1280]{1,0:T(8,128)S(1)} %get-tuple-element.28), channel_id=1, source_target_pairs={{0,1},{1,0},{2,3},{3,2},{4,5},{5,4},{6,7},{7,6},{8,9},{9,8},{10,11... | collective-permute-start | bytes 983048 | tf_op jit(solution)/shard_map/ppermute | solution.py:137
  28.8 7.7 %collective-permute-start.8 = (bf16[16,1280]{1,0:T(8,128)(2,1)S(1)}, bf16[16,1280]{1,0:T(8,128)(2,1)S(1)}, u32[]{:S(2)}, u32[]{:S(2)}) collective-permute-start(bf16[16,1280]{1,0:T(8,128)(2,1)S(1)} %get-tuple-element.30), channel_id=1, source_target_pairs={{0,0},{1,8},{2,2},{3,10},{4,4},{5,12},{6,6},{7,14},{8,9},{9,1},{10... | collective-permute-start | bytes 122888 | tf_op jit(solution)/shard_map/ppermute | solution.py:152
  29.5 7.0 %collective-permute-start.9 = (bf16[16,1280]{1,0:T(8,128)(2,1)S(1)}, bf16[16,1280]{1,0:T(8,128)(2,1)S(1)}, u32[]{:S(2)}, u32[]{:S(2)}) collective-permute-start(bf16[16,1280]{1,0:T(8,128)(2,1)S(1)} %get-tuple-element.31), channel_id=1, source_target_pairs={{0,4},{1,10},{2,6},{3,8},{4,0},{5,14},{6,2},{7,12},{8,13},{9,3},{1... | collective-permute-start | bytes 122888 | tf_op jit(solution)/shard_map/ppermute | solution.py:152
  30.0 6.5 %collective-permute-start.10 = (bf16[16,1280]{1,0:T(8,128)(2,1)S(1)}, bf16[16,1280]{1,0:T(8,128)(2,1)S(1)}, u32[]{:S(2)}, u32[]{:S(2)}) collective-permute-start(bf16[16,1280]{1,0:T(8,128)(2,1)S(1)} %get-tuple-element.32), channel_id=1, source_target_pairs={{0,2},{1,12},{2,0},{3,14},{4,6},{5,8},{6,4},{7,10},{8,11},{9,5},{1... | collective-permute-start | bytes 122888 | tf_op jit(solution)/shard_map/ppermute | solution.py:152
  30.2 6.3 %collective-permute-start.11 = (bf16[16,1280]{1,0:T(8,128)(2,1)S(1)}, bf16[16,1280]{1,0:T(8,128)(2,1)S(1)}, u32[]{:S(2)}, u32[]{:S(2)}) collective-permute-start(bf16[16,1280]{1,0:T(8,128)(2,1)S(1)} %get-tuple-element.33), channel_id=1, source_target_pairs={{0,6},{1,14},{2,4},{3,12},{4,2},{5,10},{6,0},{7,8},{8,15},{9,7},{1... | collective-permute-start | bytes 122888 | tf_op jit(solution)/shard_map/ppermute | solution.py:152
  37.4 26.3 %slice-start = ((s8[8388608]{0:T(1024)(128)(4,1)}), s8[4194304]{0:T(1024)(128)(4,1)S(1)}, s32[]{:S(2)}) async-start(s8[8388608]{0:T(1024)(128)(4,1)} %bitcast.40), calls=%async_computation | async-start | bytes 8388608
  39.3 24.3 %slice-start.1 = ((s8[8388608]{0:T(1024)(128)(4,1)}), s8[4194304]{0:T(1024)(128)(4,1)S(1)}, s32[]{:S(2)}) async-start(s8[8388608]{0:T(1024)(128)(4,1)} %bitcast.40), calls=%async_computation.1 | async-start | bytes 8388608
  40.6 11.8 %collective-permute-start.15 = (bf16[16,4096]{1,0:T(8,128)(2,1)S(1)}, bf16[16,4096]{1,0:T(8,128)(2,1)S(1)}, u32[]{:S(2)}, u32[]{:S(2)}) collective-permute-start(bf16[16,4096]{1,0:T(8,128)(2,1)S(1)} %bitcast.43), channel_id=1, source_target_pairs={{0,8},{1,9},{2,10},{3,11},{4,12},{5,13},{6,14},{7,15},{8,0},{9,1},... | collective-permute-start | bytes 393224 | tf_op jit(solution)/shard_map/ppermute | solution.py:122
  45.6 8.9 %collective-permute-start.12 = (bf16[16,4096]{1,0:T(8,128)(2,1)S(1)}, bf16[16,4096]{1,0:T(8,128)(2,1)S(1)}, u32[]{:S(2)}, u32[]{:S(2)}) collective-permute-start(bf16[16,4096]{1,0:T(8,128)(2,1)S(1)} %bitcast.44), channel_id=1, source_target_pairs={{0,4},{1,3},{2,6},{3,1},{4,0},{5,7},{6,2},{7,5},{8,12},{9,11},{10,... | collective-permute-start | bytes 393224 | tf_op jit(solution)/shard_map/ppermute | solution.py:122
  52.4 6.3 %collective-permute-start.16 = (bf16[16,4096]{1,0:T(8,128)(2,1)S(1)}, bf16[16,4096]{1,0:T(8,128)(2,1)S(1)}, u32[]{:S(2)}, u32[]{:S(2)}) collective-permute-start(bf16[16,4096]{1,0:T(8,128)(2,1)S(1)} %collective-permute-done.15.refs_4_), channel_id=1, source_target_pairs={{0,4},{1,3},{2,6},{3,1},{4,0},{5,7},{6,2},{7,5},{8,12},{9,11},{10,... | collective-permute-start | bytes 393224 | tf_op jit(solution)/shard_map/ppermute | solution.py:122
  52.4 6.3 %collective-permute-start.13 = (bf16[16,4096]{1,0:T(8,128)(2,1)S(1)}, bf16[16,4096]{1,0:T(8,128)(2,1)S(1)}, u32[]{:S(2)}, u32[]{:S(2)}) collective-permute-start(bf16[16,4096]{1,0:T(8,128)(2,1)S(1)} %bitcast.45), channel_id=1, source_target_pairs={{0,2},{1,5},{2,0},{3,7},{4,6},{5,1},{6,4},{7,3},{8,10},{9,13},{10,... | collective-permute-start | bytes 393224 | tf_op jit(solution)/shard_map/ppermute | solution.py:122
  53.7 7.1 %collective-permute-start.17 = (bf16[16,4096]{1,0:T(8,128)(2,1)S(1)}, bf16[16,4096]{1,0:T(8,128)(2,1)S(1)}, u32[]{:S(2)}, u32[]{:S(2)}) collective-permute-start(bf16[16,4096]{1,0:T(8,128)(2,1)S(1)} %collective-permute-done.15.refs_4_), channel_id=1, source_target_pairs={{0,2},{1,5},{2,0},{3,7},{4,6},{5,1},{6,4},{7,3},{8,10},{9,13},{10,... | collective-permute-start | bytes 393224 | tf_op jit(solution)/shard_map/ppermute | solution.py:122
  54.4 6.4 %collective-permute-start.14 = (bf16[16,4096]{1,0:T(8,128)(2,1)S(1)}, bf16[16,4096]{1,0:T(8,128)(2,1)S(1)}, u32[]{:S(2)}, u32[]{:S(2)}) collective-permute-start(bf16[16,4096]{1,0:T(8,128)(2,1)S(1)} %collective-permute-done.12.refs_1_), channel_id=1, source_target_pairs={{0,2},{1,5},{2,0},{3,7},{4,6},{5,1},{6,4},{7,3},{8,10},{9,13},{10,... | collective-permute-start | bytes 393224 | tf_op jit(solution)/shard_map/ppermute | solution.py:122
  58.7 5.0 %collective-permute-start.18 = (bf16[16,4096]{1,0:T(8,128)(2,1)S(1)}, bf16[16,4096]{1,0:T(8,128)(2,1)S(1)}, u32[]{:S(2)}, u32[]{:S(2)}) collective-permute-start(bf16[16,4096]{1,0:T(8,128)(2,1)S(1)} %collective-permute-done.16.refs_5_), channel_id=1, source_target_pairs={{0,2},{1,5},{2,0},{3,7},{4,6},{5,1},{6,4},{7,3},{8,10},{9,13},{10,... | collective-permute-start | bytes 393224 | tf_op jit(solution)/shard_map/ppermute | solution.py:122
  65.0 1.6 %collective-permute-start.19 = (f32[64,1024]{1,0:T(8,128)S(1)}, f32[64,1024]{1,0:T(8,128)S(1)}, u32[]{:S(2)}, u32[]{:S(2)}) collective-permute-start(f32[64,1024]{1,0:T(8,128)S(1)} %get-tuple-element.36), channel_id=1, source_target_pairs={{0,1},{1,0},{2,3},{3,2},{4,5},{5,4},{6,7},{7,6},{8,9},{9,8},{10,11... | collective-permute-start | bytes 786440 | tf_op jit(solution)/shard_map/ppermute | solution.py:137
  66.6 4.2 %collective-permute-start.20 = (bf16[16,1024]{1,0:T(8,128)(2,1)S(1)}, bf16[16,1024]{1,0:T(8,128)(2,1)S(1)}, u32[]{:S(2)}, u32[]{:S(2)}) collective-permute-start(bf16[16,1024]{1,0:T(8,128)(2,1)S(1)} %get-tuple-element.37), channel_id=1, source_target_pairs={{0,0},{1,8},{2,2},{3,10},{4,4},{5,12},{6,6},{7,14},{8,9},{9,1},{10... | collective-permute-start | bytes 98312 | tf_op jit(solution)/shard_map/ppermute | solution.py:152
  67.3 4.0 %collective-permute-start.21 = (bf16[16,1024]{1,0:T(8,128)(2,1)S(1)}, bf16[16,1024]{1,0:T(8,128)(2,1)S(1)}, u32[]{:S(2)}, u32[]{:S(2)}) collective-permute-start(bf16[16,1024]{1,0:T(8,128)(2,1)S(1)} %get-tuple-element.38), channel_id=1, source_target_pairs={{0,4},{1,10},{2,6},{3,8},{4,0},{5,14},{6,2},{7,12},{8,13},{9,3},{1... | collective-permute-start | bytes 98312 | tf_op jit(solution)/shard_map/ppermute | solution.py:152
  67.4 3.9 %collective-permute-start.22 = (bf16[16,1024]{1,0:T(8,128)(2,1)S(1)}, bf16[16,1024]{1,0:T(8,128)(2,1)S(1)}, u32[]{:S(2)}, u32[]{:S(2)}) collective-permute-start(bf16[16,1024]{1,0:T(8,128)(2,1)S(1)} %get-tuple-element.39), channel_id=1, source_target_pairs={{0,2},{1,12},{2,0},{3,14},{4,6},{5,8},{6,4},{7,10},{8,11},{9,5},{1... | collective-permute-start | bytes 98312 | tf_op jit(solution)/shard_map/ppermute | solution.py:152
  68.8 4.8 %collective-permute-start.23 = (bf16[16,1024]{1,0:T(8,128)(2,1)S(1)}, bf16[16,1024]{1,0:T(8,128)(2,1)S(1)}, u32[]{:S(2)}, u32[]{:S(2)}) collective-permute-start(bf16[16,1024]{1,0:T(8,128)(2,1)S(1)} %get-tuple-element.40), channel_id=1, source_target_pairs={{0,6},{1,14},{2,4},{3,12},{4,2},{5,10},{6,0},{7,8},{8,15},{9,7},{1... | collective-permute-start | bytes 98312 | tf_op jit(solution)/shard_map/ppermute | solution.py:152
  73.6 5.8 %collective-permute-start.24 = (bf16[4,16,1024]{2,1,0:T(8,128)(2,1)S(1)}, bf16[4,16,1024]{2,1,0:T(8,128)(2,1)S(1)}, u32[]{:S(2)}, u32[]{:S(2)}) collective-permute-start(bf16[4,16,1024]{2,1,0:T(8,128)(2,1)S(1)} %pad_maximum_fusion.1.own_ref), channel_id=1, source_target_pairs={{0,1},{1,0},{2,3},{3,2},{4,5},{5,4},{6,7},{7,6},{8,9},{9,8},{10,11... | collective-permute-start | bytes 393224 | tf_op jit(solution)/shard_map/ppermute | solution.py:137

commit v3 on v2

--- a/solution.py
+++ b/solution.py
@@ -122,10 +122,12 @@
     return lax.ppermute(block, ("out", "inp"), pairs)
 
 
-def gather_blocks(block):
+def gather_blocks(block, *marks):
     far = swap_blocks(block, "far")
     near = swap_blocks(block, "near")
     last = swap_blocks(block, "last")
+    if marks:
+        far = after(far, *marks)
     near_last = swap_blocks(near, "last")
     far_near = swap_blocks(far, "near")
     far_last = swap_blocks(far, "last")
@@ -174,7 +176,7 @@
 MEGABYTE = 1 << 20
 
 
-def on_chip(kernel, out_shape, scalars, *operands, scratch=(), megabytes=16, moved=1, place=VMEM_SPEC):
+def on_chip(kernel, out_shape, scalars, *operands, scratch=(), megabytes=8, moved=1, place=VMEM_SPEC):
     return pl.pallas_call(
         kernel,
         out_shape=out_shape,
@@ -212,8 +214,8 @@
 
 
 def fetch_kernel(*refs):
-    count = (len(refs) - 1) // 2
-    arrivals = refs[-1]
+    count = (len(refs) - 2) // 2
+    mark_ref, arrivals = refs[-2:]
     copies = []
     for n in range(count):
         source, target = refs[n], refs[count + n]
@@ -223,6 +225,7 @@
             copies.append(pltpu.make_async_copy(source.at[here], target.at[here], arrivals.at[n, part]))
     for copy in copies:
         copy.start()
+    mark_ref[...] = jnp.zeros_like(mark_ref)
     for copy in copies:
         copy.wait()
 
@@ -231,12 +234,16 @@
     return pltpu.with_memory_space_constraint(array, pltpu.HBM)
 
 
+ANYWHERE = pl.BlockSpec(memory_space=pl.ANY)
+
+
 def fetched(*arrays):
-    return pl.pallas_call(
+    *near, mark = pl.pallas_call(
         fetch_kernel,
-        out_shape=[pltpu.VMEM(array.shape, array.dtype) for array in arrays],
-        in_specs=[pl.BlockSpec(memory_space=pl.ANY)] * len(arrays),
-        out_specs=[VMEM_SPEC] * len(arrays),
+        out_shape=[pltpu.VMEM(array.shape, array.dtype) for array in arrays]
+        + [jax.ShapeDtypeStruct((8, 128), jnp.float32)],
+        in_specs=[ANYWHERE] * len(arrays),
+        out_specs=[VMEM_SPEC] * (len(arrays) + 1),
         scratch_shapes=[pltpu.SemaphoreType.DMA((len(arrays), 4))],
         compiler_params=pltpu.CompilerParams(vmem_limit_bytes=MEGABYTE),
         cost_estimate=pl.CostEstimate(
@@ -245,6 +252,22 @@
             transcendentals=0,
         ),
     )(*map(distant, arrays))
+    return near, mark
+
+
+def after_kernel(*refs):
+    pass
+
+
+def after(block, *others):
+    return pl.pallas_call(
+        after_kernel,
+        out_shape=jax.ShapeDtypeStruct(block.shape, block.dtype),
+        in_specs=[ANYWHERE] * (1 + len(others)),
+        out_specs=ANYWHERE,
+        input_output_aliases={0: 0},
+        compiler_params=pltpu.CompilerParams(vmem_limit_bytes=MEGABYTE),
+    )(block, *others)
 
 
 def stack_rows(core, pieces, rows_ref):
@@ -312,16 +335,13 @@
         out_ref[...] = total.astype(jnp.bfloat16)
 
 
-def place_kernel(own_places, other_places, own_ref, other_ref, out_ref):
+def place_kernel(own_ref, other_ref, out_ref):
     core = lax.axis_index("inp")
     width = own_ref.shape[2]
     for column in range(4):
-        own = own_ref[own_places[column]]
-        other = other_ref[other_places[column]]
-        left = jnp.where(core == 0, own.astype(jnp.float32), other.astype(jnp.float32))
-        right = jnp.where(core == 0, other.astype(jnp.float32), own.astype(jnp.float32))
-        out_ref[:, column * width : (column + 1) * width] = left.astype(jnp.bfloat16)
-        out_ref[:, (column + 4) * width : (column + 5) * width] = right.astype(jnp.bfloat16)
+        for ref, its_core in ((own_ref, core), (other_ref, 1 - core)):
+            start = pl.multiple_of((its_core * 4 + column) * width, width)
+            out_ref[:, pl.ds(start, width)] = ref[place_of(column, crossing(its_core))]
 
 
 def attend_both(queries, new_keys, new_values, cache_keys, cache_values, lengths):
@@ -373,9 +393,9 @@
         ],
         place=pl.BlockSpec(memory_space=pltpu.HBM),
     )
-    near_query, near_key, near_value = fetched(query_weight, key_matrix, value_matrix)
-    cache_keys, cache_values = fetched(cache_keys, cache_values)
-    lower, upper = gather_blocks(own)
+    (near_query, near_key, near_value), weight_mark = fetched(query_weight, key_matrix, value_matrix)
+    (cache_keys, cache_values), cache_mark = fetched(cache_keys, cache_values)
+    lower, upper = gather_blocks(own, weight_mark)
     given, kept, tags = on_chip(
         project_kernel,
         [shape((4 * count, qkv_cols), jnp.float32)] * 2 + [shape((4 * count, 128), jnp.float32)],
@@ -423,12 +443,10 @@
         round_kernel, [shape((count, mix_cols), jnp.bfloat16)] * 4, (), kept, swap_cores(given)
     )
     own_half = jnp.stack(hand_out(outgoing))
-    own_places = jnp.stack([place_of(c, crossing(core)) for c in range(4)]).astype(jnp.int32)
-    other_places = jnp.stack([place_of(c, crossing(1 - core)) for c in range(4)]).astype(jnp.int32)
     mixed = on_chip(
         place_kernel,
         shape((count, width), jnp.bfloat16),
-        (own_places, other_places),
+        (),
         own_half,
         swap_cores(own_half),
     )

time: 80.9 us -> 79.5 us (0.983)
  waiting for transfers between devices: 25.4 us -> 19.2 us
  starting transfers between devices: 36.3 us -> 41.9 us
    ppermute x14, waiting for transfers between devices: 18.9 us -> 11.7 us  [swap_blocks(): return lax.ppermute(block, ('out', 'inp'), pairs)]
    ppermute x14, starting transfers between devices: 22.9 us -> 28.7 us  [swap_blocks(): return lax.ppermute(block, ('out', 'inp'), pairs)]
    ppermute x8, waiting for transfers between devices: 2.72 us -> 3.65 us  [hand_out(): received.append(lax.ppermute(block, ('out', 'inp'), pairs))]
  transfers between devices with their start and end apart: 25 -> 25, of which waited for: 12 -> 14; matrix products, arithmetic and copies ran while one was open for 1% -> 0% of each run, Pallas kernels for 9% -> 10%
where the time goes in v3:
time: 79.5 us; the launch traced here: 79.3 us
  starting transfers between devices  41.9 us (53%)
  waiting for transfers between devices  19.2 us (24%)
  Pallas kernels  13.4 us (17%)
  matrix products  3.24 us (4%)
  other arithmetic  1.19 us (1%)
    ppermute x14, starting transfers between devices, swap_blocks(): return lax.ppermute(block, ('out', 'inp'), pairs)  28.7 us
    ppermute x14, waiting for transfers between devices, swap_blocks(): return lax.ppermute(block, ('out', 'inp'), pairs)  11.7 us
    ppermute x8, starting transfers between devices, hand_out(): received.append(lax.ppermute(block, ('out', 'inp'), pairs))  8.4 us
    pallas_call x2, Pallas kernels, fetched(): pl.pallas_call(fetch_kernel, out_shape=[pltpu.VMEM(array.shape, array.dty...  8.1 us
    pallas_call x6, Pallas kernels, on_chip(): pl.pallas_call(kernel, out_shape=out_shape, in_specs=[SMEM_SPEC] * len(sc...  5.32 us
    ppermute x3, starting transfers between devices, swap_cores(): return lax.ppermute(block, 'inp', [(0, 1), (1, 0)])  4.75 us
    ppermute x3, waiting for transfers between devices, swap_cores(): return lax.ppermute(block, 'inp', [(0, 1), (1, 0)])  3.83 us
    ppermute x8, waiting for transfers between devices, hand_out(): received.append(lax.ppermute(block, ('out', 'inp'), pairs))  3.65 us
  transfers between devices with their start and end apart: 25, of which 14 were waited for; matrix products, arithmetic and copies ran while one was open for 0% of the time, Pallas kernels for 10%

profile of v3, /device:TPU:0, one launch (start us, length us, event | category | flops | bytes accessed | tf_op | source)
XLA Modules:
  0.0 79.3 jit_solution(12291927187868103810)
XLA Ops:
  0.0 1.2 %shard_map.101.refs_0_ = bf16[16,4224]{1,0:T(8,128)(2,1)S(1)} custom-call(s32[8]{0:T(128)} %position_hbm.1, bf16[16,8192]{1,0:T(8,128)(2,1)} %bitcast.40, f32[1,8192]{1,0:T(1,128)} %bitcast.45), custom_call_target="tpu_custom_call" | custom-call | bytes 1048576 | tf_op jit(solution)/shard_map/pallas_call | solution.py:180
  1.2 0.0 copy-start
  1.3 4.1 %collective-permute-start.3 = (bf16[16,4224]{1,0:T(8,128)(2,1)S(1)}, bf16[16,4224]{1,0:T(8,128)(2,1)S(1)}, u32[]{:S(2)}, u32[]{:S(2)}) collective-permute-start(bf16[16,4224]{1,0:T(8,128)(2,1)S(1)} %shard_map.101.refs_0_), channel_id=1, source_target_pairs={{0,8},{1,9},{2,10},{3,11},{4,12},{5,13},{6,14},{7,15},{8,0},{9,1},... | collective-permute-start | bytes 405512 | tf_op jit(solution)/shard_map/ppermute | solution.py:122
  5.4 1.6 %collective-permute-start = (bf16[16,4224]{1,0:T(8,128)(2,1)S(1)}, bf16[16,4224]{1,0:T(8,128)(2,1)S(1)}, u32[]{:S(2)}, u32[]{:S(2)}) collective-permute-start(bf16[16,4224]{1,0:T(8,128)(2,1)S(1)} %shard_map.101.refs_0_), channel_id=1, source_target_pairs={{0,4},{1,3},{2,6},{3,1},{4,0},{5,7},{6,2},{7,5},{8,12},{9,11},{10,... | collective-permute-start | bytes 405512 | tf_op jit(solution)/shard_map/ppermute | solution.py:122
  6.9 4.0 %shard_map.102 = (bf16[4096,1024]{1,0:T(8,128)(2,1)S(1)}, bf16[4096,128]{1,0:T(8,128)(2,1)S(1)}, bf16[4096,128]{1,0:T(8,128)(2,1)S(1)}, f32[8,128]{1,0:T(8,128)S(1)}) custom-call(bf16[4096,1024]{1,0:T(8,128)(2,1)} %refs_0_.3, bf16[4096,128]{1,0:T(8,128)(2,1)} %refs_1_.3, bf16[4096,128]{1,0:T(8,128)(2,1)} %refs_2_.1), custom_call_target="tpu_custom_call" | custom-call | bytes 10485760 | tf_op jit(solution)/shard_map/pallas_call | solution.py:241
  11.0 1.0 %collective-permute-done.3.refs_0_ = bf16[16,4224]{1,0:T(8,128)(2,1)S(1)} collective-permute-done((bf16[16,4224]{1,0:T(8,128)(2,1)S(1)}, bf16[16,4224]{1,0:T(8,128)(2,1)S(1)}, u32[]{:S(2)}, u32[]{:S(2)}) %collective-permute-start.3) | collective-permute-done | bytes 135200 | tf_op jit(solution)/shard_map/ppermute | solution.py:122
  11.9 0.6 collective-permute-start.4
  12.6 1.5 %collective-permute-start.1 = (bf16[16,4224]{1,0:T(8,128)(2,1)S(1)}, bf16[16,4224]{1,0:T(8,128)(2,1)S(1)}, u32[]{:S(2)}, u32[]{:S(2)}) collective-permute-start(bf16[16,4224]{1,0:T(8,128)(2,1)S(1)} %shard_map.101.refs_0_), channel_id=1, source_target_pairs={{0,2},{1,5},{2,0},{3,7},{4,6},{5,1},{6,4},{7,3},{8,10},{9,13},{10,... | collective-permute-start | bytes 405512 | tf_op jit(solution)/shard_map/ppermute | solution.py:122
  14.1 0.5 collective-permute-start.5
  14.6 1.5 %collective-permute-start.2 = (bf16[16,4224]{1,0:T(8,128)(2,1)S(1)}, bf16[16,4224]{1,0:T(8,128)(2,1)S(1)}, u32[]{:S(2)}, u32[]{:S(2)}) collective-permute-start(bf16[16,4224]{1,0:T(8,128)(2,1)S(1)} %collective-permute-done.refs_1_), channel_id=1, source_target_pairs={{0,2},{1,5},{2,0},{3,7},{4,6},{5,1},{6,4},{7,3},{8,10},{9,13},{10,... | collective-permute-start | bytes 405512 | tf_op jit(solution)/shard_map/ppermute | solution.py:122
  16.1 2.3 %collective-permute-done.4.refs_5_ = bf16[16,4224]{1,0:T(8,128)(2,1)S(1)} collective-permute-done((bf16[16,4224]{1,0:T(8,128)(2,1)S(1)}, bf16[16,4224]{1,0:T(8,128)(2,1)S(1)}, u32[]{:S(2)}, u32[]{:S(2)}) %collective-permute-start.4) | collective-permute-done | bytes 135200 | tf_op jit(solution)/shard_map/ppermute | solution.py:122
  18.4 1.7 %collective-permute-start.6 = (bf16[16,4224]{1,0:T(8,128)(2,1)S(1)}, bf16[16,4224]{1,0:T(8,128)(2,1)S(1)}, u32[]{:S(2)}, u32[]{:S(2)}) collective-permute-start(bf16[16,4224]{1,0:T(8,128)(2,1)S(1)} %collective-permute-done.4.refs_5_), channel_id=1, source_target_pairs={{0,2},{1,5},{2,0},{3,7},{4,6},{5,1},{6,4},{7,3},{8,10},{9,13},{10,... | collective-permute-start | bytes 405512 | tf_op jit(solution)/shard_map/ppermute | solution.py:122
  20.0 0.1 iota_compare_fusion
  20.1 0.4 collective-permute-done.2.refs_3_
  20.5 2.8 %collective-permute-done.6.refs_7_ = bf16[16,4224]{1,0:T(8,128)(2,1)S(1)} collective-permute-done((bf16[16,4224]{1,0:T(8,128)(2,1)S(1)}, bf16[16,4224]{1,0:T(8,128)(2,1)S(1)}, u32[]{:S(2)}, u32[]{:S(2)}) %collective-permute-start.6) | collective-permute-done | bytes 135200 | tf_op jit(solution)/shard_map/ppermute | solution.py:122
  23.4 1.9 %shard_map.104 = (f32[64,1280]{1,0:T(8,128)S(1)}, f32[64,1280]{1,0:T(8,128)S(1)}, f32[64,128]{1,0:T(8,128)S(1)}) custom-call(bf16[16,4224]{1,0:T(8,128)(2,1)S(1)} %shard_map.101.refs_0_, bf16[16,4224]{1,0:T(8,128)(2,1)S(1)} %collective-permute-done.refs_1_, bf16[16,4224]{1,0:T(8,128)(2,1)S(1)} %collective-permute-done.1.refs_2_, ...), custom_call_target="tpu_custom_call" | custom-call | bytes 1048576 | tf_op jit(solution)/shard_map/pallas_call | solution.py:180
  25.2 0.2 fusion.22
  25.4 0.1 collective-permute-start.7
  25.5 0.2 fusion.28
  25.7 0.1 pad_maximum_fusion.2
  25.8 1.3 %collective-permute-done.7.arrived_ref = f32[64,1280]{1,0:T(8,128)S(1)} collective-permute-done((f32[64,1280]{1,0:T(8,128)S(1)}, f32[64,1280]{1,0:T(8,128)S(1)}, u32[]{:S(2)}, u32[]{:S(2)}) %collective-permute-start.7) | collective-permute-done | bytes 327712 | tf_op jit(solution)/shard_map/ppermute | solution.py:139
  27.1 0.2 shard_map.105
  27.3 0.7 collective-permute-start.8
  27.9 0.4 collective-permute-start.9
  28.4 1.8 %collective-permute-start.10 = (bf16[16,1280]{1,0:T(8,128)(2,1)S(1)}, bf16[16,1280]{1,0:T(8,128)(2,1)S(1)}, u32[]{:S(2)}, u32[]{:S(2)}) collective-permute-start(bf16[16,1280]{1,0:T(8,128)(2,1)S(1)} %get-tuple-element.34), channel_id=1, source_target_pairs={{0,2},{1,12},{2,0},{3,14},{4,6},{5,8},{6,4},{7,10},{8,11},{9,5},{1... | collective-permute-start | bytes 122888 | tf_op jit(solution)/shard_map/ppermute | solution.py:154
  30.1 1.4 %collective-permute-start.11 = (bf16[16,1280]{1,0:T(8,128)(2,1)S(1)}, bf16[16,1280]{1,0:T(8,128)(2,1)S(1)}, u32[]{:S(2)}, u32[]{:S(2)}) collective-permute-start(bf16[16,1280]{1,0:T(8,128)(2,1)S(1)} %get-tuple-element.35), channel_id=1, source_target_pairs={{0,6},{1,14},{2,4},{3,12},{4,2},{5,10},{6,0},{7,8},{8,15},{9,7},{1... | collective-permute-start | bytes 122888 | tf_op jit(solution)/shard_map/ppermute | solution.py:154
  31.5 4.1 %shard_map.100 = (bf16[8,512,4,128]{3,2,1,0:T(4,128)(2,1)S(1)}, bf16[8,512,4,128]{3,2,1,0:T(4,128)(2,1)S(1)}, f32[8,128]{1,0:T(8,128)}) custom-call(bf16[8,512,4,128]{3,2,1,0:T(4,128)(2,1)} %refs_0_.2, bf16[8,512,4,128]{3,2,1,0:T(4,128)(2,1)} %refs_1_.2), custom_call_target="tpu_custom_call" | custom-call | bytes 8388608 | tf_op jit(solution)/shard_map/pallas_call | solution.py:241
  35.6 0.0 collective-permute-done.9
  35.6 0.0 collective-permute-done.10
  35.7 0.7 fusion.31
  36.4 0.0 slice-start
  36.5 1.4 %fusion.30 = (f32[8,4,2,8]{3,2,1,0:T(2,128)S(1)}, f32[8,4,2,8,512]{4,3,2,1,0:T(8,128)S(1)}) fusion(bf16[8,512,4,128,1]{3,2,1,0,4:T(4,128)(2,1)S(1)} %bitcast.34, bf16[4,2,8,8,128]{4,2,3,1,0:T(8,128)(2,1)S(1)} %slice.20, pred[8,512]{1,0:T(8,128)(4,1)S(1)} %iota_compare_fusion), kind=kOutput, calls=%fused_computation.55 | convolution fusion | flops 67894784 | bytes 5380096 | tf_op jit(solution)/shard_map/ktrgd,rckd->rktgc/dot_general | solution.py:350
  37.9 0.1 fusion.18
  38.0 0.4 fusion.13
  38.4 0.0 slice-start.1
  38.4 0.9 %fusion.2 = f32[8,4,128,2,8]{2,4,3,1,0:T(8,128)S(1)} fusion(bf16[8,512,4,128,1]{3,2,1,0,4:T(4,128)(2,1)S(1)} %bitcast.39, f32[8,4,2,8,512]{4,3,2,1,0:T(8,128)S(1)} %get-tuple-element.53, f32[8,4,2,8]{3,2,1,0:T(2,128)S(1)} %add.69, f32[8,4,2,8]{3,2,1,0:T(2,128)S(1)} %max.7), kind=kOutput, calls=%fused_computation.2 | convolution fusion | flops 67895296 | bytes 5509120 | tf_op jit(solution)/shard_map/rktgc,rckd->trkgd/dot_general | solution.py:362
  39.3 0.3 fusion.11
  39.6 0.1 copy.23
  39.7 4.8 %collective-permute-start.15 = (bf16[16,4096]{1,0:T(8,128)(2,1)S(1)}, bf16[16,4096]{1,0:T(8,128)(2,1)S(1)}, u32[]{:S(2)}, u32[]{:S(2)}) collective-permute-start(bf16[16,4096]{1,0:T(8,128)(2,1)S(1)} %bitcast.35), channel_id=1, source_target_pairs={{0,8},{1,9},{2,10},{3,11},{4,12},{5,13},{6,14},{7,15},{8,0},{9,1},... | collective-permute-start | bytes 393224 | tf_op jit(solution)/shard_map/ppermute | solution.py:122
  44.5 2.6 %collective-permute-start.12 = (bf16[16,4096]{1,0:T(8,128)(2,1)S(1)}, bf16[16,4096]{1,0:T(8,128)(2,1)S(1)}, u32[]{:S(2)}, u32[]{:S(2)}) collective-permute-start(bf16[16,4096]{1,0:T(8,128)(2,1)S(1)} %bitcast.36), channel_id=1, source_target_pairs={{0,4},{1,3},{2,6},{3,1},{4,0},{5,7},{6,2},{7,5},{8,12},{9,11},{10,... | collective-permute-start | bytes 393224 | tf_op jit(solution)/shard_map/ppermute | solution.py:122
  47.1 0.8 %collective-permute-done.15.refs_4_ = bf16[16,4096]{1,0:T(8,128)(2,1)S(1)} collective-permute-done((bf16[16,4096]{1,0:T(8,128)(2,1)S(1)}, bf16[16,4096]{1,0:T(8,128)(2,1)S(1)}, u32[]{:S(2)}, u32[]{:S(2)}) %collective-permute-start.15) | collective-permute-done | bytes 131104 | tf_op jit(solution)/shard_map/ppermute | solution.py:122
  47.9 4.5 %collective-permute-start.16 = (bf16[16,4096]{1,0:T(8,128)(2,1)S(1)}, bf16[16,4096]{1,0:T(8,128)(2,1)S(1)}, u32[]{:S(2)}, u32[]{:S(2)}) collective-permute-start(bf16[16,4096]{1,0:T(8,128)(2,1)S(1)} %collective-permute-done.15.refs_4_), channel_id=1, source_target_pairs={{0,4},{1,3},{2,6},{3,1},{4,0},{5,7},{6,2},{7,5},{8,12},{9,11},{10,... | collective-permute-start | bytes 393224 | tf_op jit(solution)/shard_map/ppermute | solution.py:122
  52.4 0.4 collective-permute-start.13
  52.8 1.6 %collective-permute-start.17 = (bf16[16,4096]{1,0:T(8,128)(2,1)S(1)}, bf16[16,4096]{1,0:T(8,128)(2,1)S(1)}, u32[]{:S(2)}, u32[]{:S(2)}) collective-permute-start(bf16[16,4096]{1,0:T(8,128)(2,1)S(1)} %collective-permute-done.15.refs_4_), channel_id=1, source_target_pairs={{0,2},{1,5},{2,0},{3,7},{4,6},{5,1},{6,4},{7,3},{8,10},{9,13},{10,... | collective-permute-start | bytes 393224 | tf_op jit(solution)/shard_map/ppermute | solution.py:122
  54.5 0.0 collective-permute-done.12.refs_1_
  54.5 0.4 collective-permute-start.14
  54.9 1.5 %collective-permute-done.16.refs_5_ = bf16[16,4096]{1,0:T(8,128)(2,1)S(1)} collective-permute-done((bf16[16,4096]{1,0:T(8,128)(2,1)S(1)}, bf16[16,4096]{1,0:T(8,128)(2,1)S(1)}, u32[]{:S(2)}, u32[]{:S(2)}) %collective-permute-start.16) | collective-permute-done | bytes 131104 | tf_op jit(solution)/shard_map/ppermute | solution.py:122
  56.3 2.9 %collective-permute-start.18 = (bf16[16,4096]{1,0:T(8,128)(2,1)S(1)}, bf16[16,4096]{1,0:T(8,128)(2,1)S(1)}, u32[]{:S(2)}, u32[]{:S(2)}) collective-permute-start(bf16[16,4096]{1,0:T(8,128)(2,1)S(1)} %collective-permute-done.16.refs_5_), channel_id=1, source_target_pairs={{0,2},{1,5},{2,0},{3,7},{4,6},{5,1},{6,4},{7,3},{8,10},{9,13},{10,... | collective-permute-start | bytes 393224 | tf_op jit(solution)/shard_map/ppermute | solution.py:122
  59.2 0.0 collective-permute-done.13.refs_2_
  59.2 1.0 %collective-permute-done.14.refs_3_ = bf16[16,4096]{1,0:T(8,128)(2,1)S(1)} collective-permute-done((bf16[16,4096]{1,0:T(8,128)(2,1)S(1)}, bf16[16,4096]{1,0:T(8,128)(2,1)S(1)}, u32[]{:S(2)}, u32[]{:S(2)}) %collective-permute-start.14) | collective-permute-done | bytes 131104 | tf_op jit(solution)/shard_map/ppermute | solution.py:122
  60.2 1.9 %collective-permute-done.18.refs_7_ = bf16[16,4096]{1,0:T(8,128)(2,1)S(1)} collective-permute-done((bf16[16,4096]{1,0:T(8,128)(2,1)S(1)}, bf16[16,4096]{1,0:T(8,128)(2,1)S(1)}, u32[]{:S(2)}, u32[]{:S(2)}) %collective-permute-start.18) | collective-permute-done | bytes 131104 | tf_op jit(solution)/shard_map/ppermute | solution.py:122
  62.2 1.3 %shard_map.106 = (f32[64,1024]{1,0:T(8,128)S(1)}, f32[64,1024]{1,0:T(8,128)S(1)}) custom-call(bf16[16,4096]{1,0:T(8,128)(2,1)S(1)} %bitcast.38, bf16[16,4096]{1,0:T(8,128)(2,1)S(1)} %collective-permute-done.12.refs_1_, bf16[16,4096]{1,0:T(8,128)(2,1)S(1)} %collective-permute-done.13.refs_2_, bf16[16,4096]{1,0:T(8,128)(2,1)S(1)} %collective-permute-done.14.refs_3_, ...), custom_call_target="tpu_custom_call" | custom-call | bytes 1048576 | tf_op jit(solution)/shard_map/pallas_call | solution.py:180
  63.5 0.1 collective-permute-start.19
  63.6 1.5 %collective-permute-done.19.arrived_ref = f32[64,1024]{1,0:T(8,128)S(1)} collective-permute-done((f32[64,1024]{1,0:T(8,128)S(1)}, f32[64,1024]{1,0:T(8,128)S(1)}, u32[]{:S(2)}, u32[]{:S(2)}) %collective-permute-start.19) | collective-permute-done | bytes 262176 | tf_op jit(solution)/shard_map/ppermute | solution.py:139
  65.1 0.7 collective-permute-start.20
  65.8 1.7 %collective-permute-start.21 = (bf16[16,1024]{1,0:T(8,128)(2,1)S(1)}, bf16[16,1024]{1,0:T(8,128)(2,1)S(1)}, u32[]{:S(2)}, u32[]{:S(2)}) collective-permute-start(bf16[16,1024]{1,0:T(8,128)(2,1)S(1)} %get-tuple-element.40), channel_id=1, source_target_pairs={{0,4},{1,10},{2,6},{3,8},{4,0},{5,14},{6,2},{7,12},{8,13},{9,3},{1... | collective-permute-start | bytes 98312 | tf_op jit(solution)/shard_map/ppermute | solution.py:154
  67.5 0.5 collective-permute-start.22
  67.9 1.4 %collective-permute-start.23 = (bf16[16,1024]{1,0:T(8,128)(2,1)S(1)}, bf16[16,1024]{1,0:T(8,128)(2,1)S(1)}, u32[]{:S(2)}, u32[]{:S(2)}) collective-permute-start(bf16[16,1024]{1,0:T(8,128)(2,1)S(1)} %get-tuple-element.42), channel_id=1, source_target_pairs={{0,6},{1,14},{2,4},{3,12},{4,2},{5,10},{6,0},{7,8},{8,15},{9,7},{1... | collective-permute-start | bytes 98312 | tf_op jit(solution)/shard_map/ppermute | solution.py:154
  69.3 0.4 collective-permute-done.21
  69.8 1.6 %collective-permute-done.22 = bf16[16,1024]{1,0:T(8,128)(2,1)S(1)} collective-permute-done((bf16[16,1024]{1,0:T(8,128)(2,1)S(1)}, bf16[16,1024]{1,0:T(8,128)(2,1)S(1)}, u32[]{:S(2)}, u32[]{:S(2)}) %collective-permute-start.22) | collective-permute-done | bytes 32800 | tf_op jit(solution)/shard_map/ppermute | solution.py:154
  71.4 1.6 %collective-permute-done.23 = bf16[16,1024]{1,0:T(8,128)(2,1)S(1)} collective-permute-done((bf16[16,1024]{1,0:T(8,128)(2,1)S(1)}, bf16[16,1024]{1,0:T(8,128)(2,1)S(1)}, u32[]{:S(2)}, u32[]{:S(2)}) %collective-permute-start.23) | collective-permute-done | bytes 32800 | tf_op jit(solution)/shard_map/ppermute | solution.py:154
  73.0 4.6 %collective-permute-start.24 = (bf16[4,16,1024]{2,1,0:T(8,128)(2,1)S(1)}, bf16[4,16,1024]{2,1,0:T(8,128)(2,1)S(1)}, u32[]{:S(2)}, u32[]{:S(2)}) collective-permute-start(bf16[4,16,1024]{2,1,0:T(8,128)(2,1)S(1)} %pad_maximum_fusion.1.own_ref), channel_id=1, source_target_pairs={{0,1},{1,0},{2,3},{3,2},{4,5},{5,4},{6,7},{7,6},{8,9},{9,8},{10,11... | collective-permute-start | bytes 393224 | tf_op jit(solution)/shard_map/ppermute | solution.py:139
  77.6 1.0 %collective-permute-done.24.other_ref = bf16[4,16,1024]{2,1,0:T(8,128)(2,1)S(1)} collective-permute-done((bf16[4,16,1024]{2,1,0:T(8,128)(2,1)S(1)}, bf16[4,16,1024]{2,1,0:T(8,128)(2,1)S(1)}, u32[]{:S(2)}, u32[]{:S(2)}) %collective-permute-start.24) | collective-permute-done | bytes 131104 | tf_op jit(solution)/shard_map/ppermute | solution.py:139
  78.6 0.7 shard_map.108
  (23 shorter events, 0.2 us)
Async XLA Ops:
  1.2 18.8 %copy-start = (s32[8]{0:T(128)S(1)}, s32[8]{0:T(128)}, u32[]{:S(2)}) copy-start(s32[8]{0:T(128)} %param.18) | copy-start | bytes 100
  1.3 10.7 %collective-permute-start.3 = (bf16[16,4224]{1,0:T(8,128)(2,1)S(1)}, bf16[16,4224]{1,0:T(8,128)(2,1)S(1)}, u32[]{:S(2)}, u32[]{:S(2)}) collective-permute-start(bf16[16,4224]{1,0:T(8,128)(2,1)S(1)} %shard_map.101.refs_0_), channel_id=1, source_target_pairs={{0,8},{1,9},{2,10},{3,11},{4,12},{5,13},{6,14},{7,15},{8,0},{9,1},... | collective-permute-start | bytes 405512 | tf_op jit(solution)/shard_map/ppermute | solution.py:122
  5.4 9.2 %collective-permute-start = (bf16[16,4224]{1,0:T(8,128)(2,1)S(1)}, bf16[16,4224]{1,0:T(8,128)(2,1)S(1)}, u32[]{:S(2)}, u32[]{:S(2)}) collective-permute-start(bf16[16,4224]{1,0:T(8,128)(2,1)S(1)} %shard_map.101.refs_0_), channel_id=1, source_target_pairs={{0,4},{1,3},{2,6},{3,1},{4,0},{5,7},{6,2},{7,5},{8,12},{9,11},{10,... | collective-permute-start | bytes 405512 | tf_op jit(solution)/shard_map/ppermute | solution.py:122
  11.9 6.4 %collective-permute-start.4 = (bf16[16,4224]{1,0:T(8,128)(2,1)S(1)}, bf16[16,4224]{1,0:T(8,128)(2,1)S(1)}, u32[]{:S(2)}, u32[]{:S(2)}) collective-permute-start(bf16[16,4224]{1,0:T(8,128)(2,1)S(1)} %shard_map.103.refs_4_), channel_id=1, source_target_pairs={{0,4},{1,3},{2,6},{3,1},{4,0},{5,7},{6,2},{7,5},{8,12},{9,11},{10,... | collective-permute-start | bytes 405512 | tf_op jit(solution)/shard_map/ppermute | solution.py:122
  12.6 7.6 %collective-permute-start.1 = (bf16[16,4224]{1,0:T(8,128)(2,1)S(1)}, bf16[16,4224]{1,0:T(8,128)(2,1)S(1)}, u32[]{:S(2)}, u32[]{:S(2)}) collective-permute-start(bf16[16,4224]{1,0:T(8,128)(2,1)S(1)} %shard_map.101.refs_0_), channel_id=1, source_target_pairs={{0,2},{1,5},{2,0},{3,7},{4,6},{5,1},{6,4},{7,3},{8,10},{9,13},{10,... | collective-permute-start | bytes 405512 | tf_op jit(solution)/shard_map/ppermute | solution.py:122
  14.1 6.1 %collective-permute-start.5 = (bf16[16,4224]{1,0:T(8,128)(2,1)S(1)}, bf16[16,4224]{1,0:T(8,128)(2,1)S(1)}, u32[]{:S(2)}, u32[]{:S(2)}) collective-permute-start(bf16[16,4224]{1,0:T(8,128)(2,1)S(1)} %shard_map.103.refs_4_), channel_id=1, source_target_pairs={{0,2},{1,5},{2,0},{3,7},{4,6},{5,1},{6,4},{7,3},{8,10},{9,13},{10,... | collective-permute-start | bytes 405512 | tf_op jit(solution)/shard_map/ppermute | solution.py:122
  14.6 6.0 %collective-permute-start.2 = (bf16[16,4224]{1,0:T(8,128)(2,1)S(1)}, bf16[16,4224]{1,0:T(8,128)(2,1)S(1)}, u32[]{:S(2)}, u32[]{:S(2)}) collective-permute-start(bf16[16,4224]{1,0:T(8,128)(2,1)S(1)} %collective-permute-done.refs_1_), channel_id=1, source_target_pairs={{0,2},{1,5},{2,0},{3,7},{4,6},{5,1},{6,4},{7,3},{8,10},{9,13},{10,... | collective-permute-start | bytes 405512 | tf_op jit(solution)/shard_map/ppermute | solution.py:122
  18.4 5.0 %collective-permute-start.6 = (bf16[16,4224]{1,0:T(8,128)(2,1)S(1)}, bf16[16,4224]{1,0:T(8,128)(2,1)S(1)}, u32[]{:S(2)}, u32[]{:S(2)}) collective-permute-start(bf16[16,4224]{1,0:T(8,128)(2,1)S(1)} %collective-permute-done.4.refs_5_), channel_id=1, source_target_pairs={{0,2},{1,5},{2,0},{3,7},{4,6},{5,1},{6,4},{7,3},{8,10},{9,13},{10,... | collective-permute-start | bytes 405512 | tf_op jit(solution)/shard_map/ppermute | solution.py:122
  25.4 1.7 %collective-permute-start.7 = (f32[64,1280]{1,0:T(8,128)S(1)}, f32[64,1280]{1,0:T(8,128)S(1)}, u32[]{:S(2)}, u32[]{:S(2)}) collective-permute-start(f32[64,1280]{1,0:T(8,128)S(1)} %get-tuple-element.30), channel_id=1, source_target_pairs={{0,1},{1,0},{2,3},{3,2},{4,5},{5,4},{6,7},{7,6},{8,9},{9,8},{10,11... | collective-permute-start | bytes 983048 | tf_op jit(solution)/shard_map/ppermute | solution.py:139
  27.3 8.3 %collective-permute-start.8 = (bf16[16,1280]{1,0:T(8,128)(2,1)S(1)}, bf16[16,1280]{1,0:T(8,128)(2,1)S(1)}, u32[]{:S(2)}, u32[]{:S(2)}) collective-permute-start(bf16[16,1280]{1,0:T(8,128)(2,1)S(1)} %get-tuple-element.32), channel_id=1, source_target_pairs={{0,0},{1,8},{2,2},{3,10},{4,4},{5,12},{6,6},{7,14},{8,9},{9,1},{10... | collective-permute-start | bytes 122888 | tf_op jit(solution)/shard_map/ppermute | solution.py:154
  27.9 7.6 %collective-permute-start.9 = (bf16[16,1280]{1,0:T(8,128)(2,1)S(1)}, bf16[16,1280]{1,0:T(8,128)(2,1)S(1)}, u32[]{:S(2)}, u32[]{:S(2)}) collective-permute-start(bf16[16,1280]{1,0:T(8,128)(2,1)S(1)} %get-tuple-element.33), channel_id=1, source_target_pairs={{0,4},{1,10},{2,6},{3,8},{4,0},{5,14},{6,2},{7,12},{8,13},{9,3},{1... | collective-permute-start | bytes 122888 | tf_op jit(solution)/shard_map/ppermute | solution.py:154
  28.4 7.2 %collective-permute-start.10 = (bf16[16,1280]{1,0:T(8,128)(2,1)S(1)}, bf16[16,1280]{1,0:T(8,128)(2,1)S(1)}, u32[]{:S(2)}, u32[]{:S(2)}) collective-permute-start(bf16[16,1280]{1,0:T(8,128)(2,1)S(1)} %get-tuple-element.34), channel_id=1, source_target_pairs={{0,2},{1,12},{2,0},{3,14},{4,6},{5,8},{6,4},{7,10},{8,11},{9,5},{1... | collective-permute-start | bytes 122888 | tf_op jit(solution)/shard_map/ppermute | solution.py:154
  30.1 5.5 %collective-permute-start.11 = (bf16[16,1280]{1,0:T(8,128)(2,1)S(1)}, bf16[16,1280]{1,0:T(8,128)(2,1)S(1)}, u32[]{:S(2)}, u32[]{:S(2)}) collective-permute-start(bf16[16,1280]{1,0:T(8,128)(2,1)S(1)} %get-tuple-element.35), channel_id=1, source_target_pairs={{0,6},{1,14},{2,4},{3,12},{4,2},{5,10},{6,0},{7,8},{8,15},{9,7},{1... | collective-permute-start | bytes 122888 | tf_op jit(solution)/shard_map/ppermute | solution.py:154
  36.4 25.7 %slice-start = ((s8[8388608]{0:T(1024)(128)(4,1)}), s8[4194304]{0:T(1024)(128)(4,1)S(1)}, s32[]{:S(2)}) async-start(s8[8388608]{0:T(1024)(128)(4,1)} %bitcast.32), calls=%async_computation | async-start | bytes 8388608
  38.4 23.7 %slice-start.1 = ((s8[8388608]{0:T(1024)(128)(4,1)}), s8[4194304]{0:T(1024)(128)(4,1)S(1)}, s32[]{:S(2)}) async-start(s8[8388608]{0:T(1024)(128)(4,1)} %bitcast.32), calls=%async_computation.1 | async-start | bytes 8388608
  39.7 8.2 %collective-permute-start.15 = (bf16[16,4096]{1,0:T(8,128)(2,1)S(1)}, bf16[16,4096]{1,0:T(8,128)(2,1)S(1)}, u32[]{:S(2)}, u32[]{:S(2)}) collective-permute-start(bf16[16,4096]{1,0:T(8,128)(2,1)S(1)} %bitcast.35), channel_id=1, source_target_pairs={{0,8},{1,9},{2,10},{3,11},{4,12},{5,13},{6,14},{7,15},{8,0},{9,1},... | collective-permute-start | bytes 393224 | tf_op jit(solution)/shard_map/ppermute | solution.py:122
  44.5 9.9 %collective-permute-start.12 = (bf16[16,4096]{1,0:T(8,128)(2,1)S(1)}, bf16[16,4096]{1,0:T(8,128)(2,1)S(1)}, u32[]{:S(2)}, u32[]{:S(2)}) collective-permute-start(bf16[16,4096]{1,0:T(8,128)(2,1)S(1)} %bitcast.36), channel_id=1, source_target_pairs={{0,4},{1,3},{2,6},{3,1},{4,0},{5,7},{6,2},{7,5},{8,12},{9,11},{10,... | collective-permute-start | bytes 393224 | tf_op jit(solution)/shard_map/ppermute | solution.py:122
  47.9 8.4 %collective-permute-start.16 = (bf16[16,4096]{1,0:T(8,128)(2,1)S(1)}, bf16[16,4096]{1,0:T(8,128)(2,1)S(1)}, u32[]{:S(2)}, u32[]{:S(2)}) collective-permute-start(bf16[16,4096]{1,0:T(8,128)(2,1)S(1)} %collective-permute-done.15.refs_4_), channel_id=1, source_target_pairs={{0,4},{1,3},{2,6},{3,1},{4,0},{5,7},{6,2},{7,5},{8,12},{9,11},{10,... | collective-permute-start | bytes 393224 | tf_op jit(solution)/shard_map/ppermute | solution.py:122
  52.4 6.8 %collective-permute-start.13 = (bf16[16,4096]{1,0:T(8,128)(2,1)S(1)}, bf16[16,4096]{1,0:T(8,128)(2,1)S(1)}, u32[]{:S(2)}, u32[]{:S(2)}) collective-permute-start(bf16[16,4096]{1,0:T(8,128)(2,1)S(1)} %bitcast.37), channel_id=1, source_target_pairs={{0,2},{1,5},{2,0},{3,7},{4,6},{5,1},{6,4},{7,3},{8,10},{9,13},{10,... | collective-permute-start | bytes 393224 | tf_op jit(solution)/shard_map/ppermute | solution.py:122
  52.8 7.4 %collective-permute-start.17 = (bf16[16,4096]{1,0:T(8,128)(2,1)S(1)}, bf16[16,4096]{1,0:T(8,128)(2,1)S(1)}, u32[]{:S(2)}, u32[]{:S(2)}) collective-permute-start(bf16[16,4096]{1,0:T(8,128)(2,1)S(1)} %collective-permute-done.15.refs_4_), channel_id=1, source_target_pairs={{0,2},{1,5},{2,0},{3,7},{4,6},{5,1},{6,4},{7,3},{8,10},{9,13},{10,... | collective-permute-start | bytes 393224 | tf_op jit(solution)/shard_map/ppermute | solution.py:122
  54.5 5.7 %collective-permute-start.14 = (bf16[16,4096]{1,0:T(8,128)(2,1)S(1)}, bf16[16,4096]{1,0:T(8,128)(2,1)S(1)}, u32[]{:S(2)}, u32[]{:S(2)}) collective-permute-start(bf16[16,4096]{1,0:T(8,128)(2,1)S(1)} %collective-permute-done.12.refs_1_), channel_id=1, source_target_pairs={{0,2},{1,5},{2,0},{3,7},{4,6},{5,1},{6,4},{7,3},{8,10},{9,13},{10,... | collective-permute-start | bytes 393224 | tf_op jit(solution)/shard_map/ppermute | solution.py:122
  56.3 5.8 %collective-permute-start.18 = (bf16[16,4096]{1,0:T(8,128)(2,1)S(1)}, bf16[16,4096]{1,0:T(8,128)(2,1)S(1)}, u32[]{:S(2)}, u32[]{:S(2)}) collective-permute-start(bf16[16,4096]{1,0:T(8,128)(2,1)S(1)} %collective-permute-done.16.refs_5_), channel_id=1, source_target_pairs={{0,2},{1,5},{2,0},{3,7},{4,6},{5,1},{6,4},{7,3},{8,10},{9,13},{10,... | collective-permute-start | bytes 393224 | tf_op jit(solution)/shard_map/ppermute | solution.py:122
  63.5 1.6 %collective-permute-start.19 = (f32[64,1024]{1,0:T(8,128)S(1)}, f32[64,1024]{1,0:T(8,128)S(1)}, u32[]{:S(2)}, u32[]{:S(2)}) collective-permute-start(f32[64,1024]{1,0:T(8,128)S(1)} %get-tuple-element.38), channel_id=1, source_target_pairs={{0,1},{1,0},{2,3},{3,2},{4,5},{5,4},{6,7},{7,6},{8,9},{9,8},{10,11... | collective-permute-start | bytes 786440 | tf_op jit(solution)/shard_map/ppermute | solution.py:139
  65.1 4.2 %collective-permute-start.20 = (bf16[16,1024]{1,0:T(8,128)(2,1)S(1)}, bf16[16,1024]{1,0:T(8,128)(2,1)S(1)}, u32[]{:S(2)}, u32[]{:S(2)}) collective-permute-start(bf16[16,1024]{1,0:T(8,128)(2,1)S(1)} %get-tuple-element.39), channel_id=1, source_target_pairs={{0,0},{1,8},{2,2},{3,10},{4,4},{5,12},{6,6},{7,14},{8,9},{9,1},{10... | collective-permute-start | bytes 98312 | tf_op jit(solution)/shard_map/ppermute | solution.py:154
  65.8 4.0 %collective-permute-start.21 = (bf16[16,1024]{1,0:T(8,128)(2,1)S(1)}, bf16[16,1024]{1,0:T(8,128)(2,1)S(1)}, u32[]{:S(2)}, u32[]{:S(2)}) collective-permute-start(bf16[16,1024]{1,0:T(8,128)(2,1)S(1)} %get-tuple-element.40), channel_id=1, source_target_pairs={{0,4},{1,10},{2,6},{3,8},{4,0},{5,14},{6,2},{7,12},{8,13},{9,3},{1... | collective-permute-start | bytes 98312 | tf_op jit(solution)/shard_map/ppermute | solution.py:154
  67.5 3.9 %collective-permute-start.22 = (bf16[16,1024]{1,0:T(8,128)(2,1)S(1)}, bf16[16,1024]{1,0:T(8,128)(2,1)S(1)}, u32[]{:S(2)}, u32[]{:S(2)}) collective-permute-start(bf16[16,1024]{1,0:T(8,128)(2,1)S(1)} %get-tuple-element.41), channel_id=1, source_target_pairs={{0,2},{1,12},{2,0},{3,14},{4,6},{5,8},{6,4},{7,10},{8,11},{9,5},{1... | collective-permute-start | bytes 98312 | tf_op jit(solution)/shard_map/ppermute | solution.py:154
  67.9 5.0 %collective-permute-start.23 = (bf16[16,1024]{1,0:T(8,128)(2,1)S(1)}, bf16[16,1024]{1,0:T(8,128)(2,1)S(1)}, u32[]{:S(2)}, u32[]{:S(2)}) collective-permute-start(bf16[16,1024]{1,0:T(8,128)(2,1)S(1)} %get-tuple-element.42), channel_id=1, source_target_pairs={{0,6},{1,14},{2,4},{3,12},{4,2},{5,10},{6,0},{7,8},{8,15},{9,7},{1... | collective-permute-start | bytes 98312 | tf_op jit(solution)/shard_map/ppermute | solution.py:154
  73.0 5.6 %collective-permute-start.24 = (bf16[4,16,1024]{2,1,0:T(8,128)(2,1)S(1)}, bf16[4,16,1024]{2,1,0:T(8,128)(2,1)S(1)}, u32[]{:S(2)}, u32[]{:S(2)}) collective-permute-start(bf16[4,16,1024]{2,1,0:T(8,128)(2,1)S(1)} %pad_maximum_fusion.1.own_ref), channel_id=1, source_target_pairs={{0,1},{1,0},{2,3},{3,2},{4,5},{5,4},{6,7},{7,6},{8,9},{9,8},{10,11... | collective-permute-start | bytes 393224 | tf_op jit(solution)/shard_map/ppermute | solution.py:139

commit v4 on v3

--- a/solution.py
+++ b/solution.py
@@ -112,35 +112,30 @@
     )
 
 
-def exchange_orders(step):
-    return {"far": (4, 4), "near": (2, 1), "last": (1, 2)}[step]
-
-
-def swap_blocks(block, step):
-    flips = exchange_orders(step)
-    pairs = [(2 * o + i, 2 * (o ^ flips[i]) + i) for o in range(8) for i in range(2)]
+ORDERS = ((2, 4, 1), (4, 1, 2))
+SETS = ((), (0,), (1,), (2,), (0, 1), (0, 2), (1, 2), (0, 1, 2))
+OFFSETS = tuple(tuple(sum(order[n] for n in chosen) for chosen in SETS) for order in ORDERS)
+
+
+def exchange(block, n):
+    pairs = [(2 * o + i, 2 * (o ^ ORDERS[i][n]) + i) for o in range(8) for i in range(2)]
     return lax.ppermute(block, ("out", "inp"), pairs)
 
 
-def gather_blocks(block, *marks):
-    far = swap_blocks(block, "far")
-    near = swap_blocks(block, "near")
-    last = swap_blocks(block, "last")
-    if marks:
-        far = after(far, *marks)
-    near_last = swap_blocks(near, "last")
-    far_near = swap_blocks(far, "near")
-    far_last = swap_blocks(far, "last")
-    far_near_last = swap_blocks(far_near, "last")
-    return (block, near, last, near_last), (far, far_near, far_last, far_near_last)
+def gather_blocks(block, mark):
+    a = exchange(block, 0)
+    b = exchange(block, 1)
+    c = exchange(block, 2)
+    c = after(c, mark)
+    bc = exchange(b, 2)
+    ab = exchange(a, 1)
+    ac = exchange(a, 2)
+    abc = exchange(ab, 2)
+    return block, a, b, c, ab, ac, bc, abc
 
 
 def swap_cores(block):
     return lax.ppermute(block, "inp", [(0, 1), (1, 0)])
-
-
-def offset_of(core, place):
-    return (0, 2, 1, 3)[place] if core == 0 else place
 
 
 def hand_out(blocks):
@@ -149,26 +144,14 @@
         pairs = []
         for o in range(8):
             for i in range(2):
-                target = o ^ (4 * i) ^ offset_of(i, place)
+                target = o ^ (4 * i) ^ place
                 pairs.append((2 * o + i, 2 * target + o // 4))
         received.append(lax.ppermute(block, ("out", "inp"), pairs))
     return received
 
 
-def place_of(column, crossed):
-    offset = column ^ (lax.axis_index("out") % 4)
-    swapped = jnp.where((offset == 1) | (offset == 2), 3 - offset, offset)
-    return jnp.where(crossed == 0, swapped, offset)
-
-
-def crossing(core):
-    return (lax.axis_index("out") // 4) ^ core
-
-
-def in_order(received):
-    crossed = crossing(lax.axis_index("inp"))
-    stacked = jnp.stack(received)
-    return jnp.stack([lax.dynamic_index_in_dim(stacked, place_of(c, crossed), 0, keepdims=False) for c in range(4)])
+def place_of(column):
+    return column ^ (lax.axis_index("out") % 4)
 
 
 VMEM_SPEC = pl.BlockSpec(memory_space=pltpu.VMEM)
@@ -270,39 +253,33 @@
     )(block, *others)
 
 
-def stack_rows(core, pieces, rows_ref):
-    rows, depth = pieces[0].shape[0], rows_ref.shape[1]
+def stack_rows(pieces, rows_ref):
+    core = lax.axis_index("inp")
+    rows = pieces[0].shape[0]
     for n, piece in enumerate(pieces):
-        upper = n // 4
-        half = (upper + core + 1) % 2
-        start = pl.multiple_of((half * 4 + n % 4) * rows, rows)
-        rows_ref[pl.ds(start, rows), :] = piece[:, :depth]
+        offset = jnp.where(core == 0, OFFSETS[0][n] ^ 4, OFFSETS[1][n])
+        rows_ref[pl.ds(pl.multiple_of(offset * rows, rows), rows), :] = piece[...]
 
 
 def project_kernel(*refs):
-    core = lax.axis_index("inp")
     pieces, (query_ref, key_ref, value_ref, given_ref, kept_ref, tag_ref, rows_ref) = refs[:8], refs[8:]
-    stack_rows(core, pieces, rows_ref)
-    count = given_ref.shape[0]
-    rows, depth = pieces[0].shape[0], rows_ref.shape[1]
-    for n in range(4):
-        lower, upper = pieces[n][:, depth:], pieces[n + 4][:, depth:]
-        tag_ref[pl.ds(n * rows, rows), :] = jnp.where(core == 0, lower.astype(jnp.float32), upper.astype(jnp.float32))
+    stack_rows(pieces, rows_ref)
+    count, depth = given_ref.shape[0], query_ref.shape[0]
+    tag_ref[...] = rows_ref[count:, depth:].astype(jnp.float32)
     first = 0
     for weight_ref in (query_ref, key_ref, value_ref):
         width = weight_ref.shape[1]
         block = min(256, width)
         for at in range(0, width, block):
-            sums = jnp.dot(rows_ref[...], weight_ref[:, at : at + block], preferred_element_type=jnp.float32)
+            sums = jnp.dot(rows_ref[:, :depth], weight_ref[:, at : at + block], preferred_element_type=jnp.float32)
             given_ref[:, first + at : first + at + block] = sums[:count]
             kept_ref[:, first + at : first + at + block] = sums[count:]
         first += width
 
 
 def mix_kernel(*refs):
-    core = lax.axis_index("inp")
     pieces, (weight_ref, given_ref, kept_ref, rows_ref) = refs[:8], refs[8:]
-    stack_rows(core, pieces, rows_ref)
+    stack_rows(pieces, rows_ref)
     count = given_ref.shape[0]
     for at in range(0, weight_ref.shape[1], 256):
         sums = jnp.dot(rows_ref[...], weight_ref[:, at : at + 256], preferred_element_type=jnp.float32)
@@ -310,19 +287,15 @@
         kept_ref[:, at : at + 256] = sums[count:]
 
 
-ARRIVAL = (0, 2, 1, 3)
-
-
 def turn_kernel(kept_ref, arrived_ref, cosine_ref, sine_ref, *out_refs):
     rows = out_refs[0].shape[0]
     heads = kept_ref.shape[1] // HEAD_SIZE
     for n, out_ref in enumerate(out_refs):
         here = pl.ds(n * rows, rows)
-        there = pl.ds(ARRIVAL[n] * rows, rows)
         cosine, sine = cosine_ref[here, :], sine_ref[here, :]
         for head in range(heads):
             columns = slice(head * HEAD_SIZE, (head + 1) * HEAD_SIZE)
-            total = kept_ref[here, columns] + arrived_ref[there, columns]
+            total = kept_ref[here, columns] + arrived_ref[here, columns]
             if head < heads - 1:
                 total = total * cosine + pltpu.roll(total, HEAD_SIZE // 2, 1) * sine
             out_ref[:, columns] = total.astype(jnp.bfloat16)
@@ -331,7 +304,7 @@
 def round_kernel(kept_ref, arrived_ref, *out_refs):
     rows = out_refs[0].shape[0]
     for n, out_ref in enumerate(out_refs):
-        total = kept_ref[pl.ds(n * rows, rows), :] + arrived_ref[pl.ds(ARRIVAL[n] * rows, rows), :]
+        total = kept_ref[pl.ds(n * rows, rows), :] + arrived_ref[pl.ds(n * rows, rows), :]
         out_ref[...] = total.astype(jnp.bfloat16)
 
 
@@ -341,27 +314,112 @@
     for column in range(4):
         for ref, its_core in ((own_ref, core), (other_ref, 1 - core)):
             start = pl.multiple_of((its_core * 4 + column) * width, width)
-            out_ref[:, pl.ds(start, width)] = ref[place_of(column, crossing(its_core))]
-
-
-def attend_both(queries, new_keys, new_values, cache_keys, cache_values, lengths):
-    factor = HEAD_SIZE ** (-0.5)
-    steps = queries.shape[1]
-    cached = jnp.einsum("ktrgd,rckd->rktgc", queries, cache_keys, preferred_element_type=jnp.float32) * factor
-    visible = jnp.arange(cache_keys.shape[1])[None, :] < lengths[:, None]
-    cached = jnp.where(visible[:, None, None, None, :], cached, -jnp.inf)
-    fresh = jnp.einsum("ktrgd,knrd->rktgn", queries, new_keys, preferred_element_type=jnp.float32) * factor
-    causal = jnp.arange(steps)[:, None] >= jnp.arange(steps)[None, :]
-    fresh = jnp.where(causal[None, None, :, None, :], fresh, -jnp.inf)
-    highest = jnp.maximum(jnp.max(cached, axis=-1), jnp.max(fresh, axis=-1))
-    cached_exp = jnp.exp(cached - highest[..., None])
-    fresh_exp = jnp.exp(fresh - highest[..., None])
-    totals = jnp.sum(cached_exp, axis=-1) + jnp.sum(fresh_exp, axis=-1)
-    cached_prob = (cached_exp / totals[..., None]).astype(jnp.bfloat16)
-    fresh_prob = (fresh_exp / totals[..., None]).astype(jnp.bfloat16)
-    attended = jnp.einsum("rktgc,rckd->trkgd", cached_prob, cache_values, preferred_element_type=jnp.float32)
-    attended = attended + jnp.einsum("rktgn,knrd->trkgd", fresh_prob, new_values, preferred_element_type=jnp.float32)
-    return attended.astype(jnp.bfloat16)
+            out_ref[:, pl.ds(start, width)] = ref[place_of(column)]
+
+
+def attend_kernel(length_ref, *refs):
+    received, refs = refs[:4], refs[4:]
+    keys, values, out_ref, query_rows, fresh_keys, fresh_values, scores = refs
+    rows, columns = keys.shape[0], keys.shape[1]
+    group = query_rows.shape[2]
+    steps = received[0].shape[0] // rows
+    asking = steps * group
+    for place in range(4):
+        block = received[place][...].astype(jnp.float32)
+        head = place_of(place)
+        for g in range(group):
+            query_rows[head, :, g, :] = block[:, g * HEAD_SIZE : (g + 1) * HEAD_SIZE]
+        for step in range(steps):
+            here = slice(step * rows, (step + 1) * rows)
+            fresh_keys[:, step * 4 + head, :] = block[here, group * HEAD_SIZE : (group + 1) * HEAD_SIZE]
+            fresh_values[:, step * 4 + head, :] = block[here, (group + 1) * HEAD_SIZE :]
+    lane = lax.broadcasted_iota(jnp.int32, (asking, 128), 1)
+    own_step = lax.broadcasted_iota(jnp.int32, (asking, 128), 0) // group
+    own_lanes = [lane % 4 == head for head in range(4)]
+    open_to = (lane < 4 * steps) & (lane // 4 <= own_step)
+    across = (((1,), (1,)), ((), ()))
+    padding = jnp.zeros((128 - 4 * steps, HEAD_SIZE), jnp.float32)
+
+    def compact(product):
+        parts = [product[head * asking : (head + 1) * asking] for head in range(4)]
+        return jnp.where(own_lanes[0], parts[0], jnp.where(own_lanes[1], parts[1], jnp.where(own_lanes[2], parts[2], parts[3])))
+
+    def by_head(values, combine):
+        for shift in (4, 8, 16, 32, 64):
+            values = combine(values, pltpu.roll(values, shift, 1))
+        return values
+
+    maxima = []
+    for r in range(rows):
+        queries = jnp.concatenate(
+            [query_rows[head, step * rows + r] for head in range(4) for step in range(steps)]
+        ).astype(jnp.bfloat16)
+        fresh = jnp.concatenate([fresh_keys[r], padding]).astype(jnp.bfloat16)
+        product = lax.dot_general(queries, fresh, across, preferred_element_type=jnp.float32)
+        highest = jnp.where(open_to, compact(product), -jnp.inf)
+        scores[r, :, columns:] = highest
+        for at in range(0, columns, 256):
+            product = lax.dot_general(
+                queries, keys[r, at : at + 256, :], across, preferred_element_type=jnp.float32
+            )
+            for start in (at, at + 128):
+                part = compact(product[:, start - at : start - at + 128])
+                part = jnp.where(lane < 4 * length_ref[r] - start, part, -jnp.inf)
+                scores[r, :, start : start + 128] = part
+                highest = jnp.maximum(highest, part)
+        maxima.append(highest)
+    maxima = by_head(jnp.concatenate(maxima), jnp.maximum)
+    factor = HEAD_SIZE ** (-0.5) * math.log2(math.e)
+    totals = []
+    for r in range(rows):
+        highest = maxima[r * asking : (r + 1) * asking]
+        total = jnp.zeros_like(highest)
+        for start in range(0, columns + 128, 128):
+            part = jnp.exp2((scores[r, :, start : start + 128] - highest) * factor)
+            scores[r, :, start : start + 128] = part
+            total += part
+        totals.append(total)
+    shares = 1.0 / by_head(jnp.concatenate(totals), jnp.add)
+    for r in range(rows):
+        share = shares[r * asking : (r + 1) * asking]
+        spread = []
+        for start in range(0, columns + 128, 128):
+            part = scores[r, :, start : start + 128] * share
+            spread.append(
+                jnp.concatenate([jnp.where(own_lanes[head], part, 0.0) for head in range(4)]).astype(jnp.bfloat16)
+            )
+        fresh = jnp.concatenate([fresh_values[r], padding]).astype(jnp.bfloat16)
+        result = jnp.dot(spread[-1], fresh, preferred_element_type=jnp.float32)
+        result += jnp.dot(jnp.concatenate(spread[:-1], axis=1), values[r], preferred_element_type=jnp.float32)
+        for n in range(4 * steps):
+            query_rows[n // steps, n % steps * rows + r] = result[n * group : (n + 1) * group]
+    for head in range(4):
+        for g in range(group):
+            start = (head * group + g) * HEAD_SIZE
+            out_ref[:, start : start + HEAD_SIZE] = query_rows[head, :, g, :].astype(jnp.bfloat16)
+
+
+def attend(received, cache_keys, cache_values, lengths):
+    shape = jax.ShapeDtypeStruct
+    rows, columns, _ = cache_keys.shape
+    key_heads = 4
+    count, width = received[0].shape
+    group = width // HEAD_SIZE - 2
+    fresh = count // rows * key_heads
+    return pl.pallas_call(
+        attend_kernel,
+        out_shape=shape((count, key_heads * group * HEAD_SIZE), jnp.bfloat16),
+        in_specs=[SMEM_SPEC] + [VMEM_SPEC] * 6,
+        out_specs=VMEM_SPEC,
+        scratch_shapes=[
+            pltpu.VMEM((key_heads, count, group, HEAD_SIZE), jnp.float32),
+            pltpu.VMEM((rows, fresh, HEAD_SIZE), jnp.float32),
+            pltpu.VMEM((rows, fresh, HEAD_SIZE), jnp.float32),
+            pltpu.VMEM((rows, count // rows * group, columns + 128), jnp.float32),
+        ],
+        compiler_params=pltpu.CompilerParams(vmem_limit_bytes=6 * MEGABYTE),
+        cost_estimate=pl.CostEstimate(flops=0, bytes_accessed=12 * MEGABYTE, transcendentals=0),
+    )(lengths, *received, resident(cache_keys), resident(cache_values))
 
 
 def resident(array):
@@ -394,18 +452,19 @@
         place=pl.BlockSpec(memory_space=pltpu.HBM),
     )
     (near_query, near_key, near_value), weight_mark = fetched(query_weight, key_matrix, value_matrix)
-    (cache_keys, cache_values), cache_mark = fetched(cache_keys, cache_values)
-    lower, upper = gather_blocks(own, weight_mark)
+    (near_keys, near_values), cache_mark = fetched(
+        cache_keys.reshape(rows, -1, HEAD_SIZE), cache_values.reshape(rows, -1, HEAD_SIZE)
+    )
+    blocks = gather_blocks(own, weight_mark)
     given, kept, tags = on_chip(
         project_kernel,
         [shape((4 * count, qkv_cols), jnp.float32)] * 2 + [shape((4 * count, 128), jnp.float32)],
         (),
-        *lower,
-        *upper,
+        *blocks,
         resident(near_query),
         resident(near_key),
         resident(near_value),
-        scratch=[pltpu.VMEM((8 * count, half), jnp.bfloat16)],
+        scratch=[pltpu.VMEM((8 * count, half + 128), jnp.bfloat16)],
     )
     arrived = swap_cores(given)
     frequency = jnp.exp(
@@ -423,20 +482,16 @@
         jnp.concatenate([cosine, cosine], axis=-1),
         jnp.concatenate([-sine, sine], axis=-1),
     )
-    heads = in_order(hand_out(outgoing)).reshape(4, steps, rows, -1, HEAD_SIZE)
-    group = query_cols // HEAD_SIZE
-    attended = attend_both(
-        heads[:, :, :, :group], heads[:, :, :, group], heads[:, :, :, group + 1], cache_keys, cache_values, lengths
-    )
-    lower, upper = gather_blocks(attended.reshape(count, half))
+    attended = attend(hand_out(outgoing), near_keys, near_values, lengths)
+    (near_output,), output_mark = fetched(output_weight)
+    blocks = gather_blocks(attended, output_mark)
     mix_cols = output_weight.shape[1]
     given, kept = on_chip(
         mix_kernel,
         [shape((4 * count, mix_cols), jnp.float32)] * 2,
         (),
-        *lower,
-        *upper,
-        resident(output_weight),
+        *blocks,
+        resident(near_output),
         scratch=[pltpu.VMEM((8 * count, half), jnp.bfloat16)],
     )
     outgoing = on_chip(

time: 79.5 us -> 75.3 us (0.947)
  waiting for transfers between devices: 19.2 us -> 9.4 us
  Pallas kernels: 13.4 us -> 20.2 us
  matrix products: 3.24 us -> 0 us
  starting transfers between devices: 41.9 us -> 44.8 us
    ppermute x14, waiting for transfers between devices: 11.7 us -> 2.43 us  [exchange(): return lax.ppermute(block, ('out', 'inp'), pairs)]
    pallas_call x2 -> x3, Pallas kernels: 8.1 us -> 11.6 us  [fetched(): pl.pallas_call(fetch_kernel, out_shape=[pltpu.VMEM(array.shape, array.dty...]
    pallas_call x0 -> x1, Pallas kernels: none -> 3.33 us  [attend(): pl.pallas_call(attend_kernel, out_shape=shape((count, key_heads * group *...]
    dot_general x4 -> x0, matrix products: 3.24 us -> none  [the longest x1 1.37 us: attend_both(): jnp.einsum('ktrgd,rckd->rktgc', queries, cache_keys, preferred_element_ty...]
    ppermute x14, starting transfers between devices: 28.7 us -> 31.4 us  [exchange(): return lax.ppermute(block, ('out', 'inp'), pairs)]
  transfers between devices with their start and end apart: 25 -> 25, of which waited for: 14 -> 10; matrix products, arithmetic and copies ran while one was open for 0% -> 0% of each run, Pallas kernels for 10% -> 15%
where the time goes in v4:
time: 75.3 us; the launch traced here: 75.2 us
  starting transfers between devices  44.8 us (59%)
  Pallas kernels  20.2 us (27%)
  waiting for transfers between devices  9.4 us (12%)
    ppermute x14, starting transfers between devices, exchange(): return lax.ppermute(block, ('out', 'inp'), pairs)  31.4 us
    pallas_call x3, Pallas kernels, fetched(): pl.pallas_call(fetch_kernel, out_shape=[pltpu.VMEM(array.shape, array.dty...  11.6 us
    ppermute x8, starting transfers between devices, hand_out(): received.append(lax.ppermute(block, ('out', 'inp'), pairs))  8.44 us
    pallas_call x6, Pallas kernels, on_chip(): pl.pallas_call(kernel, out_shape=out_shape, in_specs=[SMEM_SPEC] * len(sc...  5.25 us
    ppermute x3, starting transfers between devices, swap_cores(): return lax.ppermute(block, 'inp', [(0, 1), (1, 0)])  4.94 us
    ppermute x8, waiting for transfers between devices, hand_out(): received.append(lax.ppermute(block, ('out', 'inp'), pairs))  3.5 us
    ppermute x3, waiting for transfers between devices, swap_cores(): return lax.ppermute(block, 'inp', [(0, 1), (1, 0)])  3.47 us
    pallas_call x1, Pallas kernels, attend(): pl.pallas_call(attend_kernel, out_shape=shape((count, key_heads * group *...  3.33 us
  transfers between devices with their start and end apart: 25, of which 10 were waited for; matrix products, arithmetic and copies ran while one was open for 0% of the time, Pallas kernels for 15%

profile of v4, /device:TPU:0, one launch (start us, length us, event | category | flops | bytes accessed | tf_op | source)
XLA Modules:
  0.0 75.2 jit_solution(9649221193595232742)
XLA Ops:
  0.0 1.2 %shard_map.100.refs_0_ = bf16[16,4224]{1,0:T(8,128)(2,1)S(1)} custom-call(s32[8]{0:T(128)} %position_hbm.1, bf16[16,8192]{1,0:T(8,128)(2,1)} %bitcast.11, f32[1,8192]{1,0:T(1,128)} %bitcast.12), custom_call_target="tpu_custom_call" | custom-call | bytes 1048576 | tf_op jit(solution)/shard_map/pallas_call | solution.py:163
  1.2 3.1 %collective-permute-start = (bf16[16,4224]{1,0:T(8,128)(2,1)S(1)}, bf16[16,4224]{1,0:T(8,128)(2,1)S(1)}, u32[]{:S(2)}, u32[]{:S(2)}) collective-permute-start(bf16[16,4224]{1,0:T(8,128)(2,1)S(1)} %shard_map.100.refs_0_), channel_id=1, source_target_pairs={{0,4},{1,9},{2,6},{3,11},{4,0},{5,13},{6,2},{7,15},{8,12},{9,1},{1... | collective-permute-start | bytes 405512 | tf_op jit(solution)/shard_map/ppermute | solution.py:122
  4.3 2.6 %collective-permute-start.1 = (bf16[16,4224]{1,0:T(8,128)(2,1)S(1)}, bf16[16,4224]{1,0:T(8,128)(2,1)S(1)}, u32[]{:S(2)}, u32[]{:S(2)}) collective-permute-start(bf16[16,4224]{1,0:T(8,128)(2,1)S(1)} %shard_map.100.refs_0_), channel_id=1, source_target_pairs={{0,8},{1,3},{2,10},{3,1},{4,12},{5,7},{6,14},{7,5},{8,0},{9,11},{1... | collective-permute-start | bytes 405512 | tf_op jit(solution)/shard_map/ppermute | solution.py:122
  6.9 1.5 %collective-permute-done.refs_1_ = bf16[16,4224]{1,0:T(8,128)(2,1)S(1)} collective-permute-done((bf16[16,4224]{1,0:T(8,128)(2,1)S(1)}, bf16[16,4224]{1,0:T(8,128)(2,1)S(1)}, u32[]{:S(2)}, u32[]{:S(2)}) %collective-permute-start) | collective-permute-done | bytes 135200 | tf_op jit(solution)/shard_map/ppermute | solution.py:122
  8.4 2.3 %collective-permute-start.3 = (bf16[16,4224]{1,0:T(8,128)(2,1)S(1)}, bf16[16,4224]{1,0:T(8,128)(2,1)S(1)}, u32[]{:S(2)}, u32[]{:S(2)}) collective-permute-start(bf16[16,4224]{1,0:T(8,128)(2,1)S(1)} %collective-permute-done.refs_1_), channel_id=1, source_target_pairs={{0,8},{1,3},{2,10},{3,1},{4,12},{5,7},{6,14},{7,5},{8,0},{9,11},{1... | collective-permute-start | bytes 405512 | tf_op jit(solution)/shard_map/ppermute | solution.py:122
  10.7 1.5 %collective-permute-start.2 = (bf16[16,4224]{1,0:T(8,128)(2,1)S(1)}, bf16[16,4224]{1,0:T(8,128)(2,1)S(1)}, u32[]{:S(2)}, u32[]{:S(2)}) collective-permute-start(bf16[16,4224]{1,0:T(8,128)(2,1)S(1)} %shard_map.100.refs_0_), channel_id=1, source_target_pairs={{0,2},{1,5},{2,0},{3,7},{4,6},{5,1},{6,4},{7,3},{8,10},{9,13},{10,... | collective-permute-start | bytes 405512 | tf_op jit(solution)/shard_map/ppermute | solution.py:122
  12.2 0.5 collective-permute-start.4
  12.7 0.0 collective-permute-done.1.refs_2_
  12.7 1.5 %collective-permute-start.5 = (bf16[16,4224]{1,0:T(8,128)(2,1)S(1)}, bf16[16,4224]{1,0:T(8,128)(2,1)S(1)}, u32[]{:S(2)}, u32[]{:S(2)}) collective-permute-start(bf16[16,4224]{1,0:T(8,128)(2,1)S(1)} %collective-permute-done.1.refs_2_), channel_id=1, source_target_pairs={{0,2},{1,5},{2,0},{3,7},{4,6},{5,1},{6,4},{7,3},{8,10},{9,13},{10,... | collective-permute-start | bytes 405512 | tf_op jit(solution)/shard_map/ppermute | solution.py:122
  14.3 0.2 collective-permute-done.3.refs_4_
  14.4 3.1 %collective-permute-start.6 = (bf16[16,4224]{1,0:T(8,128)(2,1)S(1)}, bf16[16,4224]{1,0:T(8,128)(2,1)S(1)}, u32[]{:S(2)}, u32[]{:S(2)}) collective-permute-start(bf16[16,4224]{1,0:T(8,128)(2,1)S(1)} %collective-permute-done.3.refs_4_), channel_id=1, source_target_pairs={{0,2},{1,5},{2,0},{3,7},{4,6},{5,1},{6,4},{7,3},{8,10},{9,13},{10,... | collective-permute-start | bytes 405512 | tf_op jit(solution)/shard_map/ppermute | solution.py:122
  17.5 4.0 %shard_map.101 = (bf16[4096,1024]{1,0:T(8,128)(2,1)S(1)}, bf16[4096,128]{1,0:T(8,128)(2,1)S(1)}, bf16[4096,128]{1,0:T(8,128)(2,1)S(1)}, f32[8,128]{1,0:T(8,128)S(1)}) custom-call(bf16[4096,1024]{1,0:T(8,128)(2,1)} %refs_0_.2, bf16[4096,128]{1,0:T(8,128)(2,1)} %refs_1_.1, bf16[4096,128]{1,0:T(8,128)(2,1)} %refs_2_.1), custom_call_target="tpu_custom_call" | custom-call | bytes 10485760 | tf_op jit(solution)/shard_map/pallas_call | solution.py:224
  21.6 0.0 collective-permute-done.2.refs_0_
  21.6 0.0 collective-permute-done.4.refs_5_
  21.6 0.0 collective-permute-done.5.refs_6_
  21.6 0.0 collective-permute-done.6.refs_7_
  21.6 0.0 copy-start
  21.6 1.9 %shard_map.103 = (f32[64,1280]{1,0:T(8,128)S(1)}, f32[64,1280]{1,0:T(8,128)S(1)}, f32[64,128]{1,0:T(8,128)S(1)}) custom-call(bf16[16,4224]{1,0:T(8,128)(2,1)S(1)} %shard_map.100.refs_0_, bf16[16,4224]{1,0:T(8,128)(2,1)S(1)} %collective-permute-done.refs_1_, bf16[16,4224]{1,0:T(8,128)(2,1)S(1)} %collective-permute-done.1.refs_2_, ...), custom_call_target="tpu_custom_call" | custom-call | bytes 1048576 | tf_op jit(solution)/shard_map/pallas_call | solution.py:163
  23.5 0.2 fusion.3
  23.7 0.1 collective-permute-start.7
  23.8 0.2 fusion.7
  24.0 0.1 pad_maximum_fusion.1
  24.1 1.3 %collective-permute-done.7.arrived_ref = f32[64,1280]{1,0:T(8,128)S(1)} collective-permute-done((f32[64,1280]{1,0:T(8,128)S(1)}, f32[64,1280]{1,0:T(8,128)S(1)}, u32[]{:S(2)}, u32[]{:S(2)}) %collective-permute-start.7) | collective-permute-done | bytes 327712 | tf_op jit(solution)/shard_map/ppermute | solution.py:138
  25.4 0.2 shard_map.104
  25.5 1.1 %collective-permute-start.10 = (bf16[16,1280]{1,0:T(8,128)(2,1)S(1)}, bf16[16,1280]{1,0:T(8,128)(2,1)S(1)}, u32[]{:S(2)}, u32[]{:S(2)}) collective-permute-start(bf16[16,1280]{1,0:T(8,128)(2,1)S(1)} %get-tuple-element.35), channel_id=1, source_target_pairs={{0,4},{1,12},{2,6},{3,14},{4,0},{5,8},{6,2},{7,10},{8,13},{9,5},{1... | collective-permute-start | bytes 122888 | tf_op jit(solution)/shard_map/ppermute | solution.py:149
  26.6 1.3 %collective-permute-start.11 = (bf16[16,1280]{1,0:T(8,128)(2,1)S(1)}, bf16[16,1280]{1,0:T(8,128)(2,1)S(1)}, u32[]{:S(2)}, u32[]{:S(2)}) collective-permute-start(bf16[16,1280]{1,0:T(8,128)(2,1)S(1)} %get-tuple-element.36), channel_id=1, source_target_pairs={{0,6},{1,14},{2,4},{3,12},{4,2},{5,10},{6,0},{7,8},{8,15},{9,7},{1... | collective-permute-start | bytes 122888 | tf_op jit(solution)/shard_map/ppermute | solution.py:149
  27.9 0.7 collective-permute-start.8
  28.6 1.2 %collective-permute-start.9 = (bf16[16,1280]{1,0:T(8,128)(2,1)S(1)}, bf16[16,1280]{1,0:T(8,128)(2,1)S(1)}, u32[]{:S(2)}, u32[]{:S(2)}) collective-permute-start(bf16[16,1280]{1,0:T(8,128)(2,1)S(1)} %get-tuple-element.34), channel_id=1, source_target_pairs={{0,2},{1,10},{2,0},{3,8},{4,6},{5,14},{6,4},{7,12},{8,11},{9,3},{1... | collective-permute-start | bytes 122888 | tf_op jit(solution)/shard_map/ppermute | solution.py:149
  29.8 4.1 %shard_map.105 = (bf16[8,2048,128]{2,1,0:T(8,128)(2,1)S(1)}, bf16[8,2048,128]{2,1,0:T(8,128)(2,1)S(1)}, f32[8,128]{1,0:T(8,128)}) custom-call(bf16[8,2048,128]{2,1,0:T(8,128)(2,1)} %bitcast.9, bf16[8,2048,128]{2,1,0:T(8,128)(2,1)} %bitcast.10), custom_call_target="tpu_custom_call" | custom-call | bytes 8388608 | tf_op jit(solution)/shard_map/pallas_call | solution.py:224
  33.9 0.0 collective-permute-done.10.refs_2_
  33.9 0.0 collective-permute-done.11.refs_3_
  33.9 0.0 collective-permute-done.8.refs_0_
  33.9 0.0 collective-permute-done.9.refs_1_
  33.9 0.0 copy-done
  33.9 3.3 %shard_map.106.refs_0_ = bf16[16,4096]{1,0:T(8,128)(2,1)S(1)} custom-call(s32[8]{0:T(128)S(1)} %copy-done, bf16[16,1280]{1,0:T(8,128)(2,1)S(1)} %collective-permute-done.8.refs_0_, bf16[16,1280]{1,0:T(8,128)(2,1)S(1)} %collective-permute-done.9.refs_1_, bf16[16,1280]{1,0:T(8,128)(2,1)S(1)} %collective-permute-done.10.refs_2_, ...), custom_call_target="tpu_custom_call" | custom-call | bytes 12582912 | tf_op jit(solution)/shard_map/pallas_call | solution.py:409
  37.3 1.1 %collective-permute-start.12 = (bf16[16,4096]{1,0:T(8,128)(2,1)S(1)}, bf16[16,4096]{1,0:T(8,128)(2,1)S(1)}, u32[]{:S(2)}, u32[]{:S(2)}) collective-permute-start(bf16[16,4096]{1,0:T(8,128)(2,1)S(1)} %shard_map.106.refs_0_), channel_id=1, source_target_pairs={{0,4},{1,9},{2,6},{3,11},{4,0},{5,13},{6,2},{7,15},{8,12},{9,1},{1... | collective-permute-start | bytes 393224 | tf_op jit(solution)/shard_map/ppermute | solution.py:122
  38.4 5.9 %collective-permute-start.13 = (bf16[16,4096]{1,0:T(8,128)(2,1)S(1)}, bf16[16,4096]{1,0:T(8,128)(2,1)S(1)}, u32[]{:S(2)}, u32[]{:S(2)}) collective-permute-start(bf16[16,4096]{1,0:T(8,128)(2,1)S(1)} %shard_map.106.refs_0_), channel_id=1, source_target_pairs={{0,8},{1,3},{2,10},{3,1},{4,12},{5,7},{6,14},{7,5},{8,0},{9,11},{1... | collective-permute-start | bytes 393224 | tf_op jit(solution)/shard_map/ppermute | solution.py:122
  44.3 0.0 collective-permute-done.12.refs_1_
  44.3 4.2 %collective-permute-start.15 = (bf16[16,4096]{1,0:T(8,128)(2,1)S(1)}, bf16[16,4096]{1,0:T(8,128)(2,1)S(1)}, u32[]{:S(2)}, u32[]{:S(2)}) collective-permute-start(bf16[16,4096]{1,0:T(8,128)(2,1)S(1)} %collective-permute-done.12.refs_1_), channel_id=1, source_target_pairs={{0,8},{1,3},{2,10},{3,1},{4,12},{5,7},{6,14},{7,5},{8,0},{9,11},{1... | collective-permute-start | bytes 393224 | tf_op jit(solution)/shard_map/ppermute | solution.py:122
  48.5 2.1 %collective-permute-start.14 = (bf16[16,4096]{1,0:T(8,128)(2,1)S(1)}, bf16[16,4096]{1,0:T(8,128)(2,1)S(1)}, u32[]{:S(2)}, u32[]{:S(2)}) collective-permute-start(bf16[16,4096]{1,0:T(8,128)(2,1)S(1)} %shard_map.106.refs_0_), channel_id=1, source_target_pairs={{0,2},{1,5},{2,0},{3,7},{4,6},{5,1},{6,4},{7,3},{8,10},{9,13},{10,... | collective-permute-start | bytes 393224 | tf_op jit(solution)/shard_map/ppermute | solution.py:122
  50.6 0.0 collective-permute-start.16
  50.7 0.0 collective-permute-done.13.refs_2_
  50.7 2.0 %collective-permute-start.17 = (bf16[16,4096]{1,0:T(8,128)(2,1)S(1)}, bf16[16,4096]{1,0:T(8,128)(2,1)S(1)}, u32[]{:S(2)}, u32[]{:S(2)}) collective-permute-start(bf16[16,4096]{1,0:T(8,128)(2,1)S(1)} %collective-permute-done.13.refs_2_), channel_id=1, source_target_pairs={{0,2},{1,5},{2,0},{3,7},{4,6},{5,1},{6,4},{7,3},{8,10},{9,13},{10,... | collective-permute-start | bytes 393224 | tf_op jit(solution)/shard_map/ppermute | solution.py:122
  52.7 0.5 collective-permute-done.15.refs_4_
  53.2 1.5 %collective-permute-start.18 = (bf16[16,4096]{1,0:T(8,128)(2,1)S(1)}, bf16[16,4096]{1,0:T(8,128)(2,1)S(1)}, u32[]{:S(2)}, u32[]{:S(2)}) collective-permute-start(bf16[16,4096]{1,0:T(8,128)(2,1)S(1)} %collective-permute-done.15.refs_4_), channel_id=1, source_target_pairs={{0,2},{1,5},{2,0},{3,7},{4,6},{5,1},{6,4},{7,3},{8,10},{9,13},{10,... | collective-permute-start | bytes 393224 | tf_op jit(solution)/shard_map/ppermute | solution.py:122
  54.7 3.5 %shard_map.107 = (bf16[4096,1024]{1,0:T(8,128)(2,1)S(1)}, f32[8,128]{1,0:T(8,128)S(1)}) custom-call(bf16[4096,1024]{1,0:T(8,128)(2,1)} %refs_0_.3), custom_call_target="tpu_custom_call" | custom-call | bytes 8388608 | tf_op jit(solution)/shard_map/pallas_call | solution.py:224
  58.2 0.0 collective-permute-done.14.refs_0_
  58.2 0.0 collective-permute-done.16.refs_5_
  58.2 0.0 collective-permute-done.17.refs_6_
  58.2 0.2 collective-permute-done.18.refs_7_
  58.4 1.3 %shard_map.109 = (f32[64,1024]{1,0:T(8,128)S(1)}, f32[64,1024]{1,0:T(8,128)S(1)}) custom-call(bf16[16,4096]{1,0:T(8,128)(2,1)S(1)} %shard_map.106.refs_0_, bf16[16,4096]{1,0:T(8,128)(2,1)S(1)} %collective-permute-done.12.refs_1_, bf16[16,4096]{1,0:T(8,128)(2,1)S(1)} %collective-permute-done.13.refs_2_, bf16[16,4096]{1,0:T(8,128)(2,1)S(1)} %shard_map.108.refs_3_, ...), custom_call_target="tpu_custom_call" | custom-call | bytes 1048576 | tf_op jit(solution)/shard_map/pallas_call | solution.py:163
  59.7 0.6 collective-permute-start.19
  60.3 1.2 %collective-permute-done.19.arrived_ref = f32[64,1024]{1,0:T(8,128)S(1)} collective-permute-done((f32[64,1024]{1,0:T(8,128)S(1)}, f32[64,1024]{1,0:T(8,128)S(1)}, u32[]{:S(2)}, u32[]{:S(2)}) %collective-permute-start.19) | collective-permute-done | bytes 262176 | tf_op jit(solution)/shard_map/ppermute | solution.py:138
  61.5 0.7 collective-permute-start.20
  62.2 1.3 %collective-permute-start.21 = (bf16[16,1024]{1,0:T(8,128)(2,1)S(1)}, bf16[16,1024]{1,0:T(8,128)(2,1)S(1)}, u32[]{:S(2)}, u32[]{:S(2)}) collective-permute-start(bf16[16,1024]{1,0:T(8,128)(2,1)S(1)} %get-tuple-element.44), channel_id=1, source_target_pairs={{0,2},{1,10},{2,0},{3,8},{4,6},{5,14},{6,4},{7,12},{8,11},{9,3},{1... | collective-permute-start | bytes 98312 | tf_op jit(solution)/shard_map/ppermute | solution.py:149
  63.4 1.0 %collective-permute-start.22 = (bf16[16,1024]{1,0:T(8,128)(2,1)S(1)}, bf16[16,1024]{1,0:T(8,128)(2,1)S(1)}, u32[]{:S(2)}, u32[]{:S(2)}) collective-permute-start(bf16[16,1024]{1,0:T(8,128)(2,1)S(1)} %get-tuple-element.45), channel_id=1, source_target_pairs={{0,4},{1,12},{2,6},{3,14},{4,0},{5,8},{6,2},{7,10},{8,13},{9,5},{1... | collective-permute-start | bytes 98312 | tf_op jit(solution)/shard_map/ppermute | solution.py:149
  64.4 1.3 %collective-permute-start.23 = (bf16[16,1024]{1,0:T(8,128)(2,1)S(1)}, bf16[16,1024]{1,0:T(8,128)(2,1)S(1)}, u32[]{:S(2)}, u32[]{:S(2)}) collective-permute-start(bf16[16,1024]{1,0:T(8,128)(2,1)S(1)} %get-tuple-element.46), channel_id=1, source_target_pairs={{0,6},{1,14},{2,4},{3,12},{4,2},{5,10},{6,0},{7,8},{8,15},{9,7},{1... | collective-permute-start | bytes 98312 | tf_op jit(solution)/shard_map/ppermute | solution.py:149
  65.7 0.0 collective-permute-done.20
  65.7 0.4 collective-permute-done.21
  66.1 1.2 %collective-permute-done.22 = bf16[16,1024]{1,0:T(8,128)(2,1)S(1)} collective-permute-done((bf16[16,1024]{1,0:T(8,128)(2,1)S(1)}, bf16[16,1024]{1,0:T(8,128)(2,1)S(1)}, u32[]{:S(2)}, u32[]{:S(2)}) %collective-permute-start.22) | collective-permute-done | bytes 32800 | tf_op jit(solution)/shard_map/ppermute | solution.py:149
  67.4 1.8 %collective-permute-done.23 = bf16[16,1024]{1,0:T(8,128)(2,1)S(1)} collective-permute-done((bf16[16,1024]{1,0:T(8,128)(2,1)S(1)}, bf16[16,1024]{1,0:T(8,128)(2,1)S(1)}, u32[]{:S(2)}, u32[]{:S(2)}) %collective-permute-start.23) | collective-permute-done | bytes 32800 | tf_op jit(solution)/shard_map/ppermute | solution.py:149
  69.2 4.2 %collective-permute-start.24 = (bf16[4,16,1024]{2,1,0:T(8,128)(2,1)S(1)}, bf16[4,16,1024]{2,1,0:T(8,128)(2,1)S(1)}, u32[]{:S(2)}, u32[]{:S(2)}) collective-permute-start(bf16[4,16,1024]{2,1,0:T(8,128)(2,1)S(1)} %pad_maximum_fusion.own_ref), channel_id=1, source_target_pairs={{0,1},{1,0},{2,3},{3,2},{4,5},{5,4},{6,7},{7,6},{8,9},{9,8},{10,11... | collective-permute-start | bytes 393224 | tf_op jit(solution)/shard_map/ppermute | solution.py:138
  73.5 1.0 %collective-permute-done.24.other_ref = bf16[4,16,1024]{2,1,0:T(8,128)(2,1)S(1)} collective-permute-done((bf16[4,16,1024]{2,1,0:T(8,128)(2,1)S(1)}, bf16[4,16,1024]{2,1,0:T(8,128)(2,1)S(1)}, u32[]{:S(2)}, u32[]{:S(2)}) %collective-permute-start.24) | collective-permute-done | bytes 131104 | tf_op jit(solution)/shard_map/ppermute | solution.py:138
  74.5 0.7 shard_map.111
  (5 shorter events, 0.1 us)
Async XLA Ops:
  1.2 7.2 %collective-permute-start = (bf16[16,4224]{1,0:T(8,128)(2,1)S(1)}, bf16[16,4224]{1,0:T(8,128)(2,1)S(1)}, u32[]{:S(2)}, u32[]{:S(2)}) collective-permute-start(bf16[16,4224]{1,0:T(8,128)(2,1)S(1)} %shard_map.100.refs_0_), channel_id=1, source_target_pairs={{0,4},{1,9},{2,6},{3,11},{4,0},{5,13},{6,2},{7,15},{8,12},{9,1},{1... | collective-permute-start | bytes 405512 | tf_op jit(solution)/shard_map/ppermute | solution.py:122
  4.3 8.4 %collective-permute-start.1 = (bf16[16,4224]{1,0:T(8,128)(2,1)S(1)}, bf16[16,4224]{1,0:T(8,128)(2,1)S(1)}, u32[]{:S(2)}, u32[]{:S(2)}) collective-permute-start(bf16[16,4224]{1,0:T(8,128)(2,1)S(1)} %shard_map.100.refs_0_), channel_id=1, source_target_pairs={{0,8},{1,3},{2,10},{3,1},{4,12},{5,7},{6,14},{7,5},{8,0},{9,11},{1... | collective-permute-start | bytes 405512 | tf_op jit(solution)/shard_map/ppermute | solution.py:122
  8.4 6.0 %collective-permute-start.3 = (bf16[16,4224]{1,0:T(8,128)(2,1)S(1)}, bf16[16,4224]{1,0:T(8,128)(2,1)S(1)}, u32[]{:S(2)}, u32[]{:S(2)}) collective-permute-start(bf16[16,4224]{1,0:T(8,128)(2,1)S(1)} %collective-permute-done.refs_1_), channel_id=1, source_target_pairs={{0,8},{1,3},{2,10},{3,1},{4,12},{5,7},{6,14},{7,5},{8,0},{9,11},{1... | collective-permute-start | bytes 405512 | tf_op jit(solution)/shard_map/ppermute | solution.py:122
  10.7 10.9 %collective-permute-start.2 = (bf16[16,4224]{1,0:T(8,128)(2,1)S(1)}, bf16[16,4224]{1,0:T(8,128)(2,1)S(1)}, u32[]{:S(2)}, u32[]{:S(2)}) collective-permute-start(bf16[16,4224]{1,0:T(8,128)(2,1)S(1)} %shard_map.100.refs_0_), channel_id=1, source_target_pairs={{0,2},{1,5},{2,0},{3,7},{4,6},{5,1},{6,4},{7,3},{8,10},{9,13},{10,... | collective-permute-start | bytes 405512 | tf_op jit(solution)/shard_map/ppermute | solution.py:122
  12.2 9.4 %collective-permute-start.4 = (bf16[16,4224]{1,0:T(8,128)(2,1)S(1)}, bf16[16,4224]{1,0:T(8,128)(2,1)S(1)}, u32[]{:S(2)}, u32[]{:S(2)}) collective-permute-start(bf16[16,4224]{1,0:T(8,128)(2,1)S(1)} %collective-permute-done.refs_1_), channel_id=1, source_target_pairs={{0,2},{1,5},{2,0},{3,7},{4,6},{5,1},{6,4},{7,3},{8,10},{9,13},{10,... | collective-permute-start | bytes 405512 | tf_op jit(solution)/shard_map/ppermute | solution.py:122
  12.7 8.9 %collective-permute-start.5 = (bf16[16,4224]{1,0:T(8,128)(2,1)S(1)}, bf16[16,4224]{1,0:T(8,128)(2,1)S(1)}, u32[]{:S(2)}, u32[]{:S(2)}) collective-permute-start(bf16[16,4224]{1,0:T(8,128)(2,1)S(1)} %collective-permute-done.1.refs_2_), channel_id=1, source_target_pairs={{0,2},{1,5},{2,0},{3,7},{4,6},{5,1},{6,4},{7,3},{8,10},{9,13},{10,... | collective-permute-start | bytes 405512 | tf_op jit(solution)/shard_map/ppermute | solution.py:122
  14.4 7.2 %collective-permute-start.6 = (bf16[16,4224]{1,0:T(8,128)(2,1)S(1)}, bf16[16,4224]{1,0:T(8,128)(2,1)S(1)}, u32[]{:S(2)}, u32[]{:S(2)}) collective-permute-start(bf16[16,4224]{1,0:T(8,128)(2,1)S(1)} %collective-permute-done.3.refs_4_), channel_id=1, source_target_pairs={{0,2},{1,5},{2,0},{3,7},{4,6},{5,1},{6,4},{7,3},{8,10},{9,13},{10,... | collective-permute-start | bytes 405512 | tf_op jit(solution)/shard_map/ppermute | solution.py:122
  21.6 12.3 %copy-start = (s32[8]{0:T(128)S(1)}, s32[8]{0:T(128)}, u32[]{:S(2)}) copy-start(s32[8]{0:T(128)} %length_ref.1) | copy-start | bytes 100
  23.7 1.7 %collective-permute-start.7 = (f32[64,1280]{1,0:T(8,128)S(1)}, f32[64,1280]{1,0:T(8,128)S(1)}, u32[]{:S(2)}, u32[]{:S(2)}) collective-permute-start(f32[64,1280]{1,0:T(8,128)S(1)} %get-tuple-element.31), channel_id=1, source_target_pairs={{0,1},{1,0},{2,3},{3,2},{4,5},{5,4},{6,7},{7,6},{8,9},{9,8},{10,11... | collective-permute-start | bytes 983048 | tf_op jit(solution)/shard_map/ppermute | solution.py:138
  25.5 8.3 %collective-permute-start.10 = (bf16[16,1280]{1,0:T(8,128)(2,1)S(1)}, bf16[16,1280]{1,0:T(8,128)(2,1)S(1)}, u32[]{:S(2)}, u32[]{:S(2)}) collective-permute-start(bf16[16,1280]{1,0:T(8,128)(2,1)S(1)} %get-tuple-element.35), channel_id=1, source_target_pairs={{0,4},{1,12},{2,6},{3,14},{4,0},{5,8},{6,2},{7,10},{8,13},{9,5},{1... | collective-permute-start | bytes 122888 | tf_op jit(solution)/shard_map/ppermute | solution.py:149
  26.6 7.2 %collective-permute-start.11 = (bf16[16,1280]{1,0:T(8,128)(2,1)S(1)}, bf16[16,1280]{1,0:T(8,128)(2,1)S(1)}, u32[]{:S(2)}, u32[]{:S(2)}) collective-permute-start(bf16[16,1280]{1,0:T(8,128)(2,1)S(1)} %get-tuple-element.36), channel_id=1, source_target_pairs={{0,6},{1,14},{2,4},{3,12},{4,2},{5,10},{6,0},{7,8},{8,15},{9,7},{1... | collective-permute-start | bytes 122888 | tf_op jit(solution)/shard_map/ppermute | solution.py:149
  27.9 6.0 %collective-permute-start.8 = (bf16[16,1280]{1,0:T(8,128)(2,1)S(1)}, bf16[16,1280]{1,0:T(8,128)(2,1)S(1)}, u32[]{:S(2)}, u32[]{:S(2)}) collective-permute-start(bf16[16,1280]{1,0:T(8,128)(2,1)S(1)} %get-tuple-element.33), channel_id=1, source_target_pairs={{0,0},{1,8},{2,2},{3,10},{4,4},{5,12},{6,6},{7,14},{8,9},{9,1},{10... | collective-permute-start | bytes 122888 | tf_op jit(solution)/shard_map/ppermute | solution.py:149
  28.6 5.3 %collective-permute-start.9 = (bf16[16,1280]{1,0:T(8,128)(2,1)S(1)}, bf16[16,1280]{1,0:T(8,128)(2,1)S(1)}, u32[]{:S(2)}, u32[]{:S(2)}) collective-permute-start(bf16[16,1280]{1,0:T(8,128)(2,1)S(1)} %get-tuple-element.34), channel_id=1, source_target_pairs={{0,2},{1,10},{2,0},{3,8},{4,6},{5,14},{6,4},{7,12},{8,11},{9,3},{1... | collective-permute-start | bytes 122888 | tf_op jit(solution)/shard_map/ppermute | solution.py:149
  37.3 7.0 %collective-permute-start.12 = (bf16[16,4096]{1,0:T(8,128)(2,1)S(1)}, bf16[16,4096]{1,0:T(8,128)(2,1)S(1)}, u32[]{:S(2)}, u32[]{:S(2)}) collective-permute-start(bf16[16,4096]{1,0:T(8,128)(2,1)S(1)} %shard_map.106.refs_0_), channel_id=1, source_target_pairs={{0,4},{1,9},{2,6},{3,11},{4,0},{5,13},{6,2},{7,15},{8,12},{9,1},{1... | collective-permute-start | bytes 393224 | tf_op jit(solution)/shard_map/ppermute | solution.py:122
  38.4 12.3 %collective-permute-start.13 = (bf16[16,4096]{1,0:T(8,128)(2,1)S(1)}, bf16[16,4096]{1,0:T(8,128)(2,1)S(1)}, u32[]{:S(2)}, u32[]{:S(2)}) collective-permute-start(bf16[16,4096]{1,0:T(8,128)(2,1)S(1)} %shard_map.106.refs_0_), channel_id=1, source_target_pairs={{0,8},{1,3},{2,10},{3,1},{4,12},{5,7},{6,14},{7,5},{8,0},{9,11},{1... | collective-permute-start | bytes 393224 | tf_op jit(solution)/shard_map/ppermute | solution.py:122
  44.3 8.9 %collective-permute-start.15 = (bf16[16,4096]{1,0:T(8,128)(2,1)S(1)}, bf16[16,4096]{1,0:T(8,128)(2,1)S(1)}, u32[]{:S(2)}, u32[]{:S(2)}) collective-permute-start(bf16[16,4096]{1,0:T(8,128)(2,1)S(1)} %collective-permute-done.12.refs_1_), channel_id=1, source_target_pairs={{0,8},{1,3},{2,10},{3,1},{4,12},{5,7},{6,14},{7,5},{8,0},{9,11},{1... | collective-permute-start | bytes 393224 | tf_op jit(solution)/shard_map/ppermute | solution.py:122
  48.5 9.7 %collective-permute-start.14 = (bf16[16,4096]{1,0:T(8,128)(2,1)S(1)}, bf16[16,4096]{1,0:T(8,128)(2,1)S(1)}, u32[]{:S(2)}, u32[]{:S(2)}) collective-permute-start(bf16[16,4096]{1,0:T(8,128)(2,1)S(1)} %shard_map.106.refs_0_), channel_id=1, source_target_pairs={{0,2},{1,5},{2,0},{3,7},{4,6},{5,1},{6,4},{7,3},{8,10},{9,13},{10,... | collective-permute-start | bytes 393224 | tf_op jit(solution)/shard_map/ppermute | solution.py:122
  50.6 7.6 %collective-permute-start.16 = (bf16[16,4096]{1,0:T(8,128)(2,1)S(1)}, bf16[16,4096]{1,0:T(8,128)(2,1)S(1)}, u32[]{:S(2)}, u32[]{:S(2)}) collective-permute-start(bf16[16,4096]{1,0:T(8,128)(2,1)S(1)} %collective-permute-done.12.refs_1_), channel_id=1, source_target_pairs={{0,2},{1,5},{2,0},{3,7},{4,6},{5,1},{6,4},{7,3},{8,10},{9,13},{10,... | collective-permute-start | bytes 393224 | tf_op jit(solution)/shard_map/ppermute | solution.py:122
  50.7 7.5 %collective-permute-start.17 = (bf16[16,4096]{1,0:T(8,128)(2,1)S(1)}, bf16[16,4096]{1,0:T(8,128)(2,1)S(1)}, u32[]{:S(2)}, u32[]{:S(2)}) collective-permute-start(bf16[16,4096]{1,0:T(8,128)(2,1)S(1)} %collective-permute-done.13.refs_2_), channel_id=1, source_target_pairs={{0,2},{1,5},{2,0},{3,7},{4,6},{5,1},{6,4},{7,3},{8,10},{9,13},{10,... | collective-permute-start | bytes 393224 | tf_op jit(solution)/shard_map/ppermute | solution.py:122
  53.2 5.2 %collective-permute-start.18 = (bf16[16,4096]{1,0:T(8,128)(2,1)S(1)}, bf16[16,4096]{1,0:T(8,128)(2,1)S(1)}, u32[]{:S(2)}, u32[]{:S(2)}) collective-permute-start(bf16[16,4096]{1,0:T(8,128)(2,1)S(1)} %collective-permute-done.15.refs_4_), channel_id=1, source_target_pairs={{0,2},{1,5},{2,0},{3,7},{4,6},{5,1},{6,4},{7,3},{8,10},{9,13},{10,... | collective-permute-start | bytes 393224 | tf_op jit(solution)/shard_map/ppermute | solution.py:122
  59.7 1.8 %collective-permute-start.19 = (f32[64,1024]{1,0:T(8,128)S(1)}, f32[64,1024]{1,0:T(8,128)S(1)}, u32[]{:S(2)}, u32[]{:S(2)}) collective-permute-start(f32[64,1024]{1,0:T(8,128)S(1)} %get-tuple-element.42), channel_id=1, source_target_pairs={{0,1},{1,0},{2,3},{3,2},{4,5},{5,4},{6,7},{7,6},{8,9},{9,8},{10,11... | collective-permute-start | bytes 786440 | tf_op jit(solution)/shard_map/ppermute | solution.py:138
  61.5 4.2 %collective-permute-start.20 = (bf16[16,1024]{1,0:T(8,128)(2,1)S(1)}, bf16[16,1024]{1,0:T(8,128)(2,1)S(1)}, u32[]{:S(2)}, u32[]{:S(2)}) collective-permute-start(bf16[16,1024]{1,0:T(8,128)(2,1)S(1)} %get-tuple-element.43), channel_id=1, source_target_pairs={{0,0},{1,8},{2,2},{3,10},{4,4},{5,12},{6,6},{7,14},{8,9},{9,1},{10... | collective-permute-start | bytes 98312 | tf_op jit(solution)/shard_map/ppermute | solution.py:149
  62.2 4.0 %collective-permute-start.21 = (bf16[16,1024]{1,0:T(8,128)(2,1)S(1)}, bf16[16,1024]{1,0:T(8,128)(2,1)S(1)}, u32[]{:S(2)}, u32[]{:S(2)}) collective-permute-start(bf16[16,1024]{1,0:T(8,128)(2,1)S(1)} %get-tuple-element.44), channel_id=1, source_target_pairs={{0,2},{1,10},{2,0},{3,8},{4,6},{5,14},{6,4},{7,12},{8,11},{9,3},{1... | collective-permute-start | bytes 98312 | tf_op jit(solution)/shard_map/ppermute | solution.py:149
  63.4 3.9 %collective-permute-start.22 = (bf16[16,1024]{1,0:T(8,128)(2,1)S(1)}, bf16[16,1024]{1,0:T(8,128)(2,1)S(1)}, u32[]{:S(2)}, u32[]{:S(2)}) collective-permute-start(bf16[16,1024]{1,0:T(8,128)(2,1)S(1)} %get-tuple-element.45), channel_id=1, source_target_pairs={{0,4},{1,12},{2,6},{3,14},{4,0},{5,8},{6,2},{7,10},{8,13},{9,5},{1... | collective-permute-start | bytes 98312 | tf_op jit(solution)/shard_map/ppermute | solution.py:149
  64.4 4.8 %collective-permute-start.23 = (bf16[16,1024]{1,0:T(8,128)(2,1)S(1)}, bf16[16,1024]{1,0:T(8,128)(2,1)S(1)}, u32[]{:S(2)}, u32[]{:S(2)}) collective-permute-start(bf16[16,1024]{1,0:T(8,128)(2,1)S(1)} %get-tuple-element.46), channel_id=1, source_target_pairs={{0,6},{1,14},{2,4},{3,12},{4,2},{5,10},{6,0},{7,8},{8,15},{9,7},{1... | collective-permute-start | bytes 98312 | tf_op jit(solution)/shard_map/ppermute | solution.py:149
  69.2 5.2 %collective-permute-start.24 = (bf16[4,16,1024]{2,1,0:T(8,128)(2,1)S(1)}, bf16[4,16,1024]{2,1,0:T(8,128)(2,1)S(1)}, u32[]{:S(2)}, u32[]{:S(2)}) collective-permute-start(bf16[4,16,1024]{2,1,0:T(8,128)(2,1)S(1)} %pad_maximum_fusion.own_ref), channel_id=1, source_target_pairs={{0,1},{1,0},{2,3},{3,2},{4,5},{5,4},{6,7},{7,6},{8,9},{9,8},{10,11... | collective-permute-start | bytes 393224 | tf_op jit(solution)/shard_map/ppermute | solution.py:138

commit v5 on v4

--- a/solution.py
+++ b/solution.py
@@ -1,3 +1,4 @@
+import functools
 import math
 
 import jax
@@ -122,15 +123,16 @@
     return lax.ppermute(block, ("out", "inp"), pairs)
 
 
-def gather_blocks(block, mark):
+def gather_blocks(block, early, late):
     a = exchange(block, 0)
     b = exchange(block, 1)
     c = exchange(block, 2)
-    c = after(c, mark)
+    a = a if early is None else after(a, early)
     bc = exchange(b, 2)
     ab = exchange(a, 1)
     ac = exchange(a, 2)
     abc = exchange(ab, 2)
+    ac = ac if late is None else after(ac, late)
     return block, a, b, c, ab, ac, bc, abc
 
 
@@ -196,16 +198,16 @@
     out_ref[:, half:] = tag.astype(jnp.float32).astype(jnp.bfloat16)
 
 
-def fetch_kernel(*refs):
+def fetch_kernel(starts, *refs):
     count = (len(refs) - 2) // 2
     mark_ref, arrivals = refs[-2:]
     copies = []
     for n in range(count):
         source, target = refs[n], refs[count + n]
-        size = source.shape[0] // 4
+        size = target.shape[0] // 4
         for part in range(4):
-            here = pl.ds(part * size, size)
-            copies.append(pltpu.make_async_copy(source.at[here], target.at[here], arrivals.at[n, part]))
+            there, here = pl.ds(starts[n] + part * size, size), pl.ds(part * size, size)
+            copies.append(pltpu.make_async_copy(source.at[there], target.at[here], arrivals.at[n, part]))
     for copy in copies:
         copy.start()
     mark_ref[...] = jnp.zeros_like(mark_ref)
@@ -220,21 +222,20 @@
 ANYWHERE = pl.BlockSpec(memory_space=pl.ANY)
 
 
-def fetched(*arrays):
+def fetched(*parts):
+    shapes = [(rows,) + array.shape[1:] for array, _, rows in parts]
     *near, mark = pl.pallas_call(
-        fetch_kernel,
-        out_shape=[pltpu.VMEM(array.shape, array.dtype) for array in arrays]
+        functools.partial(fetch_kernel, [start for _, start, _ in parts]),
+        out_shape=[pltpu.VMEM(shape, part[0].dtype) for shape, part in zip(shapes, parts)]
         + [jax.ShapeDtypeStruct((8, 128), jnp.float32)],
-        in_specs=[ANYWHERE] * len(arrays),
-        out_specs=[VMEM_SPEC] * (len(arrays) + 1),
-        scratch_shapes=[pltpu.SemaphoreType.DMA((len(arrays), 4))],
+        in_specs=[ANYWHERE] * len(parts),
+        out_specs=[VMEM_SPEC] * (len(parts) + 1),
+        scratch_shapes=[pltpu.SemaphoreType.DMA((len(parts), 4))],
         compiler_params=pltpu.CompilerParams(vmem_limit_bytes=MEGABYTE),
         cost_estimate=pl.CostEstimate(
-            flops=0,
-            bytes_accessed=sum(array.size * array.dtype.itemsize for array in arrays),
-            transcendentals=0,
+            flops=0, bytes_accessed=sum(2 * math.prod(shape) for shape in shapes), transcendentals=0
         ),
-    )(*map(distant, arrays))
+    )(*[distant(array) for array, _, _ in parts])
     return near, mark
 
 
@@ -261,28 +262,40 @@
         rows_ref[pl.ds(pl.multiple_of(offset * rows, rows), rows), :] = piece[...]
 
 
+def multiply(rows_ref, weights, at, block):
+    total, first = 0.0, 0
+    for weight in weights:
+        depth = weight.shape[0]
+        total += jnp.dot(
+            rows_ref[:, first : first + depth], weight[:, at : at + block], preferred_element_type=jnp.float32
+        )
+        first += depth
+    return total
+
+
 def project_kernel(*refs):
-    pieces, (query_ref, key_ref, value_ref, given_ref, kept_ref, tag_ref, rows_ref) = refs[:8], refs[8:]
+    pieces, key_ref, value_ref, queries = refs[:8], refs[8], refs[9], refs[10:-4]
+    given_ref, kept_ref, tag_ref, rows_ref = refs[-4:]
     stack_rows(pieces, rows_ref)
-    count, depth = given_ref.shape[0], query_ref.shape[0]
+    count, depth = given_ref.shape[0], key_ref.shape[0]
     tag_ref[...] = rows_ref[count:, depth:].astype(jnp.float32)
     first = 0
-    for weight_ref in (query_ref, key_ref, value_ref):
-        width = weight_ref.shape[1]
+    for weights in (queries, (key_ref,), (value_ref,)):
+        width = weights[0].shape[1]
         block = min(256, width)
         for at in range(0, width, block):
-            sums = jnp.dot(rows_ref[:, :depth], weight_ref[:, at : at + block], preferred_element_type=jnp.float32)
+            sums = multiply(rows_ref, weights, at, block)
             given_ref[:, first + at : first + at + block] = sums[:count]
             kept_ref[:, first + at : first + at + block] = sums[count:]
         first += width
 
 
 def mix_kernel(*refs):
-    pieces, (weight_ref, given_ref, kept_ref, rows_ref) = refs[:8], refs[8:]
+    pieces, weights, (given_ref, kept_ref, rows_ref) = refs[:8], refs[8:-3], refs[-3:]
     stack_rows(pieces, rows_ref)
     count = given_ref.shape[0]
-    for at in range(0, weight_ref.shape[1], 256):
-        sums = jnp.dot(rows_ref[...], weight_ref[:, at : at + 256], preferred_element_type=jnp.float32)
+    for at in range(0, weights[0].shape[1], 256):
+        sums = multiply(rows_ref, weights, at, 256)
         given_ref[:, at : at + 256] = sums[:count]
         kept_ref[:, at : at + 256] = sums[count:]
 
@@ -451,19 +464,22 @@
         ],
         place=pl.BlockSpec(memory_space=pltpu.HBM),
     )
-    (near_query, near_key, near_value), weight_mark = fetched(query_weight, key_matrix, value_matrix)
+    depth = query_weight.shape[0]
+    (query_first, near_key, near_value,), early = fetched((query_weight, 0, depth * 2048 // 4096), (key_matrix, 0, depth), (value_matrix, 0, depth))
+    (query_second,), late = fetched((query_weight, depth * 2048 // 4096, depth - depth * 2048 // 4096))
     (near_keys, near_values), cache_mark = fetched(
-        cache_keys.reshape(rows, -1, HEAD_SIZE), cache_values.reshape(rows, -1, HEAD_SIZE)
-    )
-    blocks = gather_blocks(own, weight_mark)
+        (cache_keys.reshape(rows, -1, HEAD_SIZE), 0, rows), (cache_values.reshape(rows, -1, HEAD_SIZE), 0, rows)
+    )
+    blocks = gather_blocks(own, early, late)
     given, kept, tags = on_chip(
         project_kernel,
         [shape((4 * count, qkv_cols), jnp.float32)] * 2 + [shape((4 * count, 128), jnp.float32)],
         (),
         *blocks,
-        resident(near_query),
         resident(near_key),
         resident(near_value),
+        resident(query_first),
+        resident(query_second),
         scratch=[pltpu.VMEM((8 * count, half + 128), jnp.bfloat16)],
     )
     arrived = swap_cores(given)
@@ -483,15 +499,17 @@
         jnp.concatenate([-sine, sine], axis=-1),
     )
     attended = attend(hand_out(outgoing), near_keys, near_values, lengths)
-    (near_output,), output_mark = fetched(output_weight)
-    blocks = gather_blocks(attended, output_mark)
+    (output_first,), early = fetched((output_weight, 0, depth * 2048 // 4096))
+    (output_second,), late = fetched((output_weight, depth * 2048 // 4096, depth - depth * 2048 // 4096))
+    blocks = gather_blocks(attended, early, late)
     mix_cols = output_weight.shape[1]
     given, kept = on_chip(
         mix_kernel,
         [shape((4 * count, mix_cols), jnp.float32)] * 2,
         (),
         *blocks,
-        resident(near_output),
+        resident(output_first),
+        resident(output_second),
         scratch=[pltpu.VMEM((8 * count, half), jnp.bfloat16)],
     )
     outgoing = on_chip(

time: 75.3 us -> 74.7 us (level)
  starting transfers between devices: 44.8 us -> 34.7 us
  waiting for transfers between devices: 9.4 us -> 16.9 us
  Pallas kernels: 20.2 us -> 22.2 us
    ppermute x14, starting transfers between devices: 31.4 us -> 22.6 us  [exchange(): return lax.ppermute(block, ('out', 'inp'), pairs)]
    ppermute x14, waiting for transfers between devices: 2.43 us -> 9.7 us  [exchange(): return lax.ppermute(block, ('out', 'inp'), pairs)]
    pallas_call x3 -> x5, Pallas kernels: 11.6 us -> 13.5 us  [fetched(): pl.pallas_call(functools.partial(fetch_kernel, [start for _, start, _ in...]
    ppermute x3, starting transfers between devices: 4.94 us -> 3.7 us  [swap_cores(): return lax.ppermute(block, 'inp', [(0, 1), (1, 0)])]
  transfers between devices with their start and end apart: 25 -> 25, of which waited for: 10 -> 12; matrix products, arithmetic and copies ran while one was open for 0% -> 0% of each run, Pallas kernels for 15% -> 18%
where the time goes in v5:
time: 74.7 us; the launch traced here: 74.5 us
  starting transfers between devices  34.7 us (46%)
  Pallas kernels  22.2 us (30%)
  waiting for transfers between devices  16.9 us (23%)
    ppermute x14, starting transfers between devices, exchange(): return lax.ppermute(block, ('out', 'inp'), pairs)  22.6 us
    pallas_call x5, Pallas kernels, fetched(): pl.pallas_call(functools.partial(fetch_kernel, [start for _, start, _ in...  13.5 us
    ppermute x14, waiting for transfers between devices, exchange(): return lax.ppermute(block, ('out', 'inp'), pairs)  9.7 us
    ppermute x8, starting transfers between devices, hand_out(): received.append(lax.ppermute(block, ('out', 'inp'), pairs))  8.44 us
    pallas_call x6, Pallas kernels, on_chip(): pl.pallas_call(kernel, out_shape=out_shape, in_specs=[SMEM_SPEC] * len(sc...  5.29 us
    ppermute x3, waiting for transfers between devices, swap_cores(): return lax.ppermute(block, 'inp', [(0, 1), (1, 0)])  3.83 us
    ppermute x3, starting transfers between devices, swap_cores(): return lax.ppermute(block, 'inp', [(0, 1), (1, 0)])  3.7 us
    ppermute x8, waiting for transfers between devices, hand_out(): received.append(lax.ppermute(block, ('out', 'inp'), pairs))  3.36 us
  transfers between devices with their start and end apart: 25, of which 12 were waited for; matrix products, arithmetic and copies ran while one was open for 0% of the time, Pallas kernels for 18%

profile of v5, /device:TPU:0, one launch (start us, length us, event | category | flops | bytes accessed | tf_op | source)
XLA Modules:
  0.0 74.5 jit_solution(13000965830449960700)
XLA Ops:
  0.0 1.2 %shard_map.100.refs_0_ = bf16[16,4224]{1,0:T(8,128)(2,1)S(1)} custom-call(s32[8]{0:T(128)} %position_hbm.1, bf16[16,8192]{1,0:T(8,128)(2,1)} %bitcast.11, f32[1,8192]{1,0:T(1,128)} %bitcast.12), custom_call_target="tpu_custom_call" | custom-call | bytes 1048576 | tf_op jit(solution)/shard_map/pallas_call | solution.py:165
  1.2 3.1 %collective-permute-start = (bf16[16,4224]{1,0:T(8,128)(2,1)S(1)}, bf16[16,4224]{1,0:T(8,128)(2,1)S(1)}, u32[]{:S(2)}, u32[]{:S(2)}) collective-permute-start(bf16[16,4224]{1,0:T(8,128)(2,1)S(1)} %shard_map.100.refs_0_), channel_id=1, source_target_pairs={{0,4},{1,9},{2,6},{3,11},{4,0},{5,13},{6,2},{7,15},{8,12},{9,1},{1... | collective-permute-start | bytes 405512 | tf_op jit(solution)/shard_map/ppermute | solution.py:123
  4.3 2.6 %collective-permute-start.1 = (bf16[16,4224]{1,0:T(8,128)(2,1)S(1)}, bf16[16,4224]{1,0:T(8,128)(2,1)S(1)}, u32[]{:S(2)}, u32[]{:S(2)}) collective-permute-start(bf16[16,4224]{1,0:T(8,128)(2,1)S(1)} %shard_map.100.refs_0_), channel_id=1, source_target_pairs={{0,8},{1,3},{2,10},{3,1},{4,12},{5,7},{6,14},{7,5},{8,0},{9,11},{1... | collective-permute-start | bytes 405512 | tf_op jit(solution)/shard_map/ppermute | solution.py:123
  6.9 2.9 %shard_map.101 = (bf16[2048,1024]{1,0:T(8,128)(2,1)S(1)}, bf16[4096,128]{1,0:T(8,128)(2,1)S(1)}, bf16[4096,128]{1,0:T(8,128)(2,1)S(1)}, f32[8,128]{1,0:T(8,128)S(1)}) custom-call(bf16[4096,1024]{1,0:T(8,128)(2,1)} %refs_0_.5, bf16[4096,128]{1,0:T(8,128)(2,1)} %refs_1_.1, bf16[4096,128]{1,0:T(8,128)(2,1)} %refs_2_.1), custom_call_target="tpu_custom_call" | custom-call | bytes 6291456 | tf_op jit(solution)/shard_map/pallas_call | solution.py:227
  9.8 0.0 collective-permute-done.refs_0_
  9.8 0.9 %collective-permute-start.3 = (bf16[16,4224]{1,0:T(8,128)(2,1)S(1)}, bf16[16,4224]{1,0:T(8,128)(2,1)S(1)}, u32[]{:S(2)}, u32[]{:S(2)}) collective-permute-start(bf16[16,4224]{1,0:T(8,128)(2,1)S(1)} %shard_map.102.refs_1_), channel_id=1, source_target_pairs={{0,8},{1,3},{2,10},{3,1},{4,12},{5,7},{6,14},{7,5},{8,0},{9,11},{1... | collective-permute-start | bytes 405512 | tf_op jit(solution)/shard_map/ppermute | solution.py:123
  10.7 1.5 %collective-permute-start.4 = (bf16[16,4224]{1,0:T(8,128)(2,1)S(1)}, bf16[16,4224]{1,0:T(8,128)(2,1)S(1)}, u32[]{:S(2)}, u32[]{:S(2)}) collective-permute-start(bf16[16,4224]{1,0:T(8,128)(2,1)S(1)} %shard_map.102.refs_1_), channel_id=1, source_target_pairs={{0,2},{1,5},{2,0},{3,7},{4,6},{5,1},{6,4},{7,3},{8,10},{9,13},{10,... | collective-permute-start | bytes 405512 | tf_op jit(solution)/shard_map/ppermute | solution.py:123
  12.2 0.5 collective-permute-start.2
  12.7 0.0 collective-permute-done.1.refs_2_
  12.7 1.5 %collective-permute-start.5 = (bf16[16,4224]{1,0:T(8,128)(2,1)S(1)}, bf16[16,4224]{1,0:T(8,128)(2,1)S(1)}, u32[]{:S(2)}, u32[]{:S(2)}) collective-permute-start(bf16[16,4224]{1,0:T(8,128)(2,1)S(1)} %collective-permute-done.1.refs_2_), channel_id=1, source_target_pairs={{0,2},{1,5},{2,0},{3,7},{4,6},{5,1},{6,4},{7,3},{8,10},{9,13},{10,... | collective-permute-start | bytes 405512 | tf_op jit(solution)/shard_map/ppermute | solution.py:123
  14.3 3.1 %collective-permute-done.3.refs_4_ = bf16[16,4224]{1,0:T(8,128)(2,1)S(1)} collective-permute-done((bf16[16,4224]{1,0:T(8,128)(2,1)S(1)}, bf16[16,4224]{1,0:T(8,128)(2,1)S(1)}, u32[]{:S(2)}, u32[]{:S(2)}) %collective-permute-start.3) | collective-permute-done | bytes 135200 | tf_op jit(solution)/shard_map/ppermute | solution.py:123
  17.3 1.5 %collective-permute-start.6 = (bf16[16,4224]{1,0:T(8,128)(2,1)S(1)}, bf16[16,4224]{1,0:T(8,128)(2,1)S(1)}, u32[]{:S(2)}, u32[]{:S(2)}) collective-permute-start(bf16[16,4224]{1,0:T(8,128)(2,1)S(1)} %collective-permute-done.3.refs_4_), channel_id=1, source_target_pairs={{0,2},{1,5},{2,0},{3,7},{4,6},{5,1},{6,4},{7,3},{8,10},{9,13},{10,... | collective-permute-start | bytes 405512 | tf_op jit(solution)/shard_map/ppermute | solution.py:123
  18.9 2.2 %shard_map.103 = (bf16[2048,1024]{1,0:T(8,128)(2,1)S(1)}, f32[8,128]{1,0:T(8,128)S(1)}) custom-call(bf16[4096,1024]{1,0:T(8,128)(2,1)} %refs_0_.5), custom_call_target="tpu_custom_call" | custom-call | bytes 4194304 | tf_op jit(solution)/shard_map/pallas_call | solution.py:227
  21.1 0.0 collective-permute-done.4.refs_0_
  21.1 0.0 collective-permute-done.2.refs_3_
  21.1 0.0 collective-permute-done.5.refs_6_
  21.1 1.2 %collective-permute-done.6.refs_7_ = bf16[16,4224]{1,0:T(8,128)(2,1)S(1)} collective-permute-done((bf16[16,4224]{1,0:T(8,128)(2,1)S(1)}, bf16[16,4224]{1,0:T(8,128)(2,1)S(1)}, u32[]{:S(2)}, u32[]{:S(2)}) %collective-permute-start.6) | collective-permute-done | bytes 135200 | tf_op jit(solution)/shard_map/ppermute | solution.py:123
  22.3 1.9 %shard_map.105 = (f32[64,1280]{1,0:T(8,128)S(1)}, f32[64,1280]{1,0:T(8,128)S(1)}, f32[64,128]{1,0:T(8,128)S(1)}) custom-call(bf16[16,4224]{1,0:T(8,128)(2,1)S(1)} %shard_map.100.refs_0_, bf16[16,4224]{1,0:T(8,128)(2,1)S(1)} %shard_map.102.refs_1_, bf16[16,4224]{1,0:T(8,128)(2,1)S(1)} %collective-permute-done.1.refs_2_, ...), custom_call_target="tpu_custom_call" | custom-call | bytes 1048576 | tf_op jit(solution)/shard_map/pallas_call | solution.py:165
  24.3 0.2 fusion.3
  24.4 0.1 collective-permute-start.7
  24.5 0.2 fusion.7
  24.7 0.1 pad_maximum_fusion.1
  24.8 1.3 %collective-permute-done.7.arrived_ref = f32[64,1280]{1,0:T(8,128)S(1)} collective-permute-done((f32[64,1280]{1,0:T(8,128)S(1)}, f32[64,1280]{1,0:T(8,128)S(1)}, u32[]{:S(2)}, u32[]{:S(2)}) %collective-permute-start.7) | collective-permute-done | bytes 327712 | tf_op jit(solution)/shard_map/ppermute | solution.py:140
  26.1 0.2 shard_map.106
  26.3 0.4 collective-permute-start.10
  26.7 2.6 %collective-permute-start.11 = (bf16[16,1280]{1,0:T(8,128)(2,1)S(1)}, bf16[16,1280]{1,0:T(8,128)(2,1)S(1)}, u32[]{:S(2)}, u32[]{:S(2)}) collective-permute-start(bf16[16,1280]{1,0:T(8,128)(2,1)S(1)} %get-tuple-element.42), channel_id=1, source_target_pairs={{0,6},{1,14},{2,4},{3,12},{4,2},{5,10},{6,0},{7,8},{8,15},{9,7},{1... | collective-permute-start | bytes 122888 | tf_op jit(solution)/shard_map/ppermute | solution.py:151
  29.3 0.7 collective-permute-start.8
  30.0 0.6 collective-permute-start.9
  30.5 4.1 %shard_map.107 = (bf16[8,2048,128]{2,1,0:T(8,128)(2,1)S(1)}, bf16[8,2048,128]{2,1,0:T(8,128)(2,1)S(1)}, f32[8,128]{1,0:T(8,128)}) custom-call(bf16[8,2048,128]{2,1,0:T(8,128)(2,1)} %bitcast.9, bf16[8,2048,128]{2,1,0:T(8,128)(2,1)} %bitcast.10), custom_call_target="tpu_custom_call" | custom-call | bytes 8388608 | tf_op jit(solution)/shard_map/pallas_call | solution.py:227
  34.6 0.0 collective-permute-done.10.refs_2_
  34.6 0.0 collective-permute-done.11.refs_3_
  34.6 0.0 collective-permute-done.8.refs_0_
  34.7 0.0 collective-permute-done.9.refs_1_
  34.7 3.3 %shard_map.108.refs_0_ = bf16[16,4096]{1,0:T(8,128)(2,1)S(1)} custom-call(s32[8]{0:T(128)S(1)} %copy-done, bf16[16,1280]{1,0:T(8,128)(2,1)S(1)} %collective-permute-done.8.refs_0_, bf16[16,1280]{1,0:T(8,128)(2,1)S(1)} %collective-permute-done.9.refs_1_, bf16[16,1280]{1,0:T(8,128)(2,1)S(1)} %collective-permute-done.10.refs_2_, ...), custom_call_target="tpu_custom_call" | custom-call | bytes 12582912 | tf_op jit(solution)/shard_map/pallas_call | solution.py:422
  38.0 0.4 collective-permute-start.12
  38.4 2.2 %shard_map.109 = (bf16[2048,1024]{1,0:T(8,128)(2,1)S(1)}, f32[8,128]{1,0:T(8,128)S(1)}) custom-call(bf16[4096,1024]{1,0:T(8,128)(2,1)} %refs_0_.7), custom_call_target="tpu_custom_call" | custom-call | bytes 4194304 | tf_op jit(solution)/shard_map/pallas_call | solution.py:227
  40.6 5.9 %collective-permute-start.13 = (bf16[16,4096]{1,0:T(8,128)(2,1)S(1)}, bf16[16,4096]{1,0:T(8,128)(2,1)S(1)}, u32[]{:S(2)}, u32[]{:S(2)}) collective-permute-start(bf16[16,4096]{1,0:T(8,128)(2,1)S(1)} %shard_map.108.refs_0_), channel_id=1, source_target_pairs={{0,8},{1,3},{2,10},{3,1},{4,12},{5,7},{6,14},{7,5},{8,0},{9,11},{1... | collective-permute-start | bytes 393224 | tf_op jit(solution)/shard_map/ppermute | solution.py:123
  46.6 0.0 collective-permute-done.12.refs_0_
  46.6 1.5 %collective-permute-start.15 = (bf16[16,4096]{1,0:T(8,128)(2,1)S(1)}, bf16[16,4096]{1,0:T(8,128)(2,1)S(1)}, u32[]{:S(2)}, u32[]{:S(2)}) collective-permute-start(bf16[16,4096]{1,0:T(8,128)(2,1)S(1)} %shard_map.110.refs_1_), channel_id=1, source_target_pairs={{0,8},{1,3},{2,10},{3,1},{4,12},{5,7},{6,14},{7,5},{8,0},{9,11},{1... | collective-permute-start | bytes 393224 | tf_op jit(solution)/shard_map/ppermute | solution.py:123
  48.1 0.5 collective-permute-start.16
  48.7 1.5 %collective-permute-start.14 = (bf16[16,4096]{1,0:T(8,128)(2,1)S(1)}, bf16[16,4096]{1,0:T(8,128)(2,1)S(1)}, u32[]{:S(2)}, u32[]{:S(2)}) collective-permute-start(bf16[16,4096]{1,0:T(8,128)(2,1)S(1)} %shard_map.108.refs_0_), channel_id=1, source_target_pairs={{0,2},{1,5},{2,0},{3,7},{4,6},{5,1},{6,4},{7,3},{8,10},{9,13},{10,... | collective-permute-start | bytes 393224 | tf_op jit(solution)/shard_map/ppermute | solution.py:123
  50.1 2.0 %collective-permute-done.13.refs_2_ = bf16[16,4096]{1,0:T(8,128)(2,1)S(1)} collective-permute-done((bf16[16,4096]{1,0:T(8,128)(2,1)S(1)}, bf16[16,4096]{1,0:T(8,128)(2,1)S(1)}, u32[]{:S(2)}, u32[]{:S(2)}) %collective-permute-start.13) | collective-permute-done | bytes 131104 | tf_op jit(solution)/shard_map/ppermute | solution.py:123
  52.2 0.0 collective-permute-start.17
  52.2 1.6 %collective-permute-done.15.refs_4_ = bf16[16,4096]{1,0:T(8,128)(2,1)S(1)} collective-permute-done((bf16[16,4096]{1,0:T(8,128)(2,1)S(1)}, bf16[16,4096]{1,0:T(8,128)(2,1)S(1)}, u32[]{:S(2)}, u32[]{:S(2)}) %collective-permute-start.15) | collective-permute-done | bytes 131104 | tf_op jit(solution)/shard_map/ppermute | solution.py:123
  53.8 1.0 %collective-permute-start.18 = (bf16[16,4096]{1,0:T(8,128)(2,1)S(1)}, bf16[16,4096]{1,0:T(8,128)(2,1)S(1)}, u32[]{:S(2)}, u32[]{:S(2)}) collective-permute-start(bf16[16,4096]{1,0:T(8,128)(2,1)S(1)} %collective-permute-done.15.refs_4_), channel_id=1, source_target_pairs={{0,2},{1,5},{2,0},{3,7},{4,6},{5,1},{6,4},{7,3},{8,10},{9,13},{10,... | collective-permute-start | bytes 393224 | tf_op jit(solution)/shard_map/ppermute | solution.py:123
  54.8 2.2 %shard_map.111 = (bf16[2048,1024]{1,0:T(8,128)(2,1)S(1)}, f32[8,128]{1,0:T(8,128)S(1)}) custom-call(bf16[4096,1024]{1,0:T(8,128)(2,1)} %refs_0_.7), custom_call_target="tpu_custom_call" | custom-call | bytes 4194304 | tf_op jit(solution)/shard_map/pallas_call | solution.py:227
  57.0 0.0 collective-permute-done.16.refs_0_
  57.1 0.0 collective-permute-done.14.refs_3_
  57.1 0.1 collective-permute-done.17.refs_6_
  57.1 1.6 %collective-permute-done.18.refs_7_ = bf16[16,4096]{1,0:T(8,128)(2,1)S(1)} collective-permute-done((bf16[16,4096]{1,0:T(8,128)(2,1)S(1)}, bf16[16,4096]{1,0:T(8,128)(2,1)S(1)}, u32[]{:S(2)}, u32[]{:S(2)}) %collective-permute-start.18) | collective-permute-done | bytes 131104 | tf_op jit(solution)/shard_map/ppermute | solution.py:123
  58.8 1.3 %shard_map.113 = (f32[64,1024]{1,0:T(8,128)S(1)}, f32[64,1024]{1,0:T(8,128)S(1)}) custom-call(bf16[16,4096]{1,0:T(8,128)(2,1)S(1)} %shard_map.108.refs_0_, bf16[16,4096]{1,0:T(8,128)(2,1)S(1)} %shard_map.110.refs_1_, bf16[16,4096]{1,0:T(8,128)(2,1)S(1)} %collective-permute-done.13.refs_2_, bf16[16,4096]{1,0:T(8,128)(2,1)S(1)} %collective-permute-done.14.refs_3_, ...), custom_call_target="tpu_custom_call" | custom-call | bytes 1048576 | tf_op jit(solution)/shard_map/pallas_call | solution.py:165
  60.0 0.1 collective-permute-start.19
  60.1 1.5 %collective-permute-done.19.arrived_ref = f32[64,1024]{1,0:T(8,128)S(1)} collective-permute-done((f32[64,1024]{1,0:T(8,128)S(1)}, f32[64,1024]{1,0:T(8,128)S(1)}, u32[]{:S(2)}, u32[]{:S(2)}) %collective-permute-start.19) | collective-permute-done | bytes 262176 | tf_op jit(solution)/shard_map/ppermute | solution.py:140
  61.7 0.7 collective-permute-start.20
  62.3 1.1 %collective-permute-start.21 = (bf16[16,1024]{1,0:T(8,128)(2,1)S(1)}, bf16[16,1024]{1,0:T(8,128)(2,1)S(1)}, u32[]{:S(2)}, u32[]{:S(2)}) collective-permute-start(bf16[16,1024]{1,0:T(8,128)(2,1)S(1)} %get-tuple-element.52), channel_id=1, source_target_pairs={{0,2},{1,10},{2,0},{3,8},{4,6},{5,14},{6,4},{7,12},{8,11},{9,3},{1... | collective-permute-start | bytes 98312 | tf_op jit(solution)/shard_map/ppermute | solution.py:151
  63.4 0.6 collective-permute-start.22
  64.1 1.8 %collective-permute-start.23 = (bf16[16,1024]{1,0:T(8,128)(2,1)S(1)}, bf16[16,1024]{1,0:T(8,128)(2,1)S(1)}, u32[]{:S(2)}, u32[]{:S(2)}) collective-permute-start(bf16[16,1024]{1,0:T(8,128)(2,1)S(1)} %get-tuple-element.54), channel_id=1, source_target_pairs={{0,6},{1,14},{2,4},{3,12},{4,2},{5,10},{6,0},{7,8},{8,15},{9,7},{1... | collective-permute-start | bytes 98312 | tf_op jit(solution)/shard_map/ppermute | solution.py:151
  65.9 0.0 collective-permute-done.20
  65.9 0.4 collective-permute-done.21
  66.3 1.0 %collective-permute-done.22 = bf16[16,1024]{1,0:T(8,128)(2,1)S(1)} collective-permute-done((bf16[16,1024]{1,0:T(8,128)(2,1)S(1)}, bf16[16,1024]{1,0:T(8,128)(2,1)S(1)}, u32[]{:S(2)}, u32[]{:S(2)}) %collective-permute-start.22) | collective-permute-done | bytes 32800 | tf_op jit(solution)/shard_map/ppermute | solution.py:151
  67.3 1.9 %collective-permute-done.23 = bf16[16,1024]{1,0:T(8,128)(2,1)S(1)} collective-permute-done((bf16[16,1024]{1,0:T(8,128)(2,1)S(1)}, bf16[16,1024]{1,0:T(8,128)(2,1)S(1)}, u32[]{:S(2)}, u32[]{:S(2)}) %collective-permute-start.23) | collective-permute-done | bytes 32800 | tf_op jit(solution)/shard_map/ppermute | solution.py:151
  69.3 3.6 %collective-permute-start.24 = (bf16[4,16,1024]{2,1,0:T(8,128)(2,1)S(1)}, bf16[4,16,1024]{2,1,0:T(8,128)(2,1)S(1)}, u32[]{:S(2)}, u32[]{:S(2)}) collective-permute-start(bf16[4,16,1024]{2,1,0:T(8,128)(2,1)S(1)} %pad_maximum_fusion.own_ref), channel_id=1, source_target_pairs={{0,1},{1,0},{2,3},{3,2},{4,5},{5,4},{6,7},{7,6},{8,9},{9,8},{10,11... | collective-permute-start | bytes 393224 | tf_op jit(solution)/shard_map/ppermute | solution.py:140
  72.8 1.0 %collective-permute-done.24.other_ref = bf16[4,16,1024]{2,1,0:T(8,128)(2,1)S(1)} collective-permute-done((bf16[4,16,1024]{2,1,0:T(8,128)(2,1)S(1)}, bf16[4,16,1024]{2,1,0:T(8,128)(2,1)S(1)}, u32[]{:S(2)}, u32[]{:S(2)}) %collective-permute-start.24) | collective-permute-done | bytes 131104 | tf_op jit(solution)/shard_map/ppermute | solution.py:140
  73.8 0.7 shard_map.115
  (9 shorter events, 0.1 us)
Async XLA Ops:
  1.2 8.5 %collective-permute-start = (bf16[16,4224]{1,0:T(8,128)(2,1)S(1)}, bf16[16,4224]{1,0:T(8,128)(2,1)S(1)}, u32[]{:S(2)}, u32[]{:S(2)}) collective-permute-start(bf16[16,4224]{1,0:T(8,128)(2,1)S(1)} %shard_map.100.refs_0_), channel_id=1, source_target_pairs={{0,4},{1,9},{2,6},{3,11},{4,0},{5,13},{6,2},{7,15},{8,12},{9,1},{1... | collective-permute-start | bytes 405512 | tf_op jit(solution)/shard_map/ppermute | solution.py:123
  4.3 8.4 %collective-permute-start.1 = (bf16[16,4224]{1,0:T(8,128)(2,1)S(1)}, bf16[16,4224]{1,0:T(8,128)(2,1)S(1)}, u32[]{:S(2)}, u32[]{:S(2)}) collective-permute-start(bf16[16,4224]{1,0:T(8,128)(2,1)S(1)} %shard_map.100.refs_0_), channel_id=1, source_target_pairs={{0,8},{1,3},{2,10},{3,1},{4,12},{5,7},{6,14},{7,5},{8,0},{9,11},{1... | collective-permute-start | bytes 405512 | tf_op jit(solution)/shard_map/ppermute | solution.py:123
  9.8 7.5 %collective-permute-start.3 = (bf16[16,4224]{1,0:T(8,128)(2,1)S(1)}, bf16[16,4224]{1,0:T(8,128)(2,1)S(1)}, u32[]{:S(2)}, u32[]{:S(2)}) collective-permute-start(bf16[16,4224]{1,0:T(8,128)(2,1)S(1)} %shard_map.102.refs_1_), channel_id=1, source_target_pairs={{0,8},{1,3},{2,10},{3,1},{4,12},{5,7},{6,14},{7,5},{8,0},{9,11},{1... | collective-permute-start | bytes 405512 | tf_op jit(solution)/shard_map/ppermute | solution.py:123
  10.7 10.4 %collective-permute-start.4 = (bf16[16,4224]{1,0:T(8,128)(2,1)S(1)}, bf16[16,4224]{1,0:T(8,128)(2,1)S(1)}, u32[]{:S(2)}, u32[]{:S(2)}) collective-permute-start(bf16[16,4224]{1,0:T(8,128)(2,1)S(1)} %shard_map.102.refs_1_), channel_id=1, source_target_pairs={{0,2},{1,5},{2,0},{3,7},{4,6},{5,1},{6,4},{7,3},{8,10},{9,13},{10,... | collective-permute-start | bytes 405512 | tf_op jit(solution)/shard_map/ppermute | solution.py:123
  12.2 8.9 %collective-permute-start.2 = (bf16[16,4224]{1,0:T(8,128)(2,1)S(1)}, bf16[16,4224]{1,0:T(8,128)(2,1)S(1)}, u32[]{:S(2)}, u32[]{:S(2)}) collective-permute-start(bf16[16,4224]{1,0:T(8,128)(2,1)S(1)} %shard_map.100.refs_0_), channel_id=1, source_target_pairs={{0,2},{1,5},{2,0},{3,7},{4,6},{5,1},{6,4},{7,3},{8,10},{9,13},{10,... | collective-permute-start | bytes 405512 | tf_op jit(solution)/shard_map/ppermute | solution.py:123
  12.7 8.4 %collective-permute-start.5 = (bf16[16,4224]{1,0:T(8,128)(2,1)S(1)}, bf16[16,4224]{1,0:T(8,128)(2,1)S(1)}, u32[]{:S(2)}, u32[]{:S(2)}) collective-permute-start(bf16[16,4224]{1,0:T(8,128)(2,1)S(1)} %collective-permute-done.1.refs_2_), channel_id=1, source_target_pairs={{0,2},{1,5},{2,0},{3,7},{4,6},{5,1},{6,4},{7,3},{8,10},{9,13},{10,... | collective-permute-start | bytes 405512 | tf_op jit(solution)/shard_map/ppermute | solution.py:123
  17.3 5.0 %collective-permute-start.6 = (bf16[16,4224]{1,0:T(8,128)(2,1)S(1)}, bf16[16,4224]{1,0:T(8,128)(2,1)S(1)}, u32[]{:S(2)}, u32[]{:S(2)}) collective-permute-start(bf16[16,4224]{1,0:T(8,128)(2,1)S(1)} %collective-permute-done.3.refs_4_), channel_id=1, source_target_pairs={{0,2},{1,5},{2,0},{3,7},{4,6},{5,1},{6,4},{7,3},{8,10},{9,13},{10,... | collective-permute-start | bytes 405512 | tf_op jit(solution)/shard_map/ppermute | solution.py:123
  24.4 1.7 %collective-permute-start.7 = (f32[64,1280]{1,0:T(8,128)S(1)}, f32[64,1280]{1,0:T(8,128)S(1)}, u32[]{:S(2)}, u32[]{:S(2)}) collective-permute-start(f32[64,1280]{1,0:T(8,128)S(1)} %get-tuple-element.37), channel_id=1, source_target_pairs={{0,1},{1,0},{2,3},{3,2},{4,5},{5,4},{6,7},{7,6},{8,9},{9,8},{10,11... | collective-permute-start | bytes 983048 | tf_op jit(solution)/shard_map/ppermute | solution.py:140
  26.3 8.3 %collective-permute-start.10 = (bf16[16,1280]{1,0:T(8,128)(2,1)S(1)}, bf16[16,1280]{1,0:T(8,128)(2,1)S(1)}, u32[]{:S(2)}, u32[]{:S(2)}) collective-permute-start(bf16[16,1280]{1,0:T(8,128)(2,1)S(1)} %get-tuple-element.41), channel_id=1, source_target_pairs={{0,4},{1,12},{2,6},{3,14},{4,0},{5,8},{6,2},{7,10},{8,13},{9,5},{1... | collective-permute-start | bytes 122888 | tf_op jit(solution)/shard_map/ppermute | solution.py:151
  26.7 8.0 %collective-permute-start.11 = (bf16[16,1280]{1,0:T(8,128)(2,1)S(1)}, bf16[16,1280]{1,0:T(8,128)(2,1)S(1)}, u32[]{:S(2)}, u32[]{:S(2)}) collective-permute-start(bf16[16,1280]{1,0:T(8,128)(2,1)S(1)} %get-tuple-element.42), channel_id=1, source_target_pairs={{0,6},{1,14},{2,4},{3,12},{4,2},{5,10},{6,0},{7,8},{8,15},{9,7},{1... | collective-permute-start | bytes 122888 | tf_op jit(solution)/shard_map/ppermute | solution.py:151
  29.3 5.3 %collective-permute-start.8 = (bf16[16,1280]{1,0:T(8,128)(2,1)S(1)}, bf16[16,1280]{1,0:T(8,128)(2,1)S(1)}, u32[]{:S(2)}, u32[]{:S(2)}) collective-permute-start(bf16[16,1280]{1,0:T(8,128)(2,1)S(1)} %get-tuple-element.39), channel_id=1, source_target_pairs={{0,0},{1,8},{2,2},{3,10},{4,4},{5,12},{6,6},{7,14},{8,9},{9,1},{10... | collective-permute-start | bytes 122888 | tf_op jit(solution)/shard_map/ppermute | solution.py:151
  30.0 4.7 %collective-permute-start.9 = (bf16[16,1280]{1,0:T(8,128)(2,1)S(1)}, bf16[16,1280]{1,0:T(8,128)(2,1)S(1)}, u32[]{:S(2)}, u32[]{:S(2)}) collective-permute-start(bf16[16,1280]{1,0:T(8,128)(2,1)S(1)} %get-tuple-element.40), channel_id=1, source_target_pairs={{0,2},{1,10},{2,0},{3,8},{4,6},{5,14},{6,4},{7,12},{8,11},{9,3},{1... | collective-permute-start | bytes 122888 | tf_op jit(solution)/shard_map/ppermute | solution.py:151
  30.5 4.1 %copy-start = (s32[8]{0:T(128)S(1)}, s32[8]{0:T(128)}, u32[]{:S(2)}) copy-start(s32[8]{0:T(128)} %length_ref.1) | copy-start | bytes 100
  38.0 8.6 %collective-permute-start.12 = (bf16[16,4096]{1,0:T(8,128)(2,1)S(1)}, bf16[16,4096]{1,0:T(8,128)(2,1)S(1)}, u32[]{:S(2)}, u32[]{:S(2)}) collective-permute-start(bf16[16,4096]{1,0:T(8,128)(2,1)S(1)} %shard_map.108.refs_0_), channel_id=1, source_target_pairs={{0,4},{1,9},{2,6},{3,11},{4,0},{5,13},{6,2},{7,15},{8,12},{9,1},{1... | collective-permute-start | bytes 393224 | tf_op jit(solution)/shard_map/ppermute | solution.py:123
  40.6 11.5 %collective-permute-start.13 = (bf16[16,4096]{1,0:T(8,128)(2,1)S(1)}, bf16[16,4096]{1,0:T(8,128)(2,1)S(1)}, u32[]{:S(2)}, u32[]{:S(2)}) collective-permute-start(bf16[16,4096]{1,0:T(8,128)(2,1)S(1)} %shard_map.108.refs_0_), channel_id=1, source_target_pairs={{0,8},{1,3},{2,10},{3,1},{4,12},{5,7},{6,14},{7,5},{8,0},{9,11},{1... | collective-permute-start | bytes 393224 | tf_op jit(solution)/shard_map/ppermute | solution.py:123
  46.6 7.2 %collective-permute-start.15 = (bf16[16,4096]{1,0:T(8,128)(2,1)S(1)}, bf16[16,4096]{1,0:T(8,128)(2,1)S(1)}, u32[]{:S(2)}, u32[]{:S(2)}) collective-permute-start(bf16[16,4096]{1,0:T(8,128)(2,1)S(1)} %shard_map.110.refs_1_), channel_id=1, source_target_pairs={{0,8},{1,3},{2,10},{3,1},{4,12},{5,7},{6,14},{7,5},{8,0},{9,11},{1... | collective-permute-start | bytes 393224 | tf_op jit(solution)/shard_map/ppermute | solution.py:123
  48.1 8.9 %collective-permute-start.16 = (bf16[16,4096]{1,0:T(8,128)(2,1)S(1)}, bf16[16,4096]{1,0:T(8,128)(2,1)S(1)}, u32[]{:S(2)}, u32[]{:S(2)}) collective-permute-start(bf16[16,4096]{1,0:T(8,128)(2,1)S(1)} %shard_map.110.refs_1_), channel_id=1, source_target_pairs={{0,2},{1,5},{2,0},{3,7},{4,6},{5,1},{6,4},{7,3},{8,10},{9,13},{10,... | collective-permute-start | bytes 393224 | tf_op jit(solution)/shard_map/ppermute | solution.py:123
  48.7 8.4 %collective-permute-start.14 = (bf16[16,4096]{1,0:T(8,128)(2,1)S(1)}, bf16[16,4096]{1,0:T(8,128)(2,1)S(1)}, u32[]{:S(2)}, u32[]{:S(2)}) collective-permute-start(bf16[16,4096]{1,0:T(8,128)(2,1)S(1)} %shard_map.108.refs_0_), channel_id=1, source_target_pairs={{0,2},{1,5},{2,0},{3,7},{4,6},{5,1},{6,4},{7,3},{8,10},{9,13},{10,... | collective-permute-start | bytes 393224 | tf_op jit(solution)/shard_map/ppermute | solution.py:123
  52.2 5.0 %collective-permute-start.17 = (bf16[16,4096]{1,0:T(8,128)(2,1)S(1)}, bf16[16,4096]{1,0:T(8,128)(2,1)S(1)}, u32[]{:S(2)}, u32[]{:S(2)}) collective-permute-start(bf16[16,4096]{1,0:T(8,128)(2,1)S(1)} %collective-permute-done.13.refs_2_), channel_id=1, source_target_pairs={{0,2},{1,5},{2,0},{3,7},{4,6},{5,1},{6,4},{7,3},{8,10},{9,13},{10,... | collective-permute-start | bytes 393224 | tf_op jit(solution)/shard_map/ppermute | solution.py:123
  53.8 5.0 %collective-permute-start.18 = (bf16[16,4096]{1,0:T(8,128)(2,1)S(1)}, bf16[16,4096]{1,0:T(8,128)(2,1)S(1)}, u32[]{:S(2)}, u32[]{:S(2)}) collective-permute-start(bf16[16,4096]{1,0:T(8,128)(2,1)S(1)} %collective-permute-done.15.refs_4_), channel_id=1, source_target_pairs={{0,2},{1,5},{2,0},{3,7},{4,6},{5,1},{6,4},{7,3},{8,10},{9,13},{10,... | collective-permute-start | bytes 393224 | tf_op jit(solution)/shard_map/ppermute | solution.py:123
  60.0 1.6 %collective-permute-start.19 = (f32[64,1024]{1,0:T(8,128)S(1)}, f32[64,1024]{1,0:T(8,128)S(1)}, u32[]{:S(2)}, u32[]{:S(2)}) collective-permute-start(f32[64,1024]{1,0:T(8,128)S(1)} %get-tuple-element.50), channel_id=1, source_target_pairs={{0,1},{1,0},{2,3},{3,2},{4,5},{5,4},{6,7},{7,6},{8,9},{9,8},{10,11... | collective-permute-start | bytes 786440 | tf_op jit(solution)/shard_map/ppermute | solution.py:140
  61.7 4.2 %collective-permute-start.20 = (bf16[16,1024]{1,0:T(8,128)(2,1)S(1)}, bf16[16,1024]{1,0:T(8,128)(2,1)S(1)}, u32[]{:S(2)}, u32[]{:S(2)}) collective-permute-start(bf16[16,1024]{1,0:T(8,128)(2,1)S(1)} %get-tuple-element.51), channel_id=1, source_target_pairs={{0,0},{1,8},{2,2},{3,10},{4,4},{5,12},{6,6},{7,14},{8,9},{9,1},{10... | collective-permute-start | bytes 98312 | tf_op jit(solution)/shard_map/ppermute | solution.py:151
  62.3 4.0 %collective-permute-start.21 = (bf16[16,1024]{1,0:T(8,128)(2,1)S(1)}, bf16[16,1024]{1,0:T(8,128)(2,1)S(1)}, u32[]{:S(2)}, u32[]{:S(2)}) collective-permute-start(bf16[16,1024]{1,0:T(8,128)(2,1)S(1)} %get-tuple-element.52), channel_id=1, source_target_pairs={{0,2},{1,10},{2,0},{3,8},{4,6},{5,14},{6,4},{7,12},{8,11},{9,3},{1... | collective-permute-start | bytes 98312 | tf_op jit(solution)/shard_map/ppermute | solution.py:151
  63.4 3.9 %collective-permute-start.22 = (bf16[16,1024]{1,0:T(8,128)(2,1)S(1)}, bf16[16,1024]{1,0:T(8,128)(2,1)S(1)}, u32[]{:S(2)}, u32[]{:S(2)}) collective-permute-start(bf16[16,1024]{1,0:T(8,128)(2,1)S(1)} %get-tuple-element.53), channel_id=1, source_target_pairs={{0,4},{1,12},{2,6},{3,14},{4,0},{5,8},{6,2},{7,10},{8,13},{9,5},{1... | collective-permute-start | bytes 98312 | tf_op jit(solution)/shard_map/ppermute | solution.py:151
  64.1 5.2 %collective-permute-start.23 = (bf16[16,1024]{1,0:T(8,128)(2,1)S(1)}, bf16[16,1024]{1,0:T(8,128)(2,1)S(1)}, u32[]{:S(2)}, u32[]{:S(2)}) collective-permute-start(bf16[16,1024]{1,0:T(8,128)(2,1)S(1)} %get-tuple-element.54), channel_id=1, source_target_pairs={{0,6},{1,14},{2,4},{3,12},{4,2},{5,10},{6,0},{7,8},{8,15},{9,7},{1... | collective-permute-start | bytes 98312 | tf_op jit(solution)/shard_map/ppermute | solution.py:151
  69.3 4.5 %collective-permute-start.24 = (bf16[4,16,1024]{2,1,0:T(8,128)(2,1)S(1)}, bf16[4,16,1024]{2,1,0:T(8,128)(2,1)S(1)}, u32[]{:S(2)}, u32[]{:S(2)}) collective-permute-start(bf16[4,16,1024]{2,1,0:T(8,128)(2,1)S(1)} %pad_maximum_fusion.own_ref), channel_id=1, source_target_pairs={{0,1},{1,0},{2,3},{3,2},{4,5},{5,4},{6,7},{7,6},{8,9},{9,8},{10,11... | collective-permute-start | bytes 393224 | tf_op jit(solution)/shard_map/ppermute | solution.py:140

commit v6 on v5

--- a/solution.py
+++ b/solution.py
@@ -321,13 +321,14 @@
         out_ref[...] = total.astype(jnp.bfloat16)
 
 
-def place_kernel(own_ref, other_ref, out_ref):
+def place_kernel(*refs):
+    pieces, out_ref = refs[:8], refs[8]
     core = lax.axis_index("inp")
-    width = own_ref.shape[2]
-    for column in range(4):
-        for ref, its_core in ((own_ref, core), (other_ref, 1 - core)):
-            start = pl.multiple_of((its_core * 4 + column) * width, width)
-            out_ref[:, pl.ds(start, width)] = ref[place_of(column)]
+    width = pieces[0].shape[1]
+    for n, piece in enumerate(pieces):
+        its_core = core if n < 4 else 1 - core
+        start = pl.multiple_of((its_core * 4 + place_of(n % 4)) * width, width)
+        out_ref[:, pl.ds(start, width)] = piece[...]
 
 
 def attend_kernel(length_ref, *refs):
@@ -515,13 +516,13 @@
     outgoing = on_chip(
         round_kernel, [shape((count, mix_cols), jnp.bfloat16)] * 4, (), kept, swap_cores(given)
     )
-    own_half = jnp.stack(hand_out(outgoing))
+    own_half = hand_out(outgoing)
     mixed = on_chip(
         place_kernel,
         shape((count, width), jnp.bfloat16),
         (),
-        own_half,
-        swap_cores(own_half),
+        *own_half,
+        *map(swap_cores, own_half),
     )
     return mixed.reshape(steps, rows, width)
 

time: 74.7 us -> 74.5 us (level)
  waiting for transfers between devices: 16.9 us -> 13.4 us
  starting transfers between devices: 34.7 us -> 38 us
    ppermute x8, waiting for transfers between devices: 3.36 us -> 0.02 us  [hand_out(): received.append(lax.ppermute(block, ('out', 'inp'), pairs))]
    ppermute x3 -> x6, starting transfers between devices: 3.7 us -> 6.96 us  [swap_cores(): return lax.ppermute(block, 'inp', [(0, 1), (1, 0)])]
    ppermute x3 -> x6, waiting for transfers between devices: 3.83 us -> 3.7 us  [swap_cores(): return lax.ppermute(block, 'inp', [(0, 1), (1, 0)])]
  transfers between devices with their start and end apart: 25 -> 28, of which waited for: 12 -> 9; matrix products, arithmetic and copies ran while one was open for 0% -> 0% of each run, Pallas kernels for 18% -> 18%
where the time goes in v6:
time: 74.5 us; the launch traced here: 74.3 us
  starting transfers between devices  38 us (51%)
  Pallas kernels  22.2 us (30%)
  waiting for transfers between devices  13.4 us (18%)
    ppermute x14, starting transfers between devices, exchange(): return lax.ppermute(block, ('out', 'inp'), pairs)  22.6 us
    pallas_call x5, Pallas kernels, fetched(): pl.pallas_call(functools.partial(fetch_kernel, [start for _, start, _ in...  13.5 us
    ppermute x14, waiting for transfers between devices, exchange(): return lax.ppermute(block, ('out', 'inp'), pairs)  9.7 us
    ppermute x8, starting transfers between devices, hand_out(): received.append(lax.ppermute(block, ('out', 'inp'), pairs))  8.44 us
    ppermute x6, starting transfers between devices, swap_cores(): return lax.ppermute(block, 'inp', [(0, 1), (1, 0)])  6.96 us
    pallas_call x6, Pallas kernels, on_chip(): pl.pallas_call(kernel, out_shape=out_shape, in_specs=[SMEM_SPEC] * len(sc...  5.29 us
    ppermute x6, waiting for transfers between devices, swap_cores(): return lax.ppermute(block, 'inp', [(0, 1), (1, 0)])  3.7 us
    pallas_call x1, Pallas kernels, attend(): pl.pallas_call(attend_kernel, out_shape=shape((count, key_heads * group *...  3.33 us
  transfers between devices with their start and end apart: 28, of which 9 were waited for; matrix products, arithmetic and copies ran while one was open for 0% of the time, Pallas kernels for 18%

profile of v6, /device:TPU:0, one launch (start us, length us, event | category | flops | bytes accessed | tf_op | source)
XLA Modules:
  0.0 74.3 jit_solution(9126428726485646566)
XLA Ops:
  0.0 1.2 %shard_map.100.refs_0_ = bf16[16,4224]{1,0:T(8,128)(2,1)S(1)} custom-call(s32[8]{0:T(128)} %position_hbm.1, bf16[16,8192]{1,0:T(8,128)(2,1)} %bitcast.7, f32[1,8192]{1,0:T(1,128)} %bitcast.8), custom_call_target="tpu_custom_call" | custom-call | bytes 1048576 | tf_op jit(solution)/shard_map/pallas_call | solution.py:165
  1.2 3.1 %collective-permute-start = (bf16[16,4224]{1,0:T(8,128)(2,1)S(1)}, bf16[16,4224]{1,0:T(8,128)(2,1)S(1)}, u32[]{:S(2)}, u32[]{:S(2)}) collective-permute-start(bf16[16,4224]{1,0:T(8,128)(2,1)S(1)} %shard_map.100.refs_0_), channel_id=1, source_target_pairs={{0,4},{1,9},{2,6},{3,11},{4,0},{5,13},{6,2},{7,15},{8,12},{9,1},{1... | collective-permute-start | bytes 405512 | tf_op jit(solution)/shard_map/ppermute | solution.py:123
  4.3 2.6 %collective-permute-start.1 = (bf16[16,4224]{1,0:T(8,128)(2,1)S(1)}, bf16[16,4224]{1,0:T(8,128)(2,1)S(1)}, u32[]{:S(2)}, u32[]{:S(2)}) collective-permute-start(bf16[16,4224]{1,0:T(8,128)(2,1)S(1)} %shard_map.100.refs_0_), channel_id=1, source_target_pairs={{0,8},{1,3},{2,10},{3,1},{4,12},{5,7},{6,14},{7,5},{8,0},{9,11},{1... | collective-permute-start | bytes 405512 | tf_op jit(solution)/shard_map/ppermute | solution.py:123
  6.9 2.9 %shard_map.101 = (bf16[2048,1024]{1,0:T(8,128)(2,1)S(1)}, bf16[4096,128]{1,0:T(8,128)(2,1)S(1)}, bf16[4096,128]{1,0:T(8,128)(2,1)S(1)}, f32[8,128]{1,0:T(8,128)S(1)}) custom-call(bf16[4096,1024]{1,0:T(8,128)(2,1)} %refs_0_.5, bf16[4096,128]{1,0:T(8,128)(2,1)} %refs_1_.1, bf16[4096,128]{1,0:T(8,128)(2,1)} %refs_2_.1), custom_call_target="tpu_custom_call" | custom-call | bytes 6291456 | tf_op jit(solution)/shard_map/pallas_call | solution.py:227
  9.8 0.0 collective-permute-done.refs_0_
  9.8 0.9 %collective-permute-start.3 = (bf16[16,4224]{1,0:T(8,128)(2,1)S(1)}, bf16[16,4224]{1,0:T(8,128)(2,1)S(1)}, u32[]{:S(2)}, u32[]{:S(2)}) collective-permute-start(bf16[16,4224]{1,0:T(8,128)(2,1)S(1)} %shard_map.102.refs_1_), channel_id=1, source_target_pairs={{0,8},{1,3},{2,10},{3,1},{4,12},{5,7},{6,14},{7,5},{8,0},{9,11},{1... | collective-permute-start | bytes 405512 | tf_op jit(solution)/shard_map/ppermute | solution.py:123
  10.7 1.5 %collective-permute-start.4 = (bf16[16,4224]{1,0:T(8,128)(2,1)S(1)}, bf16[16,4224]{1,0:T(8,128)(2,1)S(1)}, u32[]{:S(2)}, u32[]{:S(2)}) collective-permute-start(bf16[16,4224]{1,0:T(8,128)(2,1)S(1)} %shard_map.102.refs_1_), channel_id=1, source_target_pairs={{0,2},{1,5},{2,0},{3,7},{4,6},{5,1},{6,4},{7,3},{8,10},{9,13},{10,... | collective-permute-start | bytes 405512 | tf_op jit(solution)/shard_map/ppermute | solution.py:123
  12.2 0.5 collective-permute-start.2
  12.7 0.0 collective-permute-done.1.refs_2_
  12.7 1.5 %collective-permute-start.5 = (bf16[16,4224]{1,0:T(8,128)(2,1)S(1)}, bf16[16,4224]{1,0:T(8,128)(2,1)S(1)}, u32[]{:S(2)}, u32[]{:S(2)}) collective-permute-start(bf16[16,4224]{1,0:T(8,128)(2,1)S(1)} %collective-permute-done.1.refs_2_), channel_id=1, source_target_pairs={{0,2},{1,5},{2,0},{3,7},{4,6},{5,1},{6,4},{7,3},{8,10},{9,13},{10,... | collective-permute-start | bytes 405512 | tf_op jit(solution)/shard_map/ppermute | solution.py:123
  14.3 3.1 %collective-permute-done.3.refs_4_ = bf16[16,4224]{1,0:T(8,128)(2,1)S(1)} collective-permute-done((bf16[16,4224]{1,0:T(8,128)(2,1)S(1)}, bf16[16,4224]{1,0:T(8,128)(2,1)S(1)}, u32[]{:S(2)}, u32[]{:S(2)}) %collective-permute-start.3) | collective-permute-done | bytes 135200 | tf_op jit(solution)/shard_map/ppermute | solution.py:123
  17.3 1.5 %collective-permute-start.6 = (bf16[16,4224]{1,0:T(8,128)(2,1)S(1)}, bf16[16,4224]{1,0:T(8,128)(2,1)S(1)}, u32[]{:S(2)}, u32[]{:S(2)}) collective-permute-start(bf16[16,4224]{1,0:T(8,128)(2,1)S(1)} %collective-permute-done.3.refs_4_), channel_id=1, source_target_pairs={{0,2},{1,5},{2,0},{3,7},{4,6},{5,1},{6,4},{7,3},{8,10},{9,13},{10,... | collective-permute-start | bytes 405512 | tf_op jit(solution)/shard_map/ppermute | solution.py:123
  18.9 2.2 %shard_map.103 = (bf16[2048,1024]{1,0:T(8,128)(2,1)S(1)}, f32[8,128]{1,0:T(8,128)S(1)}) custom-call(bf16[4096,1024]{1,0:T(8,128)(2,1)} %refs_0_.5), custom_call_target="tpu_custom_call" | custom-call | bytes 4194304 | tf_op jit(solution)/shard_map/pallas_call | solution.py:227
  21.1 0.0 collective-permute-done.4.refs_0_
  21.1 0.0 collective-permute-done.2.refs_3_
  21.1 1.2 %collective-permute-done.6.refs_7_ = bf16[16,4224]{1,0:T(8,128)(2,1)S(1)} collective-permute-done((bf16[16,4224]{1,0:T(8,128)(2,1)S(1)}, bf16[16,4224]{1,0:T(8,128)(2,1)S(1)}, u32[]{:S(2)}, u32[]{:S(2)}) %collective-permute-start.6) | collective-permute-done | bytes 135200 | tf_op jit(solution)/shard_map/ppermute | solution.py:123
  22.3 1.9 %shard_map.105 = (f32[64,1280]{1,0:T(8,128)S(1)}, f32[64,1280]{1,0:T(8,128)S(1)}, f32[64,128]{1,0:T(8,128)S(1)}) custom-call(bf16[16,4224]{1,0:T(8,128)(2,1)S(1)} %shard_map.100.refs_0_, bf16[16,4224]{1,0:T(8,128)(2,1)S(1)} %shard_map.102.refs_1_, bf16[16,4224]{1,0:T(8,128)(2,1)S(1)} %collective-permute-done.1.refs_2_, ...), custom_call_target="tpu_custom_call" | custom-call | bytes 1048576 | tf_op jit(solution)/shard_map/pallas_call | solution.py:165
  24.3 0.2 fusion.3
  24.4 0.1 collective-permute-start.7
  24.5 0.2 fusion.7
  24.7 0.1 pad_maximum_fusion
  24.8 1.3 %collective-permute-done.7.arrived_ref = f32[64,1280]{1,0:T(8,128)S(1)} collective-permute-done((f32[64,1280]{1,0:T(8,128)S(1)}, f32[64,1280]{1,0:T(8,128)S(1)}, u32[]{:S(2)}, u32[]{:S(2)}) %collective-permute-start.7) | collective-permute-done | bytes 327712 | tf_op jit(solution)/shard_map/ppermute | solution.py:140
  26.1 0.2 shard_map.106
  26.3 0.4 collective-permute-start.10
  26.7 2.6 %collective-permute-start.11 = (bf16[16,1280]{1,0:T(8,128)(2,1)S(1)}, bf16[16,1280]{1,0:T(8,128)(2,1)S(1)}, u32[]{:S(2)}, u32[]{:S(2)}) collective-permute-start(bf16[16,1280]{1,0:T(8,128)(2,1)S(1)} %get-tuple-element.42), channel_id=1, source_target_pairs={{0,6},{1,14},{2,4},{3,12},{4,2},{5,10},{6,0},{7,8},{8,15},{9,7},{1... | collective-permute-start | bytes 122888 | tf_op jit(solution)/shard_map/ppermute | solution.py:151
  29.3 0.7 collective-permute-start.8
  30.0 0.6 collective-permute-start.9
  30.5 4.1 %shard_map.107 = (bf16[8,2048,128]{2,1,0:T(8,128)(2,1)S(1)}, bf16[8,2048,128]{2,1,0:T(8,128)(2,1)S(1)}, f32[8,128]{1,0:T(8,128)}) custom-call(bf16[8,2048,128]{2,1,0:T(8,128)(2,1)} %bitcast.5, bf16[8,2048,128]{2,1,0:T(8,128)(2,1)} %bitcast.6), custom_call_target="tpu_custom_call" | custom-call | bytes 8388608 | tf_op jit(solution)/shard_map/pallas_call | solution.py:227
  34.6 0.0 collective-permute-done.11.refs_3_
  34.6 0.0 collective-permute-done.8.refs_0_
  34.7 3.3 %shard_map.108.refs_0_ = bf16[16,4096]{1,0:T(8,128)(2,1)S(1)} custom-call(s32[8]{0:T(128)S(1)} %copy-done, bf16[16,1280]{1,0:T(8,128)(2,1)S(1)} %collective-permute-done.8.refs_0_, bf16[16,1280]{1,0:T(8,128)(2,1)S(1)} %collective-permute-done.9.refs_1_, bf16[16,1280]{1,0:T(8,128)(2,1)S(1)} %collective-permute-done.10.refs_2_, ...), custom_call_target="tpu_custom_call" | custom-call | bytes 12582912 | tf_op jit(solution)/shard_map/pallas_call | solution.py:423
  38.0 0.4 collective-permute-start.12
  38.4 2.2 %shard_map.109 = (bf16[2048,1024]{1,0:T(8,128)(2,1)S(1)}, f32[8,128]{1,0:T(8,128)S(1)}) custom-call(bf16[4096,1024]{1,0:T(8,128)(2,1)} %refs_0_.7), custom_call_target="tpu_custom_call" | custom-call | bytes 4194304 | tf_op jit(solution)/shard_map/pallas_call | solution.py:227
  40.6 5.9 %collective-permute-start.13 = (bf16[16,4096]{1,0:T(8,128)(2,1)S(1)}, bf16[16,4096]{1,0:T(8,128)(2,1)S(1)}, u32[]{:S(2)}, u32[]{:S(2)}) collective-permute-start(bf16[16,4096]{1,0:T(8,128)(2,1)S(1)} %shard_map.108.refs_0_), channel_id=1, source_target_pairs={{0,8},{1,3},{2,10},{3,1},{4,12},{5,7},{6,14},{7,5},{8,0},{9,11},{1... | collective-permute-start | bytes 393224 | tf_op jit(solution)/shard_map/ppermute | solution.py:123
  46.6 0.0 collective-permute-done.12.refs_0_
  46.6 1.5 %collective-permute-start.15 = (bf16[16,4096]{1,0:T(8,128)(2,1)S(1)}, bf16[16,4096]{1,0:T(8,128)(2,1)S(1)}, u32[]{:S(2)}, u32[]{:S(2)}) collective-permute-start(bf16[16,4096]{1,0:T(8,128)(2,1)S(1)} %shard_map.110.refs_1_), channel_id=1, source_target_pairs={{0,8},{1,3},{2,10},{3,1},{4,12},{5,7},{6,14},{7,5},{8,0},{9,11},{1... | collective-permute-start | bytes 393224 | tf_op jit(solution)/shard_map/ppermute | solution.py:123
  48.1 0.5 collective-permute-start.16
  48.7 1.5 %collective-permute-start.14 = (bf16[16,4096]{1,0:T(8,128)(2,1)S(1)}, bf16[16,4096]{1,0:T(8,128)(2,1)S(1)}, u32[]{:S(2)}, u32[]{:S(2)}) collective-permute-start(bf16[16,4096]{1,0:T(8,128)(2,1)S(1)} %shard_map.108.refs_0_), channel_id=1, source_target_pairs={{0,2},{1,5},{2,0},{3,7},{4,6},{5,1},{6,4},{7,3},{8,10},{9,13},{10,... | collective-permute-start | bytes 393224 | tf_op jit(solution)/shard_map/ppermute | solution.py:123
  50.1 2.0 %collective-permute-done.13.refs_2_ = bf16[16,4096]{1,0:T(8,128)(2,1)S(1)} collective-permute-done((bf16[16,4096]{1,0:T(8,128)(2,1)S(1)}, bf16[16,4096]{1,0:T(8,128)(2,1)S(1)}, u32[]{:S(2)}, u32[]{:S(2)}) %collective-permute-start.13) | collective-permute-done | bytes 131104 | tf_op jit(solution)/shard_map/ppermute | solution.py:123
  52.2 0.0 collective-permute-start.17
  52.2 1.6 %collective-permute-done.15.refs_4_ = bf16[16,4096]{1,0:T(8,128)(2,1)S(1)} collective-permute-done((bf16[16,4096]{1,0:T(8,128)(2,1)S(1)}, bf16[16,4096]{1,0:T(8,128)(2,1)S(1)}, u32[]{:S(2)}, u32[]{:S(2)}) %collective-permute-start.15) | collective-permute-done | bytes 131104 | tf_op jit(solution)/shard_map/ppermute | solution.py:123
  53.8 1.0 %collective-permute-start.18 = (bf16[16,4096]{1,0:T(8,128)(2,1)S(1)}, bf16[16,4096]{1,0:T(8,128)(2,1)S(1)}, u32[]{:S(2)}, u32[]{:S(2)}) collective-permute-start(bf16[16,4096]{1,0:T(8,128)(2,1)S(1)} %collective-permute-done.15.refs_4_), channel_id=1, source_target_pairs={{0,2},{1,5},{2,0},{3,7},{4,6},{5,1},{6,4},{7,3},{8,10},{9,13},{10,... | collective-permute-start | bytes 393224 | tf_op jit(solution)/shard_map/ppermute | solution.py:123
  54.8 2.2 %shard_map.111 = (bf16[2048,1024]{1,0:T(8,128)(2,1)S(1)}, f32[8,128]{1,0:T(8,128)S(1)}) custom-call(bf16[4096,1024]{1,0:T(8,128)(2,1)} %refs_0_.7), custom_call_target="tpu_custom_call" | custom-call | bytes 4194304 | tf_op jit(solution)/shard_map/pallas_call | solution.py:227
  57.0 0.0 collective-permute-done.16.refs_0_
  57.1 0.0 collective-permute-done.14.refs_3_
  57.1 0.1 collective-permute-done.17.refs_6_
  57.1 1.6 %collective-permute-done.18.refs_7_ = bf16[16,4096]{1,0:T(8,128)(2,1)S(1)} collective-permute-done((bf16[16,4096]{1,0:T(8,128)(2,1)S(1)}, bf16[16,4096]{1,0:T(8,128)(2,1)S(1)}, u32[]{:S(2)}, u32[]{:S(2)}) %collective-permute-start.18) | collective-permute-done | bytes 131104 | tf_op jit(solution)/shard_map/ppermute | solution.py:123
  58.8 1.3 %shard_map.113 = (f32[64,1024]{1,0:T(8,128)S(1)}, f32[64,1024]{1,0:T(8,128)S(1)}) custom-call(bf16[16,4096]{1,0:T(8,128)(2,1)S(1)} %shard_map.108.refs_0_, bf16[16,4096]{1,0:T(8,128)(2,1)S(1)} %shard_map.110.refs_1_, bf16[16,4096]{1,0:T(8,128)(2,1)S(1)} %collective-permute-done.13.refs_2_, bf16[16,4096]{1,0:T(8,128)(2,1)S(1)} %collective-permute-done.14.refs_3_, ...), custom_call_target="tpu_custom_call" | custom-call | bytes 1048576 | tf_op jit(solution)/shard_map/pallas_call | solution.py:165
  60.0 0.1 collective-permute-start.19
  60.1 1.5 %collective-permute-done.19.arrived_ref = f32[64,1024]{1,0:T(8,128)S(1)} collective-permute-done((f32[64,1024]{1,0:T(8,128)S(1)}, f32[64,1024]{1,0:T(8,128)S(1)}, u32[]{:S(2)}, u32[]{:S(2)}) %collective-permute-start.19) | collective-permute-done | bytes 262176 | tf_op jit(solution)/shard_map/ppermute | solution.py:140
  61.7 0.7 collective-permute-start.20
  62.3 1.1 %collective-permute-start.21 = (bf16[16,1024]{1,0:T(8,128)(2,1)S(1)}, bf16[16,1024]{1,0:T(8,128)(2,1)S(1)}, u32[]{:S(2)}, u32[]{:S(2)}) collective-permute-start(bf16[16,1024]{1,0:T(8,128)(2,1)S(1)} %get-tuple-element.52), channel_id=1, source_target_pairs={{0,2},{1,10},{2,0},{3,8},{4,6},{5,14},{6,4},{7,12},{8,11},{9,3},{1... | collective-permute-start | bytes 98312 | tf_op jit(solution)/shard_map/ppermute | solution.py:151
  63.4 0.6 collective-permute-start.22
  64.1 1.8 %collective-permute-start.23 = (bf16[16,1024]{1,0:T(8,128)(2,1)S(1)}, bf16[16,1024]{1,0:T(8,128)(2,1)S(1)}, u32[]{:S(2)}, u32[]{:S(2)}) collective-permute-start(bf16[16,1024]{1,0:T(8,128)(2,1)S(1)} %get-tuple-element.54), channel_id=1, source_target_pairs={{0,6},{1,14},{2,4},{3,12},{4,2},{5,10},{6,0},{7,8},{8,15},{9,7},{1... | collective-permute-start | bytes 98312 | tf_op jit(solution)/shard_map/ppermute | solution.py:151
  65.9 0.0 collective-permute-done.20.refs_0_
  65.9 3.1 %collective-permute-start.24 = (bf16[16,1024]{1,0:T(8,128)(2,1)S(1)}, bf16[16,1024]{1,0:T(8,128)(2,1)S(1)}, u32[]{:S(2)}, u32[]{:S(2)}) collective-permute-start(bf16[16,1024]{1,0:T(8,128)(2,1)S(1)} %collective-permute-done.20.refs_0_), channel_id=1, source_target_pairs={{0,1},{1,0},{2,3},{3,2},{4,5},{5,4},{6,7},{7,6},{8,9},{9,8},{10,11... | collective-permute-start | bytes 98312 | tf_op jit(solution)/shard_map/ppermute | solution.py:140
  69.0 0.1 collective-permute-start.25
  69.1 0.0 collective-permute-done.22.refs_2_
  69.1 1.8 %collective-permute-start.26 = (bf16[16,1024]{1,0:T(8,128)(2,1)S(1)}, bf16[16,1024]{1,0:T(8,128)(2,1)S(1)}, u32[]{:S(2)}, u32[]{:S(2)}) collective-permute-start(bf16[16,1024]{1,0:T(8,128)(2,1)S(1)} %collective-permute-done.22.refs_2_), channel_id=1, source_target_pairs={{0,1},{1,0},{2,3},{3,2},{4,5},{5,4},{6,7},{7,6},{8,9},{9,8},{10,11... | collective-permute-start | bytes 98312 | tf_op jit(solution)/shard_map/ppermute | solution.py:140
  70.9 1.8 %collective-permute-start.27 = (bf16[16,1024]{1,0:T(8,128)(2,1)S(1)}, bf16[16,1024]{1,0:T(8,128)(2,1)S(1)}, u32[]{:S(2)}, u32[]{:S(2)}) collective-permute-start(bf16[16,1024]{1,0:T(8,128)(2,1)S(1)} %collective-permute-done.23.refs_3_), channel_id=1, source_target_pairs={{0,1},{1,0},{2,3},{3,2},{4,5},{5,4},{6,7},{7,6},{8,9},{9,8},{10,11... | collective-permute-start | bytes 98312 | tf_op jit(solution)/shard_map/ppermute | solution.py:140
  72.7 0.0 collective-permute-done.24.refs_4_
  72.7 0.0 collective-permute-done.25.refs_5_
  72.7 0.8 %collective-permute-done.27.refs_7_ = bf16[16,1024]{1,0:T(8,128)(2,1)S(1)} collective-permute-done((bf16[16,1024]{1,0:T(8,128)(2,1)S(1)}, bf16[16,1024]{1,0:T(8,128)(2,1)S(1)}, u32[]{:S(2)}, u32[]{:S(2)}) %collective-permute-start.27) | collective-permute-done | bytes 32800 | tf_op jit(solution)/shard_map/ppermute | solution.py:140
  73.6 0.7 shard_map.115
  (14 shorter events, 0.1 us)
Async XLA Ops:
  1.2 8.5 %collective-permute-start = (bf16[16,4224]{1,0:T(8,128)(2,1)S(1)}, bf16[16,4224]{1,0:T(8,128)(2,1)S(1)}, u32[]{:S(2)}, u32[]{:S(2)}) collective-permute-start(bf16[16,4224]{1,0:T(8,128)(2,1)S(1)} %shard_map.100.refs_0_), channel_id=1, source_target_pairs={{0,4},{1,9},{2,6},{3,11},{4,0},{5,13},{6,2},{7,15},{8,12},{9,1},{1... | collective-permute-start | bytes 405512 | tf_op jit(solution)/shard_map/ppermute | solution.py:123
  4.3 8.4 %collective-permute-start.1 = (bf16[16,4224]{1,0:T(8,128)(2,1)S(1)}, bf16[16,4224]{1,0:T(8,128)(2,1)S(1)}, u32[]{:S(2)}, u32[]{:S(2)}) collective-permute-start(bf16[16,4224]{1,0:T(8,128)(2,1)S(1)} %shard_map.100.refs_0_), channel_id=1, source_target_pairs={{0,8},{1,3},{2,10},{3,1},{4,12},{5,7},{6,14},{7,5},{8,0},{9,11},{1... | collective-permute-start | bytes 405512 | tf_op jit(solution)/shard_map/ppermute | solution.py:123
  9.8 7.5 %collective-permute-start.3 = (bf16[16,4224]{1,0:T(8,128)(2,1)S(1)}, bf16[16,4224]{1,0:T(8,128)(2,1)S(1)}, u32[]{:S(2)}, u32[]{:S(2)}) collective-permute-start(bf16[16,4224]{1,0:T(8,128)(2,1)S(1)} %shard_map.102.refs_1_), channel_id=1, source_target_pairs={{0,8},{1,3},{2,10},{3,1},{4,12},{5,7},{6,14},{7,5},{8,0},{9,11},{1... | collective-permute-start | bytes 405512 | tf_op jit(solution)/shard_map/ppermute | solution.py:123
  10.7 10.4 %collective-permute-start.4 = (bf16[16,4224]{1,0:T(8,128)(2,1)S(1)}, bf16[16,4224]{1,0:T(8,128)(2,1)S(1)}, u32[]{:S(2)}, u32[]{:S(2)}) collective-permute-start(bf16[16,4224]{1,0:T(8,128)(2,1)S(1)} %shard_map.102.refs_1_), channel_id=1, source_target_pairs={{0,2},{1,5},{2,0},{3,7},{4,6},{5,1},{6,4},{7,3},{8,10},{9,13},{10,... | collective-permute-start | bytes 405512 | tf_op jit(solution)/shard_map/ppermute | solution.py:123
  12.2 8.9 %collective-permute-start.2 = (bf16[16,4224]{1,0:T(8,128)(2,1)S(1)}, bf16[16,4224]{1,0:T(8,128)(2,1)S(1)}, u32[]{:S(2)}, u32[]{:S(2)}) collective-permute-start(bf16[16,4224]{1,0:T(8,128)(2,1)S(1)} %shard_map.100.refs_0_), channel_id=1, source_target_pairs={{0,2},{1,5},{2,0},{3,7},{4,6},{5,1},{6,4},{7,3},{8,10},{9,13},{10,... | collective-permute-start | bytes 405512 | tf_op jit(solution)/shard_map/ppermute | solution.py:123
  12.7 8.4 %collective-permute-start.5 = (bf16[16,4224]{1,0:T(8,128)(2,1)S(1)}, bf16[16,4224]{1,0:T(8,128)(2,1)S(1)}, u32[]{:S(2)}, u32[]{:S(2)}) collective-permute-start(bf16[16,4224]{1,0:T(8,128)(2,1)S(1)} %collective-permute-done.1.refs_2_), channel_id=1, source_target_pairs={{0,2},{1,5},{2,0},{3,7},{4,6},{5,1},{6,4},{7,3},{8,10},{9,13},{10,... | collective-permute-start | bytes 405512 | tf_op jit(solution)/shard_map/ppermute | solution.py:123
  17.3 5.0 %collective-permute-start.6 = (bf16[16,4224]{1,0:T(8,128)(2,1)S(1)}, bf16[16,4224]{1,0:T(8,128)(2,1)S(1)}, u32[]{:S(2)}, u32[]{:S(2)}) collective-permute-start(bf16[16,4224]{1,0:T(8,128)(2,1)S(1)} %collective-permute-done.3.refs_4_), channel_id=1, source_target_pairs={{0,2},{1,5},{2,0},{3,7},{4,6},{5,1},{6,4},{7,3},{8,10},{9,13},{10,... | collective-permute-start | bytes 405512 | tf_op jit(solution)/shard_map/ppermute | solution.py:123
  24.4 1.7 %collective-permute-start.7 = (f32[64,1280]{1,0:T(8,128)S(1)}, f32[64,1280]{1,0:T(8,128)S(1)}, u32[]{:S(2)}, u32[]{:S(2)}) collective-permute-start(f32[64,1280]{1,0:T(8,128)S(1)} %get-tuple-element.37), channel_id=1, source_target_pairs={{0,1},{1,0},{2,3},{3,2},{4,5},{5,4},{6,7},{7,6},{8,9},{9,8},{10,11... | collective-permute-start | bytes 983048 | tf_op jit(solution)/shard_map/ppermute | solution.py:140
  26.3 8.3 %collective-permute-start.10 = (bf16[16,1280]{1,0:T(8,128)(2,1)S(1)}, bf16[16,1280]{1,0:T(8,128)(2,1)S(1)}, u32[]{:S(2)}, u32[]{:S(2)}) collective-permute-start(bf16[16,1280]{1,0:T(8,128)(2,1)S(1)} %get-tuple-element.41), channel_id=1, source_target_pairs={{0,4},{1,12},{2,6},{3,14},{4,0},{5,8},{6,2},{7,10},{8,13},{9,5},{1... | collective-permute-start | bytes 122888 | tf_op jit(solution)/shard_map/ppermute | solution.py:151
  26.7 8.0 %collective-permute-start.11 = (bf16[16,1280]{1,0:T(8,128)(2,1)S(1)}, bf16[16,1280]{1,0:T(8,128)(2,1)S(1)}, u32[]{:S(2)}, u32[]{:S(2)}) collective-permute-start(bf16[16,1280]{1,0:T(8,128)(2,1)S(1)} %get-tuple-element.42), channel_id=1, source_target_pairs={{0,6},{1,14},{2,4},{3,12},{4,2},{5,10},{6,0},{7,8},{8,15},{9,7},{1... | collective-permute-start | bytes 122888 | tf_op jit(solution)/shard_map/ppermute | solution.py:151
  29.3 5.3 %collective-permute-start.8 = (bf16[16,1280]{1,0:T(8,128)(2,1)S(1)}, bf16[16,1280]{1,0:T(8,128)(2,1)S(1)}, u32[]{:S(2)}, u32[]{:S(2)}) collective-permute-start(bf16[16,1280]{1,0:T(8,128)(2,1)S(1)} %get-tuple-element.39), channel_id=1, source_target_pairs={{0,0},{1,8},{2,2},{3,10},{4,4},{5,12},{6,6},{7,14},{8,9},{9,1},{10... | collective-permute-start | bytes 122888 | tf_op jit(solution)/shard_map/ppermute | solution.py:151
  30.0 4.7 %collective-permute-start.9 = (bf16[16,1280]{1,0:T(8,128)(2,1)S(1)}, bf16[16,1280]{1,0:T(8,128)(2,1)S(1)}, u32[]{:S(2)}, u32[]{:S(2)}) collective-permute-start(bf16[16,1280]{1,0:T(8,128)(2,1)S(1)} %get-tuple-element.40), channel_id=1, source_target_pairs={{0,2},{1,10},{2,0},{3,8},{4,6},{5,14},{6,4},{7,12},{8,11},{9,3},{1... | collective-permute-start | bytes 122888 | tf_op jit(solution)/shard_map/ppermute | solution.py:151
  30.5 4.1 %copy-start = (s32[8]{0:T(128)S(1)}, s32[8]{0:T(128)}, u32[]{:S(2)}) copy-start(s32[8]{0:T(128)} %length_ref.1) | copy-start | bytes 100
  38.0 8.6 %collective-permute-start.12 = (bf16[16,4096]{1,0:T(8,128)(2,1)S(1)}, bf16[16,4096]{1,0:T(8,128)(2,1)S(1)}, u32[]{:S(2)}, u32[]{:S(2)}) collective-permute-start(bf16[16,4096]{1,0:T(8,128)(2,1)S(1)} %shard_map.108.refs_0_), channel_id=1, source_target_pairs={{0,4},{1,9},{2,6},{3,11},{4,0},{5,13},{6,2},{7,15},{8,12},{9,1},{1... | collective-permute-start | bytes 393224 | tf_op jit(solution)/shard_map/ppermute | solution.py:123
  40.6 11.5 %collective-permute-start.13 = (bf16[16,4096]{1,0:T(8,128)(2,1)S(1)}, bf16[16,4096]{1,0:T(8,128)(2,1)S(1)}, u32[]{:S(2)}, u32[]{:S(2)}) collective-permute-start(bf16[16,4096]{1,0:T(8,128)(2,1)S(1)} %shard_map.108.refs_0_), channel_id=1, source_target_pairs={{0,8},{1,3},{2,10},{3,1},{4,12},{5,7},{6,14},{7,5},{8,0},{9,11},{1... | collective-permute-start | bytes 393224 | tf_op jit(solution)/shard_map/ppermute | solution.py:123
  46.6 7.2 %collective-permute-start.15 = (bf16[16,4096]{1,0:T(8,128)(2,1)S(1)}, bf16[16,4096]{1,0:T(8,128)(2,1)S(1)}, u32[]{:S(2)}, u32[]{:S(2)}) collective-permute-start(bf16[16,4096]{1,0:T(8,128)(2,1)S(1)} %shard_map.110.refs_1_), channel_id=1, source_target_pairs={{0,8},{1,3},{2,10},{3,1},{4,12},{5,7},{6,14},{7,5},{8,0},{9,11},{1... | collective-permute-start | bytes 393224 | tf_op jit(solution)/shard_map/ppermute | solution.py:123
  48.1 8.9 %collective-permute-start.16 = (bf16[16,4096]{1,0:T(8,128)(2,1)S(1)}, bf16[16,4096]{1,0:T(8,128)(2,1)S(1)}, u32[]{:S(2)}, u32[]{:S(2)}) collective-permute-start(bf16[16,4096]{1,0:T(8,128)(2,1)S(1)} %shard_map.110.refs_1_), channel_id=1, source_target_pairs={{0,2},{1,5},{2,0},{3,7},{4,6},{5,1},{6,4},{7,3},{8,10},{9,13},{10,... | collective-permute-start | bytes 393224 | tf_op jit(solution)/shard_map/ppermute | solution.py:123
  48.7 8.4 %collective-permute-start.14 = (bf16[16,4096]{1,0:T(8,128)(2,1)S(1)}, bf16[16,4096]{1,0:T(8,128)(2,1)S(1)}, u32[]{:S(2)}, u32[]{:S(2)}) collective-permute-start(bf16[16,4096]{1,0:T(8,128)(2,1)S(1)} %shard_map.108.refs_0_), channel_id=1, source_target_pairs={{0,2},{1,5},{2,0},{3,7},{4,6},{5,1},{6,4},{7,3},{8,10},{9,13},{10,... | collective-permute-start | bytes 393224 | tf_op jit(solution)/shard_map/ppermute | solution.py:123
  52.2 5.0 %collective-permute-start.17 = (bf16[16,4096]{1,0:T(8,128)(2,1)S(1)}, bf16[16,4096]{1,0:T(8,128)(2,1)S(1)}, u32[]{:S(2)}, u32[]{:S(2)}) collective-permute-start(bf16[16,4096]{1,0:T(8,128)(2,1)S(1)} %collective-permute-done.13.refs_2_), channel_id=1, source_target_pairs={{0,2},{1,5},{2,0},{3,7},{4,6},{5,1},{6,4},{7,3},{8,10},{9,13},{10,... | collective-permute-start | bytes 393224 | tf_op jit(solution)/shard_map/ppermute | solution.py:123
  53.8 5.0 %collective-permute-start.18 = (bf16[16,4096]{1,0:T(8,128)(2,1)S(1)}, bf16[16,4096]{1,0:T(8,128)(2,1)S(1)}, u32[]{:S(2)}, u32[]{:S(2)}) collective-permute-start(bf16[16,4096]{1,0:T(8,128)(2,1)S(1)} %collective-permute-done.15.refs_4_), channel_id=1, source_target_pairs={{0,2},{1,5},{2,0},{3,7},{4,6},{5,1},{6,4},{7,3},{8,10},{9,13},{10,... | collective-permute-start | bytes 393224 | tf_op jit(solution)/shard_map/ppermute | solution.py:123
  60.0 1.6 %collective-permute-start.19 = (f32[64,1024]{1,0:T(8,128)S(1)}, f32[64,1024]{1,0:T(8,128)S(1)}, u32[]{:S(2)}, u32[]{:S(2)}) collective-permute-start(f32[64,1024]{1,0:T(8,128)S(1)} %get-tuple-element.50), channel_id=1, source_target_pairs={{0,1},{1,0},{2,3},{3,2},{4,5},{5,4},{6,7},{7,6},{8,9},{9,8},{10,11... | collective-permute-start | bytes 786440 | tf_op jit(solution)/shard_map/ppermute | solution.py:140
  61.7 4.2 %collective-permute-start.20 = (bf16[16,1024]{1,0:T(8,128)(2,1)S(1)}, bf16[16,1024]{1,0:T(8,128)(2,1)S(1)}, u32[]{:S(2)}, u32[]{:S(2)}) collective-permute-start(bf16[16,1024]{1,0:T(8,128)(2,1)S(1)} %get-tuple-element.51), channel_id=1, source_target_pairs={{0,0},{1,8},{2,2},{3,10},{4,4},{5,12},{6,6},{7,14},{8,9},{9,1},{10... | collective-permute-start | bytes 98312 | tf_op jit(solution)/shard_map/ppermute | solution.py:151
  62.3 6.7 %collective-permute-start.21 = (bf16[16,1024]{1,0:T(8,128)(2,1)S(1)}, bf16[16,1024]{1,0:T(8,128)(2,1)S(1)}, u32[]{:S(2)}, u32[]{:S(2)}) collective-permute-start(bf16[16,1024]{1,0:T(8,128)(2,1)S(1)} %get-tuple-element.52), channel_id=1, source_target_pairs={{0,2},{1,10},{2,0},{3,8},{4,6},{5,14},{6,4},{7,12},{8,11},{9,3},{1... | collective-permute-start | bytes 98312 | tf_op jit(solution)/shard_map/ppermute | solution.py:151
  63.4 5.7 %collective-permute-start.22 = (bf16[16,1024]{1,0:T(8,128)(2,1)S(1)}, bf16[16,1024]{1,0:T(8,128)(2,1)S(1)}, u32[]{:S(2)}, u32[]{:S(2)}) collective-permute-start(bf16[16,1024]{1,0:T(8,128)(2,1)S(1)} %get-tuple-element.53), channel_id=1, source_target_pairs={{0,4},{1,12},{2,6},{3,14},{4,0},{5,8},{6,2},{7,10},{8,13},{9,5},{1... | collective-permute-start | bytes 98312 | tf_op jit(solution)/shard_map/ppermute | solution.py:151
  64.1 6.8 %collective-permute-start.23 = (bf16[16,1024]{1,0:T(8,128)(2,1)S(1)}, bf16[16,1024]{1,0:T(8,128)(2,1)S(1)}, u32[]{:S(2)}, u32[]{:S(2)}) collective-permute-start(bf16[16,1024]{1,0:T(8,128)(2,1)S(1)} %get-tuple-element.54), channel_id=1, source_target_pairs={{0,6},{1,14},{2,4},{3,12},{4,2},{5,10},{6,0},{7,8},{8,15},{9,7},{1... | collective-permute-start | bytes 98312 | tf_op jit(solution)/shard_map/ppermute | solution.py:151
  65.9 6.8 %collective-permute-start.24 = (bf16[16,1024]{1,0:T(8,128)(2,1)S(1)}, bf16[16,1024]{1,0:T(8,128)(2,1)S(1)}, u32[]{:S(2)}, u32[]{:S(2)}) collective-permute-start(bf16[16,1024]{1,0:T(8,128)(2,1)S(1)} %collective-permute-done.20.refs_0_), channel_id=1, source_target_pairs={{0,1},{1,0},{2,3},{3,2},{4,5},{5,4},{6,7},{7,6},{8,9},{9,8},{10,11... | collective-permute-start | bytes 98312 | tf_op jit(solution)/shard_map/ppermute | solution.py:140
  69.0 3.7 %collective-permute-start.25 = (bf16[16,1024]{1,0:T(8,128)(2,1)S(1)}, bf16[16,1024]{1,0:T(8,128)(2,1)S(1)}, u32[]{:S(2)}, u32[]{:S(2)}) collective-permute-start(bf16[16,1024]{1,0:T(8,128)(2,1)S(1)} %collective-permute-done.21.refs_1_), channel_id=1, source_target_pairs={{0,1},{1,0},{2,3},{3,2},{4,5},{5,4},{6,7},{7,6},{8,9},{9,8},{10,11... | collective-permute-start | bytes 98312 | tf_op jit(solution)/shard_map/ppermute | solution.py:140
  69.1 3.6 %collective-permute-start.26 = (bf16[16,1024]{1,0:T(8,128)(2,1)S(1)}, bf16[16,1024]{1,0:T(8,128)(2,1)S(1)}, u32[]{:S(2)}, u32[]{:S(2)}) collective-permute-start(bf16[16,1024]{1,0:T(8,128)(2,1)S(1)} %collective-permute-done.22.refs_2_), channel_id=1, source_target_pairs={{0,1},{1,0},{2,3},{3,2},{4,5},{5,4},{6,7},{7,6},{8,9},{9,8},{10,11... | collective-permute-start | bytes 98312 | tf_op jit(solution)/shard_map/ppermute | solution.py:140
  70.9 2.7 %collective-permute-start.27 = (bf16[16,1024]{1,0:T(8,128)(2,1)S(1)}, bf16[16,1024]{1,0:T(8,128)(2,1)S(1)}, u32[]{:S(2)}, u32[]{:S(2)}) collective-permute-start(bf16[16,1024]{1,0:T(8,128)(2,1)S(1)} %collective-permute-done.23.refs_3_), channel_id=1, source_target_pairs={{0,1},{1,0},{2,3},{3,2},{4,5},{5,4},{6,7},{7,6},{8,9},{9,8},{10,11... | collective-permute-start | bytes 98312 | tf_op jit(solution)/shard_map/ppermute | solution.py:140
